TPU v7x, 32 devices: a whole 2x2x4 slice. The times are simulated.
32 devices in a mesh: groups: 2 (over x), expert: 16 (over z, y, core).
Axes of the slice: x: 2, y: 2, z: 4, core: 2. Of those that a mesh axis runs over, the one named last changes fastest.
Arguments:
- tokens: bfloat16 [4096, 3584], P(('groups', 'expert')), parts along dimension 0, may hold values from -6 to 6
- expert_ids: int32 [4096, 2], P(('groups', 'expert')), parts along dimension 0, may hold values from 0 to 3, all different within a row; in each aligned block of 128 rows (0 to 127, 128 to 255, ...) at most 80 rows name the same one
- gate_weights: float32 [4096, 2], P(('groups', 'expert')), parts along dimension 0, may hold values from 0.5 to 2.5
- w_gate: bfloat16 [16, 3584, 512], P('expert'), may hold values from -0.09375 to 0.09375
- w_up: bfloat16 [16, 3584, 512], P('expert'), may hold values from -0.09375 to 0.09375
- w_down: bfloat16 [16, 512, 3584], P('expert'), may hold values from -0.125 to 0.125
Outputs:
- moe_output: bfloat16 [4096, 3584], P(('groups', 'expert')), parts along dimension 0
There are 2 independent parts, one for each index of `groups`. A program takes and returns all parts, laid end to end along the dimension named above; an argument that names none is the same for every part. Nothing has to cross between parts.
Inputs may be any that keep to these rules, and one draw needn't show every extreme that they name: `expert_ids`: each row names 2 different experts. Among the rows of one device no expert is named by more than 80 rows, and in every draw some device has an expert named by exactly 80 of its rows.
All inputs are finite; a program needn't handle non-finite values.
Results may differ from a plain program's by a relative error of at most 0.0057.
Values may be sent and summed in bfloat16 or wider, within the bound.
No kernel may reach another device: no remote copies, remote signals or barrier semaphores. Data moves between devices by JAX's collectives and lax.ppermute only.
A program may use at most 128 MiB of HBM per device.

v0:
```python
import jax
import jax.numpy as jnp
from jax import lax
from jax.sharding import PartitionSpec as P

FF = 2048


def local(tokens, expert_ids, gate_weights, w_gate, w_up, w_down):
    tok_rows, features = tokens.shape
    routes = expert_ids.shape[1]
    devices = lax.axis_size("expert")
    shards = FF // w_gate.shape[2]
    experts = devices // shards
    capacity = shards * (
        (5 * tok_rows * routes * shards + 4 * devices * shards - 1) // (4 * devices * shards)
    )
    flat_ids = expert_ids.reshape(-1)
    one_hot = (flat_ids[:, None] == jnp.arange(experts, dtype=jnp.int32)[None, :]).astype(jnp.int32)
    before = jnp.cumsum(one_hot, axis=0) - one_hot
    slot_index = jnp.sum(before * one_hot, axis=1)
    position = flat_ids * capacity + slot_index
    token_index = jnp.arange(flat_ids.shape[0], dtype=jnp.int32) // routes
    matches = position[None, :] == jnp.arange(experts * capacity, dtype=jnp.int32)[:, None]
    source_row = jnp.sum(jnp.where(matches, token_index[None, :] + 1, 0), axis=1) - 1
    send_rows = jnp.where(
        (source_row >= 0)[:, None], tokens[jnp.maximum(source_row, 0)], jnp.zeros((), tokens.dtype)
    )
    packed = send_rows.reshape(experts, capacity, features)
    outgoing = jnp.broadcast_to(packed[:, None], (experts, shards, capacity, features)).reshape(
        devices, capacity, features
    )
    received = lax.all_to_all(outgoing, "expert", split_axis=0, concat_axis=0, tiled=True)
    flat_rows = received.reshape(-1, features)
    gate_proj = jnp.dot(flat_rows, w_gate[0], preferred_element_type=jnp.float32)
    up_proj = jnp.dot(flat_rows, w_up[0], preferred_element_type=jnp.float32)
    hidden = (jax.nn.silu(gate_proj) * up_proj).astype(jnp.bfloat16)
    partial_value = jnp.dot(hidden, w_down[0], preferred_element_type=jnp.float32)
    partial_value = partial_value.reshape(received.shape[0], -1, features)
    returned = lax.all_to_all(partial_value, "expert", split_axis=0, concat_axis=0, tiled=True)
    expert_out = jnp.sum(returned.reshape(experts, shards, capacity, features), axis=1).astype(
        jnp.bfloat16
    )
    out_grid = expert_out.reshape(experts * capacity, features)
    picked = out_grid[position]
    weighted = picked.astype(jnp.float32) * gate_weights.reshape(-1)[:, None]
    return jnp.sum(weighted.reshape(tok_rows, routes, features), axis=1).astype(jnp.bfloat16)


def solution(mesh):
    placed = (
        P(("groups", "expert"), None),
        P(("groups", "expert"), None),
        P(("groups", "expert"), None),
        P("expert", None, None),
        P("expert", None, None),
        P("expert", None, None),
    )
    return jax.shard_map(
        local, mesh=mesh, in_specs=placed, out_specs=P(("groups", "expert"), None), check_vma=False
    )
```

profile of v0, /device:TPU:13, one launch (start us, length us, event | category | flops | bytes accessed | tf_op | source)
XLA Modules:
  0.0 661.1 jit_solution(1765255216044205087)
XLA Ops:
  0.0 0.0 copy-start
  0.0 0.9 copy.16
  0.9 0.1 eq.39
  1.0 0.1 reshape.129
  1.2 1.2 reduce-window.6
  2.4 0.1 slice.12
  2.5 0.1 copy.18
  2.6 0.1 copy.19
  2.7 0.1 add_bitcast_fusion
  2.8 0.2 select_reduce_fusion
  3.0 0.1 ge.11
  3.1 0.0 copy-done
  3.1 3.1 gather_fusion
  6.2 1.6 broadcast_select_fusion
  7.8 2.5 broadcast_in_dim.40
  10.4 0.0 copy-start.4
  10.4 205.6 %all_to_all.10 = bf16[16,80,3584]{2,1,0:T(8,128)(2,1)S(1)} all-to-all(bf16[16,80,3584]{2,1,0:T(8,128)(2,1)S(1)} %bitcast.46), channel_id=1, replica_groups=mesh['groups'=2,'expert'=16] {'expert'}, dimensions={0} | all-to-all | bytes 18350080 | tf_op jit(solution)/shard_map/all_to_all | solution.py:33
  216.0 0.0 copy-done.4
  216.0 0.0 copy-start.5
  216.0 4.9 fusion.4
  220.9 0.0 copy-done.5
  220.9 0.0 copy-start.6
  220.9 5.3 fusion.9
  226.2 0.0 copy-done.6
  226.2 8.9 %fusion = f32[16,80,3584]{2,1,0:T(8,128)} fusion(bf16[16,80,512]{2,1,0:T(8,128)(2,1)S(1)} %bitcast.53, bf16[1,512,3584]{2,1,0:T(8,128)(2,1)S(1)} %copy-done.6), kind=kOutput, calls=%fused_computation.3 | convolution fusion | flops 4697620480 | bytes 23330816 | tf_op jit(solution)/shard_map/dot_general | solution.py:38
  235.1 0.0 copy-start.2
  235.1 0.0 copy-start.3
  235.1 6.3 all-to-all-start.1
  241.4 0.0 copy-done.2
  241.4 0.1 copy.20
  241.5 0.1 mul.50
  241.7 0.0 copy-done.3
  241.7 0.1 copy.21
  241.8 395.4 %all-to-all-done.1 = f32[16,80,3584]{2,1,0:T(8,128)} async-done(((f32[16,80,3584]{2,1,0:T(8,128)}), f32[16,80,3584]{2,1,0:T(8,128)}, u32[]{:S(2)}, u32[]{:S(2)}) %all-to-all-start.1) | async-done | bytes 18350112 | tf_op jit(solution)/shard_map/all_to_all | solution.py:40
  637.2 7.4 %bitcast_reduce_fusion = bf16[4,80,3584]{2,1,0:T(8,128)(2,1)S(1)} fusion(f32[16,80,3584]{2,1,0:T(8,128)} %all-to-all-done.1), kind=kLoop, calls=%fused_computation.2 | loop fusion | flops 3440640 | bytes 20643840 | tf_op jit(solution)/shard_map/reduce_sum | solution.py:41
  644.7 3.0 gather_fusion.1
  647.6 0.0 copy-start.1
  647.6 5.3 reshape.134
  652.9 8.2 %multiply_reduce_fusion = bf16[128,3584]{1,0:T(8,128)(2,1)} fusion(f32[128,2,3584]{2,1,0:T(2,128)} %reshape.134, f32[128,2]{1,0:T(8,128)S(1)} %copy.21), kind=kLoop, calls=%fused_computation.9 | loop fusion | flops 1376256 | bytes 4588544 | tf_op jit(solution)/shard_map/reduce_sum | solution.py:47
  661.1 0.0 copy-done.1
  (11 shorter events, 0.1 us)
Async XLA Ops:
  0.0 3.1 copy-start
  10.4 205.6 %copy-start.4 = (bf16[1,3584,512]{2,1,0:T(8,128)(2,1)S(1)}, bf16[1,3584,512]{2,1,0:T(8,128)(2,1)}, u32[]{:S(2)}) copy-start(bf16[1,3584,512]{2,1,0:T(8,128)(2,1)} %param.9) | copy-start | bytes 11010052
  216.0 4.9 copy-start.5
  220.9 5.3 copy-start.6
  235.1 6.3 copy-start.2
  235.1 6.5 copy-start.3
  235.1 402.1 %all-to-all-start.1 = ((f32[16,80,3584]{2,1,0:T(8,128)}), f32[16,80,3584]{2,1,0:T(8,128)}, u32[]{:S(2)}, u32[]{:S(2)}) async-start(f32[16,80,3584]{2,1,0:T(8,128)} %fusion), calls=%async_computation.1 | async-start | bytes 36700160 | tf_op jit(solution)/shard_map/all_to_all | solution.py:40
  647.6 13.5 %copy-start.1 = (bf16[128,3584]{1,0:T(8,128)(2,1)S(1)}, bf16[128,3584]{1,0:T(8,128)(2,1)}, u32[]{:S(2)}) copy-start(bf16[128,3584]{1,0:T(8,128)(2,1)} %param.6) | copy-start | bytes 2752516
where the time goes:
time: 661 us
  waiting for transfers between devices  395 us (60%)
  blocking collectives  206 us (31%)
  matrix products  19.1 us (3%)
  other arithmetic  18.8 us (3%)
  local copies, waits for them, and re-layouts  15.8 us (2%)
    all_to_all x1, waiting for transfers between devices, local(): lax.all_to_all(partial_value, 'expert', split_axis=0, concat_axis=0, tile...  395 us
    all_to_all x1, blocking collectives, local(): lax.all_to_all(outgoing, 'expert', split_axis=0, concat_axis=0, tiled=True)  206 us
  transfers between devices with their start and end apart: 1, of which 1 were waited for; matrix products, arithmetic and copies ran while one was open for 0% of the time, Pallas kernels for 0%

commit v1 on v0

v1 whole, which is shorter than its diff:
```python
import jax
import jax.numpy as jnp
from jax import lax
from jax.sharding import PartitionSpec as P

FF = 2048
BF = jnp.bfloat16
F32 = jnp.float32


def local(tokens, expert_ids, gate_weights, w_gate, w_up, w_down):
    tok_rows, features = tokens.shape
    routes = expert_ids.shape[1]
    devices = lax.axis_size("expert")
    shards = FF // w_gate.shape[2]
    experts = devices // shards
    capacity = shards * (
        (5 * tok_rows * routes * shards + 4 * devices * shards - 1) // (4 * devices * shards)
    )
    me = lax.axis_index("expert") // shards

    def move(x, to):
        return lax.ppermute(x, "expert", [(d, to(d)) for d in range(devices)])

    def turn(x, k):
        return move(x, lambda d: (d + k * shards) % devices) if k % experts else x

    def chip(x):
        return move(x, lambda d: d ^ 2)

    def core(x):
        return move(x, lambda d: d ^ 1)

    named = (expert_ids[:, :, None] == jnp.arange(experts, dtype=jnp.int32)).astype(F32)
    both = jnp.sum(named, axis=1)
    earlier = jnp.tril(jnp.ones((tok_rows, tok_rows), F32), -1)
    slot = jnp.dot(earlier, both, preferred_element_type=F32)
    slots = jnp.arange(capacity, dtype=F32)

    def dispatch(k):
        e = (me + k) % experts
        hot = lax.dynamic_index_in_dim(both, e, 1, keepdims=False)
        at = lax.dynamic_index_in_dim(slot, e, 1, keepdims=False)
        pick = jnp.where((at[None, :] == slots[:, None]) & (hot[None, :] > 0), 1.0, 0.0).astype(BF)
        return jnp.dot(pick, tokens, preferred_element_type=F32).astype(BF)

    def ffn(rows):
        gate = jnp.dot(rows, w_gate[0], preferred_element_type=F32)
        up = jnp.dot(rows, w_up[0], preferred_element_type=F32)
        hidden = (jax.nn.silu(gate) * up).astype(BF)
        return jnp.dot(hidden, w_down[0], preferred_element_type=F32)

    def expert(own):
        other = chip(own)
        mate_own, mate_other = core(own), core(other)
        part = ffn(jnp.concatenate([own, other, mate_own, mate_other]))
        two = part[: 2 * capacity] + core(part[2 * capacity :].astype(BF)).astype(F32)
        return (two[:capacity] + chip(two[capacity:].astype(BF)).astype(F32)).astype(BF)

    def combine(k, back):
        e = (me + k) % experts
        hot = lax.dynamic_index_in_dim(named, e, 2, keepdims=False)
        at = lax.dynamic_index_in_dim(slot, e, 1, keepdims=False)
        pick = jnp.where((at[:, None] == slots[None, :]), 1.0, 0.0).astype(BF)
        weight = jnp.sum(hot * gate_weights, axis=1)
        return weight[:, None] * jnp.dot(pick, back, preferred_element_type=F32)

    total = 0.0
    for k in range(experts):
        back = turn(expert(turn(dispatch(k), k)), -k)
        total = total + combine(k, back)
    return total.astype(BF)


def solution(mesh):
    placed = (
        P(("groups", "expert"), None),
        P(("groups", "expert"), None),
        P(("groups", "expert"), None),
        P("expert", None, None),
        P("expert", None, None),
        P("expert", None, None),
    )
    return jax.shard_map(
        local, mesh=mesh, in_specs=placed, out_specs=P(("groups", "expert"), None), check_vma=False
    )
```

time: 661 us -> 240 us (0.36)
  the two profiles are of different devices: /device:TPU:13 before, /device:TPU:0 now
where the time goes in v1:
time: 240 us; the launch traced here: 239 us
  waiting for transfers between devices  131 us (55%)
  matrix products  51.6 us (22%)
  local copies, waits for them, and re-layouts  27.3 us (11%)
  starting transfers between devices  20.8 us (9%)
  other arithmetic  7.62 us (3%)
    ppermute x26, waiting for transfers between devices, move(): return lax.ppermute(x, 'expert', [(d, to(d)) for d in range(devices)])  131 us
    dot_general x4, matrix products, ffn(): return jnp.dot(hidden, w_down[0], preferred_element_type=F32)  34.7 us
    ppermute x26, starting transfers between devices, move(): return lax.ppermute(x, 'expert', [(d, to(d)) for d in range(devices)])  20.8 us
    unnamed x41, local copies, waits for them, and re-layouts  15.4 us
    dot_general x3, matrix products, ffn(): up = jnp.dot(rows, w_up[0], preferred_element_type=F32)  10.5 us
    slice x4, local copies, waits for them, and re-layouts, expert(): two = part[:2 * capacity] + core(part[2 * capacity:].astype(BF)).astype(F32)  8.6 us
    add x4, other arithmetic, expert(): two = part[:2 * capacity] + core(part[2 * capacity:].astype(BF)).astype(F32)  6.48 us
  transfers between devices with their start and end apart: 26, of which 8 were waited for; matrix products, arithmetic and copies ran while one was open for 34% of the time, Pallas kernels for 0%

profile of v1, /device:TPU:0, one launch (start us, length us, event | category | flops | bytes accessed | tf_op | source)
XLA Modules:
  0.0 239.2 jit_solution(17003543113064896257)
XLA Ops:
  0.0 0.8 fusion.131
  1.5 3.0 %collective-permute-start = (bf16[80,3584]{1,0:T(8,128)(2,1)S(1)}, bf16[80,3584]{1,0:T(8,128)(2,1)S(1)}, u32[]{:S(2)}, u32[]{:S(2)}) collective-permute-start(bf16[80,3584]{1,0:T(8,128)(2,1)S(1)} %convolution_convert_fusion.3), channel_id=1, source_target_pairs={{0,2},{1,3},{2,0},{3,1},{4,6},{5,7},{6,4},{7,5},{8,10},{9,11},{10,... | collective-permute-start | bytes 1720328 | tf_op jit(solution)/shard_map/ppermute | solution.py:23
  4.9 2.7 %collective-permute-start.12 = (bf16[80,3584]{1,0:T(8,128)(2,1)S(1)}, bf16[80,3584]{1,0:T(8,128)(2,1)}, u32[]{:S(2)}, u32[]{:S(2)}) collective-permute-start(bf16[80,3584]{1,0:T(8,128)(2,1)S(1)} %convolution_convert_fusion.1), channel_id=1, source_target_pairs={{0,8},{1,9},{2,10},{3,11},{4,12},{5,13},{6,14},{7,15},{8,0},{9,1},... | collective-permute-start | bytes 1720328 | tf_op jit(solution)/shard_map/ppermute | solution.py:23
  7.8 1.6 collective-permute-start.5
  9.8 2.3 collective-permute-start.19
  12.1 34.2 %collective-permute-done.12 = bf16[80,3584]{1,0:T(8,128)(2,1)} collective-permute-done((bf16[80,3584]{1,0:T(8,128)(2,1)S(1)}, bf16[80,3584]{1,0:T(8,128)(2,1)}, u32[]{:S(2)}, u32[]{:S(2)}) %collective-permute-start.12) | collective-permute-done | bytes 573472 | tf_op jit(solution)/shard_map/ppermute | solution.py:23
  46.3 1.9 constant_dynamic-update-slice_fusion.7
  49.0 0.8 constant_dynamic-update-slice_fusion.3
  49.9 1.8 collective-permute-start.6
  51.6 0.9 constant_dynamic-update-slice_fusion.11
  53.4 2.2 fusion.26
  55.5 8.4 %fusion.10 = f32[320,3584]{1,0:T(8,128)} fusion(bf16[1,512,3584]{2,1,0:T(8,128)(2,1)} %param.11, f32[320,512]{1,0:T(8,128)} %fusion.26, bf16[1,3584,512]{2,1,0:T(8,128)(2,1)} %param.10, bf16[80,3584]{1,0:T(8,128)(2,1)S(1)} %collective-permute-done.2, bf16[80,3584]{1,0:T(8,128)(2,1)} %copy-done.11, bf16[80,3584]{1,0:T(8,128)(2,1)} %copy-done.10, ...), kind=kOutput, calls=%fused_computation.18 | convolution fusion | flops 2358968320 | bytes 14876672 | tf_op jit(solution)/shard_map/dot_general | solution.py:51
  64.4 0.9 constant_dynamic-update-slice_fusion.6
  65.2 1.9 slice.116
  67.2 0.6 collective-permute-start.3
  67.7 1.1 constant_dynamic-update-slice_fusion.5
  68.8 7.9 %collective-permute-done.6 = bf16[80,3584]{1,0:T(8,128)(2,1)} collective-permute-done((bf16[80,3584]{1,0:T(8,128)(2,1)S(1)}, bf16[80,3584]{1,0:T(8,128)(2,1)}, u32[]{:S(2)}, u32[]{:S(2)}) %collective-permute-start.6) | collective-permute-done | bytes 573472 | tf_op jit(solution)/shard_map/ppermute | solution.py:23
  76.8 1.9 constant_dynamic-update-slice_fusion.2
  78.7 8.7 %collective-permute-done.20 = bf16[80,3584]{1,0:T(8,128)(2,1)} collective-permute-done((bf16[80,3584]{1,0:T(8,128)(2,1)S(1)}, bf16[80,3584]{1,0:T(8,128)(2,1)}, u32[]{:S(2)}, u32[]{:S(2)}) %collective-permute-start.20) | collective-permute-done | bytes 573472 | tf_op jit(solution)/shard_map/ppermute | solution.py:23
  87.4 1.9 constant_dynamic-update-slice_fusion.10
  89.8 1.9 constant_dynamic-update-slice_fusion.1
  91.7 0.9 constant_dynamic-update-slice_fusion.9
  92.7 1.4 copy-done.5
  94.0 1.3 fusion.14
  95.4 8.6 %fusion.6 = f32[320,3584]{1,0:T(8,128)} fusion(bf16[1,512,3584]{2,1,0:T(8,128)(2,1)} %param.11, f32[320,512]{1,0:T(8,128)S(1)} %fusion.14, bf16[320,3584]{1,0:T(8,128)(2,1)} %copy-done.5, bf16[1,3584,512]{2,1,0:T(8,128)(2,1)} %param.9), kind=kOutput, calls=%fused_computation.14 | convolution fusion | flops 2349793280 | bytes 14876672 | tf_op jit(solution)/shard_map/dot_general | solution.py:51
  104.0 1.8 slice.114
  105.9 1.9 constant_dynamic-update-slice_fusion
  107.8 4.9 %fusion.16 = f32[320,512]{1,0:T(8,128)} fusion(bf16[320,3584]{1,0:T(8,128)(2,1)} %constant_dynamic-update-slice_fusion, bf16[1,3584,512]{2,1,0:T(8,128)(2,1)} %param.10), kind=kOutput, calls=%fused_computation.24 | convolution fusion | flops 1174405120 | bytes 6619136 | tf_op jit(solution)/shard_map/dot_general | solution.py:49
  112.7 8.9 %fusion.8 = f32[320,3584]{1,0:T(8,128)} fusion(bf16[1,512,3584]{2,1,0:T(8,128)(2,1)} %param.11, f32[320,512]{1,0:T(8,128)} %fusion.16, bf16[320,3584]{1,0:T(8,128)(2,1)} %constant_dynamic-update-slice_fusion, bf16[1,3584,512]{2,1,0:T(8,128)(2,1)} %param.9), kind=kOutput, calls=%fused_computation.16 | convolution fusion | flops 2349793280 | bytes 14876672 | tf_op jit(solution)/shard_map/dot_general | solution.py:51
  121.6 3.0 %slice.115 = bf16[160,3584]{1,0:T(8,128)(2,1)} slice(f32[320,3584]{1,0:T(8,128)} %fusion.8), slice={[160:320], [0:3584]} | slice | bytes 2293760 | tf_op jit(solution)/shard_map/slice | solution.py:57
  125.1 1.1 constant_dynamic-update-slice_fusion.8
  126.2 1.4 copy-done.3
  127.6 4.2 %fusion.12 = f32[320,512]{1,0:T(8,128)} fusion(bf16[320,3584]{1,0:T(8,128)(2,1)S(1)} %constant_dynamic-update-slice_fusion.8, bf16[1,3584,512]{2,1,0:T(8,128)(2,1)} %param.10), kind=kOutput, calls=%fused_computation.20 | convolution fusion | flops 1174405120 | bytes 6619136 | tf_op jit(solution)/shard_map/dot_general | solution.py:49
  131.8 8.8 %fusion.4 = f32[320,3584]{1,0:T(8,128)} fusion(bf16[1,512,3584]{2,1,0:T(8,128)(2,1)} %param.11, f32[320,512]{1,0:T(8,128)} %fusion.12, bf16[320,3584]{1,0:T(8,128)(2,1)} %copy-done.3, bf16[1,3584,512]{2,1,0:T(8,128)(2,1)} %param.9), kind=kOutput, calls=%fused_computation.12 | convolution fusion | flops 2349793280 | bytes 14876672 | tf_op jit(solution)/shard_map/dot_general | solution.py:51
  140.6 1.9 slice.113
  142.8 2.2 slice_add_fusion.3
  145.0 0.7 collective-permute-start.4
  145.8 2.6 %slice_add_fusion.1 = f32[160,3584]{1,0:T(8,128)S(1)} fusion(f32[320,3584]{1,0:T(8,128)} %fusion.6, bf16[160,3584]{1,0:T(8,128)(2,1)} %collective-permute-done.16), kind=kLoop, calls=%fused_computation.39 | loop fusion | flops 1146880 | bytes 5734400 | tf_op jit(solution)/shard_map/add | solution.py:57
  148.4 1.0 collective-permute-start.17
  149.5 1.5 slice_add_fusion.2
  151.1 1.1 collective-permute-start.10
  152.5 1.0 collective-permute-start.24
  153.5 31.9 %collective-permute-done.10 = bf16[80,3584]{1,0:T(8,128)(2,1)S(1)} collective-permute-done((bf16[80,3584]{1,0:T(8,128)(2,1)S(1)}, bf16[80,3584]{1,0:T(8,128)(2,1)S(1)}, u32[]{:S(2)}, u32[]{:S(2)}) %collective-permute-start.10) | collective-permute-done | bytes 573472 | tf_op jit(solution)/shard_map/ppermute | solution.py:23
  185.6 11.7 %collective-permute-done.24 = bf16[80,3584]{1,0:T(8,128)(2,1)S(1)} collective-permute-done((bf16[80,3584]{1,0:T(8,128)(2,1)S(1)}, bf16[80,3584]{1,0:T(8,128)(2,1)S(1)}, u32[]{:S(2)}, u32[]{:S(2)}) %collective-permute-start.24) | collective-permute-done | bytes 573472 | tf_op jit(solution)/shard_map/ppermute | solution.py:23
  197.8 2.0 collective-permute-start.18
  200.2 15.0 %collective-permute-done.25 = bf16[80,3584]{1,0:T(8,128)(2,1)S(1)} collective-permute-done((bf16[80,3584]{1,0:T(8,128)(2,1)S(1)}, bf16[80,3584]{1,0:T(8,128)(2,1)S(1)}, u32[]{:S(2)}, u32[]{:S(2)}) %collective-permute-start.25) | collective-permute-done | bytes 573472 | tf_op jit(solution)/shard_map/ppermute | solution.py:23
  216.2 21.6 %collective-permute-done.18 = bf16[80,3584]{1,0:T(8,128)(2,1)S(1)} collective-permute-done((bf16[80,3584]{1,0:T(8,128)(2,1)S(1)}, bf16[80,3584]{1,0:T(8,128)(2,1)S(1)}, u32[]{:S(2)}, u32[]{:S(2)}) %collective-permute-start.18) | collective-permute-done | bytes 573472 | tf_op jit(solution)/shard_map/ppermute | solution.py:23
  237.8 1.4 fusion.3
  (88 shorter events, 7.5 us)
Async XLA Ops:
  0.0 1.2 copy-start
  1.5 10.6 %copy-start.6 = (s32[128,2]{0,1:T(2,128)S(1)}, s32[128,2]{0,1:T(2,128)}, u32[]{:S(2)}) copy-start(s32[128,2]{0,1:T(2,128)} %param.7) | copy-start | bytes 3076
  1.5 10.6 %copy-start.7 = (f32[128,2]{0,1:T(2,128)S(1)}, f32[128,2]{0,1:T(2,128)}, u32[]{:S(2)}) copy-start(f32[128,2]{0,1:T(2,128)} %param.8) | copy-start | bytes 3076
  1.5 47.0 %collective-permute-start = (bf16[80,3584]{1,0:T(8,128)(2,1)S(1)}, bf16[80,3584]{1,0:T(8,128)(2,1)S(1)}, u32[]{:S(2)}, u32[]{:S(2)}) collective-permute-start(bf16[80,3584]{1,0:T(8,128)(2,1)S(1)} %convolution_convert_fusion.3), channel_id=1, source_target_pairs={{0,2},{1,3},{2,0},{3,1},{4,6},{5,7},{6,4},{7,5},{8,10},{9,11},{10,... | collective-permute-start | bytes 1720328 | tf_op jit(solution)/shard_map/ppermute | solution.py:23
  4.6 47.9 %collective-permute-start.1 = (bf16[80,3584]{1,0:T(8,128)(2,1)S(1)}, bf16[80,3584]{1,0:T(8,128)(2,1)S(1)}, u32[]{:S(2)}, u32[]{:S(2)}) collective-permute-start(bf16[80,3584]{1,0:T(8,128)(2,1)S(1)} %convolution_convert_fusion.3), channel_id=1, source_target_pairs={{0,1},{1,0},{2,3},{3,2},{4,5},{5,4},{6,7},{7,6},{8,9},{9,8},{10,11... | collective-permute-start | bytes 1720328 | tf_op jit(solution)/shard_map/ppermute | solution.py:23
  4.9 41.5 %collective-permute-start.12 = (bf16[80,3584]{1,0:T(8,128)(2,1)S(1)}, bf16[80,3584]{1,0:T(8,128)(2,1)}, u32[]{:S(2)}, u32[]{:S(2)}) collective-permute-start(bf16[80,3584]{1,0:T(8,128)(2,1)S(1)} %convolution_convert_fusion.1), channel_id=1, source_target_pairs={{0,8},{1,9},{2,10},{3,11},{4,12},{5,13},{6,14},{7,15},{8,0},{9,1},... | collective-permute-start | bytes 1720328 | tf_op jit(solution)/shard_map/ppermute | solution.py:23
  7.8 40.7 %collective-permute-start.5 = (bf16[80,3584]{1,0:T(8,128)(2,1)S(1)}, bf16[80,3584]{1,0:T(8,128)(2,1)S(1)}, u32[]{:S(2)}, u32[]{:S(2)}) collective-permute-start(bf16[80,3584]{1,0:T(8,128)(2,1)S(1)} %convolution_convert_fusion.2), channel_id=1, source_target_pairs={{0,4},{1,5},{2,6},{3,7},{4,8},{5,9},{6,10},{7,11},{8,12},{9,13},{1... | collective-permute-start | bytes 1720328 | tf_op jit(solution)/shard_map/ppermute | solution.py:23
  9.5 43.9 %copy-start.9 = (bf16[1,3584,512]{2,1,0:T(8,128)(2,1)S(1)}, bf16[1,3584,512]{2,1,0:T(8,128)(2,1)}, u32[]{:S(2)}) copy-start(bf16[1,3584,512]{2,1,0:T(8,128)(2,1)} %param.9) | copy-start | bytes 11010052
  9.8 40.1 %collective-permute-start.19 = (bf16[80,3584]{1,0:T(8,128)(2,1)S(1)}, bf16[80,3584]{1,0:T(8,128)(2,1)S(1)}, u32[]{:S(2)}, u32[]{:S(2)}) collective-permute-start(bf16[80,3584]{1,0:T(8,128)(2,1)S(1)} %convolution_convert_fusion), channel_id=1, source_target_pairs={{0,12},{1,13},{2,14},{3,15},{4,0},{5,1},{6,2},{7,3},{8,4},{9,5},{1... | collective-permute-start | bytes 1720328 | tf_op jit(solution)/shard_map/ppermute | solution.py:23
  48.2 16.1 %collective-permute-start.13 = (bf16[80,3584]{1,0:T(8,128)(2,1)}, bf16[80,3584]{1,0:T(8,128)(2,1)S(1)}, u32[]{:S(2)}, u32[]{:S(2)}) collective-permute-start(bf16[80,3584]{1,0:T(8,128)(2,1)} %collective-permute-done.12), channel_id=1, source_target_pairs={{0,2},{1,3},{2,0},{3,1},{4,6},{5,7},{6,4},{7,5},{8,10},{9,11},{10,... | collective-permute-start | bytes 1720328 | tf_op jit(solution)/shard_map/ppermute | solution.py:23
  48.5 18.6 %collective-permute-start.14 = (bf16[80,3584]{1,0:T(8,128)(2,1)}, bf16[80,3584]{1,0:T(8,128)(2,1)}, u32[]{:S(2)}, u32[]{:S(2)}) collective-permute-start(bf16[80,3584]{1,0:T(8,128)(2,1)} %collective-permute-done.12), channel_id=1, source_target_pairs={{0,1},{1,0},{2,3},{3,2},{4,5},{5,4},{6,7},{7,6},{8,9},{9,8},{10,11... | collective-permute-start | bytes 1720328 | tf_op jit(solution)/shard_map/ppermute | solution.py:23
  48.5 4.6 %copy-start.10 = (bf16[80,3584]{1,0:T(8,128)(2,1)}, bf16[80,3584]{1,0:T(8,128)(2,1)S(1)}, u32[]{:S(2)}) copy-start(bf16[80,3584]{1,0:T(8,128)(2,1)S(1)} %collective-permute-done) | copy-start | bytes 1720324
  48.5 4.0 %collective-permute-start.2 = (bf16[80,3584]{1,0:T(8,128)(2,1)S(1)}, bf16[80,3584]{1,0:T(8,128)(2,1)S(1)}, u32[]{:S(2)}, u32[]{:S(2)}) collective-permute-start(bf16[80,3584]{1,0:T(8,128)(2,1)S(1)} %collective-permute-done), channel_id=1, source_target_pairs={{0,1},{1,0},{2,3},{3,2},{4,5},{5,4},{6,7},{7,6},{8,9},{9,8},{10,11... | collective-permute-start | bytes 1720328 | tf_op jit(solution)/shard_map/ppermute | solution.py:23
  49.9 26.9 %collective-permute-start.6 = (bf16[80,3584]{1,0:T(8,128)(2,1)S(1)}, bf16[80,3584]{1,0:T(8,128)(2,1)}, u32[]{:S(2)}, u32[]{:S(2)}) collective-permute-start(bf16[80,3584]{1,0:T(8,128)(2,1)S(1)} %collective-permute-done.5), channel_id=1, source_target_pairs={{0,2},{1,3},{2,0},{3,1},{4,6},{5,7},{6,4},{7,5},{8,10},{9,11},{10,... | collective-permute-start | bytes 1720328 | tf_op jit(solution)/shard_map/ppermute | solution.py:23
  52.5 0.9 copy-start.11
  52.5 36.8 %collective-permute-start.7 = (bf16[80,3584]{1,0:T(8,128)(2,1)S(1)}, bf16[80,3584]{1,0:T(8,128)(2,1)}, u32[]{:S(2)}, u32[]{:S(2)}) collective-permute-start(bf16[80,3584]{1,0:T(8,128)(2,1)S(1)} %collective-permute-done.5), channel_id=1, source_target_pairs={{0,1},{1,0},{2,3},{3,2},{4,5},{5,4},{6,7},{7,6},{8,9},{9,8},{10,11... | collective-permute-start | bytes 1720328 | tf_op jit(solution)/shard_map/ppermute | solution.py:23
  52.5 34.8 %collective-permute-start.20 = (bf16[80,3584]{1,0:T(8,128)(2,1)S(1)}, bf16[80,3584]{1,0:T(8,128)(2,1)}, u32[]{:S(2)}, u32[]{:S(2)}) collective-permute-start(bf16[80,3584]{1,0:T(8,128)(2,1)S(1)} %collective-permute-done.19), channel_id=1, source_target_pairs={{0,2},{1,3},{2,0},{3,1},{4,6},{5,7},{6,4},{7,5},{8,10},{9,11},{10,... | collective-permute-start | bytes 1720328 | tf_op jit(solution)/shard_map/ppermute | solution.py:23
  64.4 27.4 %collective-permute-start.21 = (bf16[80,3584]{1,0:T(8,128)(2,1)S(1)}, bf16[80,3584]{1,0:T(8,128)(2,1)S(1)}, u32[]{:S(2)}, u32[]{:S(2)}) collective-permute-start(bf16[80,3584]{1,0:T(8,128)(2,1)S(1)} %collective-permute-done.19), channel_id=1, source_target_pairs={{0,1},{1,0},{2,3},{3,2},{4,5},{5,4},{6,7},{7,6},{8,9},{9,8},{10,11... | collective-permute-start | bytes 1720328 | tf_op jit(solution)/shard_map/ppermute | solution.py:23
  65.2 2.5 %copy-start.4 = (bf16[320,3584]{1,0:T(8,128)(2,1)S(1)}, bf16[320,3584]{1,0:T(8,128)(2,1)}, u32[]{:S(2)}) copy-start(bf16[320,3584]{1,0:T(8,128)(2,1)} %constant_dynamic-update-slice_fusion.6) | copy-start | bytes 6881284
  67.2 75.6 %collective-permute-start.3 = (bf16[160,3584]{1,0:T(8,128)(2,1)S(1)}, bf16[160,3584]{1,0:T(8,128)(2,1)}, u32[]{:S(2)}, u32[]{:S(2)}) collective-permute-start(bf16[160,3584]{1,0:T(8,128)(2,1)S(1)} %slice.116), channel_id=1, source_target_pairs={{0,1},{1,0},{2,3},{3,2},{4,5},{5,4},{6,7},{7,6},{8,9},{9,8},{10,11... | collective-permute-start | bytes 3440648 | tf_op jit(solution)/shard_map/ppermute | solution.py:23
  76.8 15.8 %collective-permute-start.15 = (bf16[80,3584]{1,0:T(8,128)(2,1)S(1)}, bf16[80,3584]{1,0:T(8,128)(2,1)S(1)}, u32[]{:S(2)}, u32[]{:S(2)}) collective-permute-start(bf16[80,3584]{1,0:T(8,128)(2,1)S(1)} %collective-permute-done.13), channel_id=1, source_target_pairs={{0,1},{1,0},{2,3},{3,2},{4,5},{5,4},{6,7},{7,6},{8,9},{9,8},{10,11... | collective-permute-start | bytes 1720328 | tf_op jit(solution)/shard_map/ppermute | solution.py:23
  78.7 15.3 %copy-start.8 = (bf16[1,3584,512]{2,1,0:T(8,128)(2,1)S(1)}, bf16[1,3584,512]{2,1,0:T(8,128)(2,1)}, u32[]{:S(2)}) copy-start(bf16[1,3584,512]{2,1,0:T(8,128)(2,1)} %param.10) | copy-start | bytes 11010052
  87.4 18.5 %collective-permute-start.8 = (bf16[80,3584]{1,0:T(8,128)(2,1)}, bf16[80,3584]{1,0:T(8,128)(2,1)}, u32[]{:S(2)}, u32[]{:S(2)}) collective-permute-start(bf16[80,3584]{1,0:T(8,128)(2,1)} %collective-permute-done.6), channel_id=1, source_target_pairs={{0,1},{1,0},{2,3},{3,2},{4,5},{5,4},{6,7},{7,6},{8,9},{9,8},{10,11... | collective-permute-start | bytes 1720328 | tf_op jit(solution)/shard_map/ppermute | solution.py:23
  89.3 35.8 %collective-permute-start.22 = (bf16[80,3584]{1,0:T(8,128)(2,1)}, bf16[80,3584]{1,0:T(8,128)(2,1)}, u32[]{:S(2)}, u32[]{:S(2)}) collective-permute-start(bf16[80,3584]{1,0:T(8,128)(2,1)} %collective-permute-done.20), channel_id=1, source_target_pairs={{0,1},{1,0},{2,3},{3,2},{4,5},{5,4},{6,7},{7,6},{8,9},{9,8},{10,11... | collective-permute-start | bytes 1720328 | tf_op jit(solution)/shard_map/ppermute | solution.py:23
  92.6 1.4 copy-start.5
  105.8 40.0 %collective-permute-start.16 = (bf16[160,3584]{1,0:T(8,128)(2,1)S(1)}, bf16[160,3584]{1,0:T(8,128)(2,1)}, u32[]{:S(2)}, u32[]{:S(2)}) collective-permute-start(bf16[160,3584]{1,0:T(8,128)(2,1)S(1)} %slice.114), channel_id=1, source_target_pairs={{0,1},{1,0},{2,3},{3,2},{4,5},{5,4},{6,7},{7,6},{8,9},{9,8},{10,11... | collective-permute-start | bytes 3440648 | tf_op jit(solution)/shard_map/ppermute | solution.py:23
  121.6 3.5 %copy-start.2 = (bf16[320,3584]{1,0:T(8,128)(2,1)S(1)}, bf16[320,3584]{1,0:T(8,128)(2,1)}, u32[]{:S(2)}) copy-start(bf16[320,3584]{1,0:T(8,128)(2,1)} %constant_dynamic-update-slice_fusion.9) | copy-start | bytes 6881284
  124.6 24.8 %collective-permute-start.9 = (bf16[160,3584]{1,0:T(8,128)(2,1)}, bf16[160,3584]{1,0:T(8,128)(2,1)}, u32[]{:S(2)}, u32[]{:S(2)}) collective-permute-start(bf16[160,3584]{1,0:T(8,128)(2,1)} %slice.115), channel_id=1, source_target_pairs={{0,1},{1,0},{2,3},{3,2},{4,5},{5,4},{6,7},{7,6},{8,9},{9,8},{10,11... | collective-permute-start | bytes 3440648 | tf_op jit(solution)/shard_map/ppermute | solution.py:23
  126.2 1.4 copy-start.3
  140.6 8.9 %slice-start = ((s8[4587520]{0:T(1024)(128)(4,1)}), s8[4194304]{0:T(1024)(128)(4,1)S(1)}, s32[]{:S(2)}) async-start(s8[4587520]{0:T(1024)(128)(4,1)} %bitcast.97), calls=%async_computation | async-start | bytes 8388608
  142.5 9.7 %collective-permute-start.23 = (bf16[160,3584]{1,0:T(8,128)(2,1)S(1)}, bf16[160,3584]{1,0:T(8,128)(2,1)S(1)}, u32[]{:S(2)}, u32[]{:S(2)}) collective-permute-start(bf16[160,3584]{1,0:T(8,128)(2,1)S(1)} %slice.113), channel_id=1, source_target_pairs={{0,1},{1,0},{2,3},{3,2},{4,5},{5,4},{6,7},{7,6},{8,9},{9,8},{10,11... | collective-permute-start | bytes 3440648 | tf_op jit(solution)/shard_map/ppermute | solution.py:23
  144.9 4.5 %slice-start.1 = ((s8[4587520]{0:T(1024)(128)(4,1)}), s8[393216]{0:T(1024)(128)(4,1)S(1)}, s32[]{:S(2)}) async-start(s8[4587520]{0:T(1024)(128)(4,1)} %bitcast.97), calls=%async_computation.1 | async-start | bytes 786432
  145.0 7.3 %slice-start.2 = ((s8[4587520]{0:T(1024)(128)(4,1)}), s8[4194304]{0:T(1024)(128)(4,1)S(1)}, s32[]{:S(2)}) async-start(s8[4587520]{0:T(1024)(128)(4,1)} %bitcast.99), calls=%async_computation.2 | async-start | bytes 8388608
  145.0 70.6 %collective-permute-start.4 = (bf16[80,3584]{1,0:T(8,128)(2,1)S(1)}, bf16[80,3584]{1,0:T(8,128)(2,1)S(1)}, u32[]{:S(2)}, u32[]{:S(2)}) collective-permute-start(bf16[80,3584]{1,0:T(8,128)(2,1)S(1)} %slice.120), channel_id=1, source_target_pairs={{0,2},{1,3},{2,0},{3,1},{4,6},{5,7},{6,4},{7,5},{8,10},{9,11},{10,... | collective-permute-start | bytes 1720328 | tf_op jit(solution)/shard_map/ppermute | solution.py:23
  148.4 3.9 %slice-start.3 = ((s8[4587520]{0:T(1024)(128)(4,1)}), s8[393216]{0:T(1024)(128)(4,1)S(1)}, s32[]{:S(2)}) async-start(s8[4587520]{0:T(1024)(128)(4,1)} %bitcast.99), calls=%async_computation.3 | async-start | bytes 786432
  148.4 49.3 %collective-permute-start.17 = (bf16[80,3584]{1,0:T(8,128)(2,1)S(1)}, bf16[80,3584]{1,0:T(8,128)(2,1)S(1)}, u32[]{:S(2)}, u32[]{:S(2)}) collective-permute-start(bf16[80,3584]{1,0:T(8,128)(2,1)S(1)} %slice.118), channel_id=1, source_target_pairs={{0,2},{1,3},{2,0},{3,1},{4,6},{5,7},{6,4},{7,5},{8,10},{9,11},{10,... | collective-permute-start | bytes 1720328 | tf_op jit(solution)/shard_map/ppermute | solution.py:23
  151.1 34.4 %collective-permute-start.10 = (bf16[80,3584]{1,0:T(8,128)(2,1)S(1)}, bf16[80,3584]{1,0:T(8,128)(2,1)S(1)}, u32[]{:S(2)}, u32[]{:S(2)}) collective-permute-start(bf16[80,3584]{1,0:T(8,128)(2,1)S(1)} %slice.119), channel_id=1, source_target_pairs={{0,2},{1,3},{2,0},{3,1},{4,6},{5,7},{6,4},{7,5},{8,10},{9,11},{10,... | collective-permute-start | bytes 1720328 | tf_op jit(solution)/shard_map/ppermute | solution.py:23
  152.5 44.8 %collective-permute-start.24 = (bf16[80,3584]{1,0:T(8,128)(2,1)S(1)}, bf16[80,3584]{1,0:T(8,128)(2,1)S(1)}, u32[]{:S(2)}, u32[]{:S(2)}) collective-permute-start(bf16[80,3584]{1,0:T(8,128)(2,1)S(1)} %slice.117), channel_id=1, source_target_pairs={{0,2},{1,3},{2,0},{3,1},{4,6},{5,7},{6,4},{7,5},{8,10},{9,11},{10,... | collective-permute-start | bytes 1720328 | tf_op jit(solution)/shard_map/ppermute | solution.py:23
  185.5 14.2 %collective-permute-start.11 = (bf16[80,3584]{1,0:T(8,128)(2,1)S(1)}, bf16[80,3584]{1,0:T(8,128)(2,1)S(1)}, u32[]{:S(2)}, u32[]{:S(2)}) collective-permute-start(bf16[80,3584]{1,0:T(8,128)(2,1)S(1)} %fusion.30), channel_id=1, source_target_pairs={{0,12},{1,13},{2,14},{3,15},{4,0},{5,1},{6,2},{7,3},{8,4},{9,5},{1... | collective-permute-start | bytes 1720328 | tf_op jit(solution)/shard_map/ppermute | solution.py:23
  197.4 17.8 %collective-permute-start.25 = (bf16[80,3584]{1,0:T(8,128)(2,1)S(1)}, bf16[80,3584]{1,0:T(8,128)(2,1)S(1)}, u32[]{:S(2)}, u32[]{:S(2)}) collective-permute-start(bf16[80,3584]{1,0:T(8,128)(2,1)S(1)} %fusion.28), channel_id=1, source_target_pairs={{0,4},{1,5},{2,6},{3,7},{4,8},{5,9},{6,10},{7,11},{8,12},{9,13},{1... | collective-permute-start | bytes 1720328 | tf_op jit(solution)/shard_map/ppermute | solution.py:23
  197.8 39.9 %collective-permute-start.18 = (bf16[80,3584]{1,0:T(8,128)(2,1)S(1)}, bf16[80,3584]{1,0:T(8,128)(2,1)S(1)}, u32[]{:S(2)}, u32[]{:S(2)}) collective-permute-start(bf16[80,3584]{1,0:T(8,128)(2,1)S(1)} %fusion.29), channel_id=1, source_target_pairs={{0,8},{1,9},{2,10},{3,11},{4,12},{5,13},{6,14},{7,15},{8,0},{9,1},... | collective-permute-start | bytes 1720328 | tf_op jit(solution)/shard_map/ppermute | solution.py:23
  237.7 1.4 copy-start.1

commit v2 on v1

v2 whole, which is shorter than its diff:
```python
import jax
import jax.numpy as jnp
from jax import lax
from jax.experimental import pallas as pl
from jax.experimental.pallas import tpu as pltpu
from jax.sharding import PartitionSpec as P

FF = 2048
BF = jnp.bfloat16
F32 = jnp.float32
HALF = 256
WIDE = 512


def ffn_kernel(a, b, c, d, wg, wu, wd, keep, send, rows, hidden, vg, vu, vd, sems):
    n = a.shape[0]
    units = wg.shape[1]
    copies = []
    for j in range(0, units, HALF):
        for src, dst in ((wg, vg), (wu, vu)):
            cols = pl.ds(j, HALF)
            copies.append(
                pltpu.make_async_copy(src.at[:, cols], dst.at[:, cols], sems.at[len(copies)])
            )
    copies.append(pltpu.make_async_copy(wd, vd, sems.at[len(copies)]))
    for copy in copies:
        copy.start()
    for i, piece in enumerate((a, b, c, d)):
        rows[i * n : (i + 1) * n, :] = piece[...]
    for i, j in enumerate(range(0, units, HALF)):
        copies[2 * i].wait()
        gate = jnp.dot(rows[...], vg[:, j : j + HALF], preferred_element_type=F32)
        copies[2 * i + 1].wait()
        up = jnp.dot(rows[...], vu[:, j : j + HALF], preferred_element_type=F32)
        hidden[:, j : j + HALF] = (gate / (1.0 + jnp.exp(-gate)) * up).astype(BF)
    copies[-1].wait()

    @pl.loop(0, vd.shape[1] // WIDE)
    def _(j):
        cols = pl.ds(pl.multiple_of(j * WIDE, WIDE), WIDE)
        part = jnp.dot(hidden[...], vd[:, cols], preferred_element_type=F32)
        keep[:, cols] = part[: 2 * n]
        send[:, cols] = part[2 * n :].astype(BF)


def ffn(pieces, wg, wu, wd):
    n, features = pieces[0].shape
    units = wg.shape[1]
    near = pl.BlockSpec(memory_space=pltpu.VMEM)
    far = pl.BlockSpec(memory_space=pl.ANY)
    return pl.pallas_call(
        ffn_kernel,
        out_shape=(
            jax.ShapeDtypeStruct((2 * n, features), F32),
            jax.ShapeDtypeStruct((2 * n, features), BF),
        ),
        in_specs=[near] * 4 + [far] * 3,
        out_specs=(near, near),
        scratch_shapes=[
            pltpu.VMEM((4 * n, features), BF),
            pltpu.VMEM((4 * n, units), BF),
            pltpu.VMEM((features, units), BF),
            pltpu.VMEM((features, units), BF),
            pltpu.VMEM((units, features), BF),
            pltpu.SemaphoreType.DMA((2 * units // HALF + 1,)),
        ],
        compiler_params=pltpu.CompilerParams(vmem_limit_bytes=30 * 2**20),
        cost_estimate=pl.CostEstimate(
            flops=24 * n * features * units, bytes_accessed=6 * features * units, transcendentals=0
        ),
    )(*pieces, wg, wu, wd)


def after(x, *done):
    done = [d for d in done if d is not None]
    return lax.optimization_barrier((x, *done))[0] if done else x


def local(tokens, expert_ids, gate_weights, w_gate, w_up, w_down):
    tok_rows, features = tokens.shape
    routes = expert_ids.shape[1]
    devices = lax.axis_size("expert")
    shards = FF // w_gate.shape[2]
    experts = devices // shards
    capacity = -(-5 * tok_rows * routes // (4 * experts))
    capacity = -(-capacity // 16) * 16
    me = lax.axis_index("expert") // shards
    wg, wu, wd = w_gate[0], w_up[0], w_down[0]

    def move(x, to):
        return lax.ppermute(x, "expert", [(d, to(d)) for d in range(devices)])

    def turn(x, k):
        return move(x, lambda d: (d + k * shards) % devices)

    def chip(x):
        return move(x, lambda d: d ^ 2)

    def core(x):
        return move(x, lambda d: d ^ 1)

    named = (expert_ids[:, :, None] == jnp.arange(experts, dtype=jnp.int32)).astype(F32)
    both = jnp.sum(named, axis=1)
    earlier = jnp.tril(jnp.ones((tok_rows, tok_rows), F32), -1)
    slot = jnp.dot(earlier, both, preferred_element_type=F32)

    def pack(chunk):
        k, first, size = chunk
        e = (me + k) % experts
        hot = lax.dynamic_index_in_dim(both, e, 1, keepdims=False)
        at = lax.dynamic_index_in_dim(slot, e, 1, keepdims=False)
        slots = jnp.arange(first, first + size, dtype=F32)
        pick = jnp.where((at[None, :] == slots[:, None]) & (hot[None, :] > 0), 1.0, 0.0).astype(BF)
        return jnp.dot(pick, tokens, preferred_element_type=F32).astype(BF)

    def combine(chunk, back):
        k, first, size = chunk
        e = (me + k) % experts
        hot = lax.dynamic_index_in_dim(named, e, 2, keepdims=False)
        at = lax.dynamic_index_in_dim(slot, e, 1, keepdims=False)
        slots = jnp.arange(first, first + size, dtype=F32)
        pick = jnp.where((at[:, None] == slots[None, :]), 1.0, 0.0).astype(BF)
        weight = jnp.sum(hot * gate_weights, axis=1)
        return weight[:, None] * jnp.dot(pick, back, preferred_element_type=F32)

    chunks = [(0, 0, capacity)]
    for k in range(1, (experts + 1) // 2):
        chunks += [(k, 0, capacity), (experts - k, 0, capacity)]
    if experts % 2 == 0:
        head = -(-capacity // 32) * 16
        chunks += [(experts // 2, 0, head)]
        if capacity > head:
            chunks += [(experts // 2, head, capacity - head)]
    count = len(chunks)
    lead = min(4, count)
    order = [("d", i) for i in range(lead)]
    back_next = 1
    for i in range(lead, count):
        order += [("r", back_next), ("d", i)]
        back_next += 1
    order += [("r", i) for i in range(back_next, count)] + [("r", 0)]

    z_last = y_last = None
    here, other, keeps, backs = {}, {}, {}, {}

    for i, chunk in enumerate(chunks):
        x = pack(chunk)
        if chunk[0]:
            x = z_last = turn(after(x, z_last), chunk[0])
        here[i] = x
    for what, i in order:
        if what == "d":
            other[i] = y_last = chip(after(here[i], y_last))
            pieces = (here[i], other[i], core(here[i]), core(other[i]))
            keep, send = ffn(pieces, wg, wu, wd)
            keeps[i] = keep + core(send).astype(F32)
        else:
            n = chunks[i][2]
            y_last = chip(after(keeps[i][n:].astype(BF), y_last))
            back = (keeps[i][:n] + y_last.astype(F32)).astype(BF)
            if chunks[i][0]:
                back = z_last = turn(after(back, z_last), -chunks[i][0])
            backs[i] = back
    total = 0.0
    for i, chunk in enumerate(chunks):
        total = total + combine(chunk, backs[i])
    return total.astype(BF)


def solution(mesh):
    placed = (
        P(("groups", "expert"), None),
        P(("groups", "expert"), None),
        P(("groups", "expert"), None),
        P("expert", None, None),
        P("expert", None, None),
        P("expert", None, None),
    )
    return jax.shard_map(
        local, mesh=mesh, in_specs=placed, out_specs=P(("groups", "expert"), None), check_vma=False
    )
```

time: 240 us -> 156 us (0.65)
  waiting for transfers between devices: 131 us -> 84.1 us
  matrix products: 51.6 us -> 4.87 us
  Pallas kernels: 0 us -> 37.1 us
  local copies, waits for them, and re-layouts: 27.3 us -> 5.06 us
  other arithmetic: 7.62 us -> 2.01 us
    ppermute x26 -> x33, waiting for transfers between devices: 131 us -> 84.1 us  [move(): return lax.ppermute(x, 'expert', [(d, to(d)) for d in range(devices)])]
    dot_general x12 -> x5, matrix products: 48.6 us -> 1.44 us  [pack(): return jnp.dot(pick, tokens, preferred_element_type=F32).astype(BF)]
    pallas_call x0 -> x5, Pallas kernels: none -> 37.1 us  [ffn(): pl.pallas_call(ffn_kernel, out_shape=(jax.ShapeDtypeStruct((2 * n, featur...]
    unnamed x41 -> x16, local copies, waits for them, and re-layouts: 15.4 us -> 4.8 us
    slice x8 -> x5, local copies, waits for them, and re-layouts: 8.84 us -> 0.24 us  [local(): y_last = chip(after(keeps[i][n:].astype(BF), y_last))]
    add x4 -> x6, other arithmetic: 6.48 us -> 0.88 us  [the longest x5 0.87 us: local(): keeps[i] = keep + core(send).astype(F32)]
    concatenate x3 -> x0, local copies, waits for them, and re-layouts: 3.05 us -> none  [expert(): part = ffn(jnp.concatenate([own, other, mate_own, mate_other]))]
    ppermute x26 -> x33, starting transfers between devices: 20.8 us -> 22.2 us  [move(): return lax.ppermute(x, 'expert', [(d, to(d)) for d in range(devices)])]
  transfers between devices with their start and end apart: 26 -> 33, of which waited for: 8 -> 13; matrix products, arithmetic and copies ran while one was open for 34% -> 2% of each run, Pallas kernels for 0% -> 24%
where the time goes in v2:
time: 156 us
  waiting for transfers between devices  84.1 us (54%)
  Pallas kernels  37.1 us (24%)
  starting transfers between devices  22.2 us (14%)
  local copies, waits for them, and re-layouts  5.06 us (3%)
  matrix products  4.87 us (3%)
  other arithmetic  2.01 us (1%)
    ppermute x33, waiting for transfers between devices, move(): return lax.ppermute(x, 'expert', [(d, to(d)) for d in range(devices)])  84.1 us
    pallas_call x5, Pallas kernels, ffn(): pl.pallas_call(ffn_kernel, out_shape=(jax.ShapeDtypeStruct((2 * n, featur...  37.1 us
    ppermute x33, starting transfers between devices, move(): return lax.ppermute(x, 'expert', [(d, to(d)) for d in range(devices)])  22.2 us
    unnamed x16, local copies, waits for them, and re-layouts  4.8 us
    dot_general x5, matrix products, combine(): return weight[:, None] * jnp.dot(pick, back, preferred_element_type=F32)  3.23 us
  transfers between devices with their start and end apart: 33, of which 13 were waited for; matrix products, arithmetic and copies ran while one was open for 2% of the time, Pallas kernels for 24%

profile of v2, /device:TPU:0, one launch (start us, length us, event | category | flops | bytes accessed | tf_op | source)
XLA Modules:
  0.0 155.8 jit_solution(16994915225849126848)
XLA Ops:
  0.0 0.8 fusion.95
  1.2 0.3 convolution_convert_fusion
  1.5 3.1 %collective-permute-start.4 = (bf16[80,3584]{1,0:T(8,128)(2,1)S(1)}, bf16[80,3584]{1,0:T(8,128)(2,1)S(1)}, u32[]{:S(2)}, u32[]{:S(2)}) collective-permute-start(bf16[80,3584]{1,0:T(8,128)(2,1)S(1)} %convolution_convert_fusion), channel_id=1, source_target_pairs={{0,4},{1,5},{2,6},{3,7},{4,8},{5,9},{6,10},{7,11},{8,12},{9,13},{1... | collective-permute-start | bytes 1720328 | tf_op jit(solution)/shard_map/ppermute | solution.py:91
  4.9 1.6 %collective-permute-start = (bf16[80,3584]{1,0:T(8,128)(2,1)S(1)}, bf16[80,3584]{1,0:T(8,128)(2,1)S(1)}, u32[]{:S(2)}, u32[]{:S(2)}) collective-permute-start(bf16[80,3584]{1,0:T(8,128)(2,1)S(1)} %convolution_convert_fusion.2.a), channel_id=1, source_target_pairs={{0,2},{1,3},{2,0},{3,1},{4,6},{5,7},{6,4},{7,5},{8,10},{9,11},{10,... | collective-permute-start | bytes 1720328 | tf_op jit(solution)/shard_map/ppermute | solution.py:91
  6.5 13.1 %collective-permute-done.4.a = bf16[80,3584]{1,0:T(8,128)(2,1)S(1)} collective-permute-done((bf16[80,3584]{1,0:T(8,128)(2,1)S(1)}, bf16[80,3584]{1,0:T(8,128)(2,1)S(1)}, u32[]{:S(2)}, u32[]{:S(2)}) %collective-permute-start.4) | collective-permute-done | bytes 573472 | tf_op jit(solution)/shard_map/ppermute | solution.py:91
  19.6 1.5 collective-permute-start.8
  21.4 2.2 %collective-permute-start.5 = (bf16[80,3584]{1,0:T(8,128)(2,1)S(1)}, bf16[80,3584]{1,0:T(8,128)(2,1)S(1)}, u32[]{:S(2)}, u32[]{:S(2)}) collective-permute-start(bf16[80,3584]{1,0:T(8,128)(2,1)S(1)} %convolution_convert_fusion.1), channel_id=1, source_target_pairs={{0,12},{1,13},{2,14},{3,15},{4,0},{5,1},{6,2},{7,3},{8,4},{9,5},{1... | collective-permute-start | bytes 1720328 | tf_op jit(solution)/shard_map/ppermute | solution.py:91
  23.6 10.2 %collective-permute-done.8.b = bf16[80,3584]{1,0:T(8,128)(2,1)S(1)} collective-permute-done((bf16[80,3584]{1,0:T(8,128)(2,1)S(1)}, bf16[80,3584]{1,0:T(8,128)(2,1)S(1)}, u32[]{:S(2)}, u32[]{:S(2)}) %collective-permute-start.8) | collective-permute-done | bytes 573472 | tf_op jit(solution)/shard_map/ppermute | solution.py:91
  33.8 0.5 collective-permute-start.1
  34.6 0.5 collective-permute-done.5.a
  35.1 2.0 %collective-permute-start.6 = (bf16[48,3584]{1,0:T(8,128)(2,1)S(1)}, bf16[48,3584]{1,0:T(8,128)(2,1)S(1)}, u32[]{:S(2)}, u32[]{:S(2)}) collective-permute-start(bf16[48,3584]{1,0:T(8,128)(2,1)S(1)} %convolution_convert_fusion.3), channel_id=1, source_target_pairs={{0,8},{1,9},{2,10},{3,11},{4,12},{5,13},{6,14},{7,15},{8,0},{9,1},... | collective-permute-start | bytes 1032200 | tf_op jit(solution)/shard_map/ppermute | solution.py:91
  37.1 0.9 collective-permute-start.12
  37.9 2.0 %copy-done.2 = bf16[1,3584,512]{2,1,0:T(8,128)(2,1)S(1)} copy-done((bf16[1,3584,512]{2,1,0:T(8,128)(2,1)S(1)}, bf16[1,3584,512]{2,1,0:T(8,128)(2,1)}, u32[]{:S(2)}) %copy-start.2) | copy-done | bytes 3670040
  40.0 2.0 %copy-done.4 = bf16[1,512,3584]{2,1,0:T(8,128)(2,1)S(1)} copy-done((bf16[1,512,3584]{2,1,0:T(8,128)(2,1)S(1)}, bf16[1,512,3584]{2,1,0:T(8,128)(2,1)}, u32[]{:S(2)}) %copy-start.4) | copy-done | bytes 3670040
  42.0 8.6 %shard_map.65 = (f32[160,3584]{1,0:T(8,128)S(1)}, bf16[160,3584]{1,0:T(8,128)(2,1)S(1)}) custom-call(bf16[80,3584]{1,0:T(8,128)(2,1)S(1)} %collective-permute-done.4.a, bf16[80,3584]{1,0:T(8,128)(2,1)S(1)} %collective-permute-done.8.b, bf16[80,3584]{1,0:T(8,128)(2,1)S(1)} %collective-permute-done.9.c, bf16[80,3584]{1,0:T(8,128)(2,1)S(1)} %collective-permute-done.10.d, ...), custom_call_target="tpu_custom_call" | custom-call | flops 3523215360 | bytes 11010048 | tf_op jit(solution)/shard_map/pallas_call | solution.py:51
  50.7 0.3 convolution_convert_fusion.4
  51.0 2.3 %collective-permute-done.6.a = bf16[48,3584]{1,0:T(8,128)(2,1)S(1)} collective-permute-done((bf16[48,3584]{1,0:T(8,128)(2,1)S(1)}, bf16[48,3584]{1,0:T(8,128)(2,1)S(1)}, u32[]{:S(2)}, u32[]{:S(2)}) %collective-permute-start.6) | collective-permute-done | bytes 344096 | tf_op jit(solution)/shard_map/ppermute | solution.py:91
  53.4 0.5 collective-permute-start.23
  53.9 1.3 collective-permute-start.13
  55.3 8.6 %shard_map.64 = (f32[160,3584]{1,0:T(8,128)S(1)}, bf16[160,3584]{1,0:T(8,128)(2,1)S(1)}) custom-call(bf16[80,3584]{1,0:T(8,128)(2,1)S(1)} %convolution_convert_fusion.2.a, bf16[80,3584]{1,0:T(8,128)(2,1)S(1)} %collective-permute-done.b, bf16[80,3584]{1,0:T(8,128)(2,1)S(1)} %collective-permute-done.1.c, bf16[80,3584]{1,0:T(8,128)(2,1)S(1)} %collective-permute-done.2.d, ...), custom_call_target="tpu_custom_call" | custom-call | flops 3523215360 | bytes 11010048 | tf_op jit(solution)/shard_map/pallas_call | solution.py:51
  64.0 4.1 %collective-permute-done.7.a = bf16[32,3584]{1,0:T(8,128)(2,1)S(1)} collective-permute-done((bf16[32,3584]{1,0:T(8,128)(2,1)S(1)}, bf16[32,3584]{1,0:T(8,128)(2,1)S(1)}, u32[]{:S(2)}, u32[]{:S(2)}) %collective-permute-start.7) | collective-permute-done | bytes 229408 | tf_op jit(solution)/shard_map/ppermute | solution.py:91
  68.2 0.5 collective-permute-start.16
  68.8 8.6 %shard_map.68 = (f32[160,3584]{1,0:T(8,128)S(1)}, bf16[160,3584]{1,0:T(8,128)(2,1)S(1)}) custom-call(bf16[80,3584]{1,0:T(8,128)(2,1)S(1)} %collective-permute-done.5.a, bf16[80,3584]{1,0:T(8,128)(2,1)S(1)} %collective-permute-done.12.b, bf16[80,3584]{1,0:T(8,128)(2,1)S(1)} %collective-permute-done.22.c, bf16[80,3584]{1,0:T(8,128)(2,1)S(1)} %collective-permute-done.23.d, ...), custom_call_target="tpu_custom_call" | custom-call | flops 3523215360 | bytes 11010048 | tf_op jit(solution)/shard_map/pallas_call | solution.py:51
  77.4 0.5 collective-permute-start.24
  78.2 0.8 collective-permute-start.14
  79.3 6.4 %shard_map.67 = (f32[96,3584]{1,0:T(8,128)S(1)}, bf16[96,3584]{1,0:T(8,128)(2,1)S(1)}) custom-call(bf16[48,3584]{1,0:T(8,128)(2,1)S(1)} %collective-permute-done.6.a, bf16[48,3584]{1,0:T(8,128)(2,1)S(1)} %collective-permute-done.13.b, bf16[48,3584]{1,0:T(8,128)(2,1)S(1)} %collective-permute-done.19.c, bf16[48,3584]{1,0:T(8,128)(2,1)S(1)} %collective-permute-done.20.d, ...), custom_call_target="tpu_custom_call" | custom-call | flops 2113929216 | bytes 11010048 | tf_op jit(solution)/shard_map/pallas_call | solution.py:51
  85.8 7.4 %collective-permute-done.14 = bf16[80,3584]{1,0:T(8,128)(2,1)S(1)} collective-permute-done((bf16[80,3584]{1,0:T(8,128)(2,1)S(1)}, bf16[80,3584]{1,0:T(8,128)(2,1)S(1)}, u32[]{:S(2)}, u32[]{:S(2)}) %collective-permute-start.14) | collective-permute-done | bytes 573472 | tf_op jit(solution)/shard_map/ppermute | solution.py:91
  93.2 0.8 collective-permute-start.15
  94.4 1.5 collective-permute-start.29
  95.8 4.1 %collective-permute-done.15.b = bf16[32,3584]{1,0:T(8,128)(2,1)S(1)} collective-permute-done((bf16[32,3584]{1,0:T(8,128)(2,1)S(1)}, bf16[32,3584]{1,0:T(8,128)(2,1)S(1)}, u32[]{:S(2)}, u32[]{:S(2)}) %collective-permute-start.15) | collective-permute-done | bytes 229408 | tf_op jit(solution)/shard_map/ppermute | solution.py:91
  99.9 0.8 collective-permute-start.25
  100.9 1.3 collective-permute-done.17.d
  102.2 0.6 copy-done.3
  102.7 5.0 %shard_map.66 = (f32[64,3584]{1,0:T(8,128)S(1)}, bf16[64,3584]{1,0:T(8,128)(2,1)S(1)}) custom-call(bf16[32,3584]{1,0:T(8,128)(2,1)S(1)} %collective-permute-done.7.a, bf16[32,3584]{1,0:T(8,128)(2,1)S(1)} %collective-permute-done.15.b, bf16[32,3584]{1,0:T(8,128)(2,1)S(1)} %collective-permute-done.16.c, bf16[32,3584]{1,0:T(8,128)(2,1)S(1)} %collective-permute-done.17.d, ...), custom_call_target="tpu_custom_call" | custom-call | flops 1409286144 | bytes 11010048 | tf_op jit(solution)/shard_map/pallas_call | solution.py:51
  107.7 0.6 collective-permute-start.18
  108.3 0.4 convolution_multiply_fusion.3
  108.7 4.4 %collective-permute-done.25 = bf16[80,3584]{1,0:T(8,128)(2,1)S(1)} collective-permute-done((bf16[80,3584]{1,0:T(8,128)(2,1)S(1)}, bf16[80,3584]{1,0:T(8,128)(2,1)S(1)}, u32[]{:S(2)}, u32[]{:S(2)}) %collective-permute-start.25) | collective-permute-done | bytes 573472 | tf_op jit(solution)/shard_map/ppermute | solution.py:91
  113.1 0.8 collective-permute-start.26
  114.2 7.2 %collective-permute-done.26 = bf16[48,3584]{1,0:T(8,128)(2,1)S(1)} collective-permute-done((bf16[48,3584]{1,0:T(8,128)(2,1)S(1)}, bf16[48,3584]{1,0:T(8,128)(2,1)S(1)}, u32[]{:S(2)}, u32[]{:S(2)}) %collective-permute-start.26) | collective-permute-done | bytes 344096 | tf_op jit(solution)/shard_map/ppermute | solution.py:91
  121.4 0.8 collective-permute-start.27
  122.2 7.8 %collective-permute-done.30 = bf16[80,3584]{1,0:T(8,128)(2,1)S(1)} collective-permute-done((bf16[80,3584]{1,0:T(8,128)(2,1)S(1)}, bf16[80,3584]{1,0:T(8,128)(2,1)S(1)}, u32[]{:S(2)}, u32[]{:S(2)}) %collective-permute-start.30) | collective-permute-done | bytes 573472 | tf_op jit(solution)/shard_map/ppermute | solution.py:91
  130.0 1.3 collective-permute-start.28
  131.3 13.7 %collective-permute-done.31 = bf16[48,3584]{1,0:T(8,128)(2,1)S(1)} collective-permute-done((bf16[48,3584]{1,0:T(8,128)(2,1)S(1)}, bf16[48,3584]{1,0:T(8,128)(2,1)S(1)}, u32[]{:S(2)}, u32[]{:S(2)}) %collective-permute-start.31) | collective-permute-done | bytes 344096 | tf_op jit(solution)/shard_map/ppermute | solution.py:91
  145.0 0.4 convolution_multiply_fusion.1
  145.5 8.0 %collective-permute-done.32 = bf16[32,3584]{1,0:T(8,128)(2,1)S(1)} collective-permute-done((bf16[32,3584]{1,0:T(8,128)(2,1)S(1)}, bf16[32,3584]{1,0:T(8,128)(2,1)S(1)}, u32[]{:S(2)}, u32[]{:S(2)}) %collective-permute-start.32) | collective-permute-done | bytes 229408 | tf_op jit(solution)/shard_map/ppermute | solution.py:91
  153.4 0.4 convolution_multiply_fusion
  153.9 0.4 fusion.3
  154.4 1.5 fusion.4
  (71 shorter events, 3.3 us)
Async XLA Ops:
  0.0 1.2 copy-start
  1.5 18.1 %collective-permute-start.4 = (bf16[80,3584]{1,0:T(8,128)(2,1)S(1)}, bf16[80,3584]{1,0:T(8,128)(2,1)S(1)}, u32[]{:S(2)}, u32[]{:S(2)}) collective-permute-start(bf16[80,3584]{1,0:T(8,128)(2,1)S(1)} %convolution_convert_fusion), channel_id=1, source_target_pairs={{0,4},{1,5},{2,6},{3,7},{4,8},{5,9},{6,10},{7,11},{8,12},{9,13},{1... | collective-permute-start | bytes 1720328 | tf_op jit(solution)/shard_map/ppermute | solution.py:91
  4.6 33.4 %copy-start.1 = (bf16[1,3584,512]{2,1,0:T(8,128)(2,1)S(1)}, bf16[1,3584,512]{2,1,0:T(8,128)(2,1)}, u32[]{:S(2)}) copy-start(bf16[1,3584,512]{2,1,0:T(8,128)(2,1)} %param.9) | copy-start | bytes 11010052
  4.9 14.7 %collective-permute-start = (bf16[80,3584]{1,0:T(8,128)(2,1)S(1)}, bf16[80,3584]{1,0:T(8,128)(2,1)S(1)}, u32[]{:S(2)}, u32[]{:S(2)}) collective-permute-start(bf16[80,3584]{1,0:T(8,128)(2,1)S(1)} %convolution_convert_fusion.2.a), channel_id=1, source_target_pairs={{0,2},{1,3},{2,0},{3,1},{4,6},{5,7},{6,4},{7,5},{8,10},{9,11},{10,... | collective-permute-start | bytes 1720328 | tf_op jit(solution)/shard_map/ppermute | solution.py:91
  19.6 14.2 %collective-permute-start.8 = (bf16[80,3584]{1,0:T(8,128)(2,1)S(1)}, bf16[80,3584]{1,0:T(8,128)(2,1)S(1)}, u32[]{:S(2)}, u32[]{:S(2)}) collective-permute-start(bf16[80,3584]{1,0:T(8,128)(2,1)S(1)} %collective-permute-done.4.a), channel_id=1, source_target_pairs={{0,2},{1,3},{2,0},{3,1},{4,6},{5,7},{6,4},{7,5},{8,10},{9,11},{10,... | collective-permute-start | bytes 1720328 | tf_op jit(solution)/shard_map/ppermute | solution.py:91
  21.4 13.7 %collective-permute-start.5 = (bf16[80,3584]{1,0:T(8,128)(2,1)S(1)}, bf16[80,3584]{1,0:T(8,128)(2,1)S(1)}, u32[]{:S(2)}, u32[]{:S(2)}) collective-permute-start(bf16[80,3584]{1,0:T(8,128)(2,1)S(1)} %convolution_convert_fusion.1), channel_id=1, source_target_pairs={{0,12},{1,13},{2,14},{3,15},{4,0},{5,1},{6,2},{7,3},{8,4},{9,5},{1... | collective-permute-start | bytes 1720328 | tf_op jit(solution)/shard_map/ppermute | solution.py:91
  23.6 13.5 %collective-permute-start.9 = (bf16[80,3584]{1,0:T(8,128)(2,1)S(1)}, bf16[80,3584]{1,0:T(8,128)(2,1)S(1)}, u32[]{:S(2)}, u32[]{:S(2)}) collective-permute-start(bf16[80,3584]{1,0:T(8,128)(2,1)S(1)} %collective-permute-done.4.a), channel_id=1, source_target_pairs={{0,1},{1,0},{2,3},{3,2},{4,5},{5,4},{6,7},{7,6},{8,9},{9,8},{10,11... | collective-permute-start | bytes 1720328 | tf_op jit(solution)/shard_map/ppermute | solution.py:91
  33.7 4.2 %collective-permute-start.10 = (bf16[80,3584]{1,0:T(8,128)(2,1)S(1)}, bf16[80,3584]{1,0:T(8,128)(2,1)S(1)}, u32[]{:S(2)}, u32[]{:S(2)}) collective-permute-start(bf16[80,3584]{1,0:T(8,128)(2,1)S(1)} %collective-permute-done.8.b), channel_id=1, source_target_pairs={{0,1},{1,0},{2,3},{3,2},{4,5},{5,4},{6,7},{7,6},{8,9},{9,8},{10,11... | collective-permute-start | bytes 1720328 | tf_op jit(solution)/shard_map/ppermute | solution.py:91
  33.8 20.1 %collective-permute-start.1 = (bf16[80,3584]{1,0:T(8,128)(2,1)S(1)}, bf16[80,3584]{1,0:T(8,128)(2,1)S(1)}, u32[]{:S(2)}, u32[]{:S(2)}) collective-permute-start(bf16[80,3584]{1,0:T(8,128)(2,1)S(1)} %convolution_convert_fusion.2.a), channel_id=1, source_target_pairs={{0,1},{1,0},{2,3},{3,2},{4,5},{5,4},{6,7},{7,6},{8,9},{9,8},{10,11... | collective-permute-start | bytes 1720328 | tf_op jit(solution)/shard_map/ppermute | solution.py:91
  34.5 20.7 %collective-permute-start.2 = (bf16[80,3584]{1,0:T(8,128)(2,1)S(1)}, bf16[80,3584]{1,0:T(8,128)(2,1)S(1)}, u32[]{:S(2)}, u32[]{:S(2)}) collective-permute-start(bf16[80,3584]{1,0:T(8,128)(2,1)S(1)} %collective-permute-done.b), channel_id=1, source_target_pairs={{0,1},{1,0},{2,3},{3,2},{4,5},{5,4},{6,7},{7,6},{8,9},{9,8},{10,11... | collective-permute-start | bytes 1720328 | tf_op jit(solution)/shard_map/ppermute | solution.py:91
  35.1 18.3 %collective-permute-start.6 = (bf16[48,3584]{1,0:T(8,128)(2,1)S(1)}, bf16[48,3584]{1,0:T(8,128)(2,1)S(1)}, u32[]{:S(2)}, u32[]{:S(2)}) collective-permute-start(bf16[48,3584]{1,0:T(8,128)(2,1)S(1)} %convolution_convert_fusion.3), channel_id=1, source_target_pairs={{0,8},{1,9},{2,10},{3,11},{4,12},{5,13},{6,14},{7,15},{8,0},{9,1},... | collective-permute-start | bytes 1032200 | tf_op jit(solution)/shard_map/ppermute | solution.py:91
  37.1 16.3 %collective-permute-start.12 = (bf16[80,3584]{1,0:T(8,128)(2,1)S(1)}, bf16[80,3584]{1,0:T(8,128)(2,1)S(1)}, u32[]{:S(2)}, u32[]{:S(2)}) collective-permute-start(bf16[80,3584]{1,0:T(8,128)(2,1)S(1)} %collective-permute-done.5.a), channel_id=1, source_target_pairs={{0,2},{1,3},{2,0},{3,1},{4,6},{5,7},{6,4},{7,5},{8,10},{9,11},{10,... | collective-permute-start | bytes 1720328 | tf_op jit(solution)/shard_map/ppermute | solution.py:91
  37.9 2.0 %copy-start.2 = (bf16[1,3584,512]{2,1,0:T(8,128)(2,1)S(1)}, bf16[1,3584,512]{2,1,0:T(8,128)(2,1)}, u32[]{:S(2)}) copy-start(bf16[1,3584,512]{2,1,0:T(8,128)(2,1)} %param.10) | copy-start | bytes 11010052
  40.0 2.0 %copy-start.4 = (bf16[1,512,3584]{2,1,0:T(8,128)(2,1)S(1)}, bf16[1,512,3584]{2,1,0:T(8,128)(2,1)}, u32[]{:S(2)}) copy-start(bf16[1,512,3584]{2,1,0:T(8,128)(2,1)} %param.11) | copy-start | bytes 11010052
  42.0 11.8 %copy-start.6 = (s32[128,2]{0,1:T(2,128)S(1)}, s32[128,2]{0,1:T(2,128)}, u32[]{:S(2)}) copy-start(s32[128,2]{0,1:T(2,128)} %param.7) | copy-start | bytes 3076
  42.0 13.2 %copy-start.7 = (f32[128,2]{0,1:T(2,128)S(1)}, f32[128,2]{0,1:T(2,128)}, u32[]{:S(2)}) copy-start(f32[128,2]{0,1:T(2,128)} %param.8) | copy-start | bytes 3076
  50.6 26.7 %collective-permute-start.11 = (bf16[160,3584]{1,0:T(8,128)(2,1)S(1)}, bf16[160,3584]{1,0:T(8,128)(2,1)S(1)}, u32[]{:S(2)}, u32[]{:S(2)}) collective-permute-start(bf16[160,3584]{1,0:T(8,128)(2,1)S(1)} %get-tuple-element.38), channel_id=1, source_target_pairs={{0,1},{1,0},{2,3},{3,2},{4,5},{5,4},{6,7},{7,6},{8,9},{9,8},{10,11... | collective-permute-start | bytes 3440648 | tf_op jit(solution)/shard_map/ppermute | solution.py:91
  53.3 10.6 %collective-permute-start.22 = (bf16[80,3584]{1,0:T(8,128)(2,1)S(1)}, bf16[80,3584]{1,0:T(8,128)(2,1)S(1)}, u32[]{:S(2)}, u32[]{:S(2)}) collective-permute-start(bf16[80,3584]{1,0:T(8,128)(2,1)S(1)} %collective-permute-done.5.a), channel_id=1, source_target_pairs={{0,1},{1,0},{2,3},{3,2},{4,5},{5,4},{6,7},{7,6},{8,9},{9,8},{10,11... | collective-permute-start | bytes 1720328 | tf_op jit(solution)/shard_map/ppermute | solution.py:91
  53.4 15.3 %collective-permute-start.23 = (bf16[80,3584]{1,0:T(8,128)(2,1)S(1)}, bf16[80,3584]{1,0:T(8,128)(2,1)S(1)}, u32[]{:S(2)}, u32[]{:S(2)}) collective-permute-start(bf16[80,3584]{1,0:T(8,128)(2,1)S(1)} %collective-permute-done.12.b), channel_id=1, source_target_pairs={{0,1},{1,0},{2,3},{3,2},{4,5},{5,4},{6,7},{7,6},{8,9},{9,8},{10,11... | collective-permute-start | bytes 1720328 | tf_op jit(solution)/shard_map/ppermute | solution.py:91
  53.9 14.3 %collective-permute-start.13 = (bf16[48,3584]{1,0:T(8,128)(2,1)S(1)}, bf16[48,3584]{1,0:T(8,128)(2,1)S(1)}, u32[]{:S(2)}, u32[]{:S(2)}) collective-permute-start(bf16[48,3584]{1,0:T(8,128)(2,1)S(1)} %collective-permute-done.6.a), channel_id=1, source_target_pairs={{0,2},{1,3},{2,0},{3,1},{4,6},{5,7},{6,4},{7,5},{8,10},{9,11},{10,... | collective-permute-start | bytes 1032200 | tf_op jit(solution)/shard_map/ppermute | solution.py:91
  55.3 12.9 %collective-permute-start.7 = (bf16[32,3584]{1,0:T(8,128)(2,1)S(1)}, bf16[32,3584]{1,0:T(8,128)(2,1)S(1)}, u32[]{:S(2)}, u32[]{:S(2)}) collective-permute-start(bf16[32,3584]{1,0:T(8,128)(2,1)S(1)} %convolution_convert_fusion.4), channel_id=1, source_target_pairs={{0,8},{1,9},{2,10},{3,11},{4,12},{5,13},{6,14},{7,15},{8,0},{9,1},... | collective-permute-start | bytes 688136 | tf_op jit(solution)/shard_map/ppermute | solution.py:91
  63.9 14.2 %collective-permute-start.3 = (bf16[160,3584]{1,0:T(8,128)(2,1)S(1)}, bf16[160,3584]{1,0:T(8,128)(2,1)S(1)}, u32[]{:S(2)}, u32[]{:S(2)}) collective-permute-start(bf16[160,3584]{1,0:T(8,128)(2,1)S(1)} %get-tuple-element.32), channel_id=1, source_target_pairs={{0,1},{1,0},{2,3},{3,2},{4,5},{5,4},{6,7},{7,6},{8,9},{9,8},{10,11... | collective-permute-start | bytes 3440648 | tf_op jit(solution)/shard_map/ppermute | solution.py:91
  68.2 11.1 %collective-permute-start.19 = (bf16[48,3584]{1,0:T(8,128)(2,1)S(1)}, bf16[48,3584]{1,0:T(8,128)(2,1)S(1)}, u32[]{:S(2)}, u32[]{:S(2)}) collective-permute-start(bf16[48,3584]{1,0:T(8,128)(2,1)S(1)} %collective-permute-done.6.a), channel_id=1, source_target_pairs={{0,1},{1,0},{2,3},{3,2},{4,5},{5,4},{6,7},{7,6},{8,9},{9,8},{10,11... | collective-permute-start | bytes 1032200 | tf_op jit(solution)/shard_map/ppermute | solution.py:91
  68.2 32.7 %collective-permute-start.16 = (bf16[32,3584]{1,0:T(8,128)(2,1)S(1)}, bf16[32,3584]{1,0:T(8,128)(2,1)S(1)}, u32[]{:S(2)}, u32[]{:S(2)}) collective-permute-start(bf16[32,3584]{1,0:T(8,128)(2,1)S(1)} %collective-permute-done.7.a), channel_id=1, source_target_pairs={{0,1},{1,0},{2,3},{3,2},{4,5},{5,4},{6,7},{7,6},{8,9},{9,8},{10,11... | collective-permute-start | bytes 688136 | tf_op jit(solution)/shard_map/ppermute | solution.py:91
  68.7 10.6 %collective-permute-start.20 = (bf16[48,3584]{1,0:T(8,128)(2,1)S(1)}, bf16[48,3584]{1,0:T(8,128)(2,1)S(1)}, u32[]{:S(2)}, u32[]{:S(2)}) collective-permute-start(bf16[48,3584]{1,0:T(8,128)(2,1)S(1)} %collective-permute-done.13.b), channel_id=1, source_target_pairs={{0,1},{1,0},{2,3},{3,2},{4,5},{5,4},{6,7},{7,6},{8,9},{9,8},{10,11... | collective-permute-start | bytes 1032200 | tf_op jit(solution)/shard_map/ppermute | solution.py:91
  77.4 16.6 %collective-permute-start.24 = (bf16[160,3584]{1,0:T(8,128)(2,1)S(1)}, bf16[160,3584]{1,0:T(8,128)(2,1)S(1)}, u32[]{:S(2)}, u32[]{:S(2)}) collective-permute-start(bf16[160,3584]{1,0:T(8,128)(2,1)S(1)} %get-tuple-element.48), channel_id=1, source_target_pairs={{0,1},{1,0},{2,3},{3,2},{4,5},{5,4},{6,7},{7,6},{8,9},{9,8},{10,11... | collective-permute-start | bytes 3440648 | tf_op jit(solution)/shard_map/ppermute | solution.py:91
  78.2 15.0 %collective-permute-start.14 = (bf16[80,3584]{1,0:T(8,128)(2,1)S(1)}, bf16[80,3584]{1,0:T(8,128)(2,1)S(1)}, u32[]{:S(2)}, u32[]{:S(2)}) collective-permute-start(bf16[80,3584]{1,0:T(8,128)(2,1)S(1)} %slice.77), channel_id=1, source_target_pairs={{0,2},{1,3},{2,0},{3,1},{4,6},{5,7},{6,4},{7,5},{8,10},{9,11},{10,... | collective-permute-start | bytes 1720328 | tf_op jit(solution)/shard_map/ppermute | solution.py:91
  85.7 15.0 %collective-permute-start.21 = (bf16[96,3584]{1,0:T(8,128)(2,1)S(1)}, bf16[96,3584]{1,0:T(8,128)(2,1)S(1)}, u32[]{:S(2)}, u32[]{:S(2)}) collective-permute-start(bf16[96,3584]{1,0:T(8,128)(2,1)S(1)} %get-tuple-element.46), channel_id=1, source_target_pairs={{0,1},{1,0},{2,3},{3,2},{4,5},{5,4},{6,7},{7,6},{8,9},{9,8},{10,11... | collective-permute-start | bytes 2064392 | tf_op jit(solution)/shard_map/ppermute | solution.py:91
  93.2 6.7 %collective-permute-start.15 = (bf16[32,3584]{1,0:T(8,128)(2,1)S(1)}, bf16[32,3584]{1,0:T(8,128)(2,1)S(1)}, u32[]{:S(2)}, u32[]{:S(2)}) collective-permute-start(bf16[32,3584]{1,0:T(8,128)(2,1)S(1)} %collective-permute-done.7.a), channel_id=1, source_target_pairs={{0,2},{1,3},{2,0},{3,1},{4,6},{5,7},{6,4},{7,5},{8,10},{9,11},{10,... | collective-permute-start | bytes 688136 | tf_op jit(solution)/shard_map/ppermute | solution.py:91
  94.2 8.0 %copy-start.5 = (bf16[1,512,3584]{2,1,0:T(8,128)(2,1)S(1)}, bf16[1,512,3584]{2,1,0:T(8,128)(2,1)}, u32[]{:S(2)}) copy-start(bf16[1,512,3584]{2,1,0:T(8,128)(2,1)} %param.11) | copy-start | bytes 11010052
  94.4 13.9 %collective-permute-start.29 = (bf16[80,3584]{1,0:T(8,128)(2,1)S(1)}, bf16[80,3584]{1,0:T(8,128)(2,1)S(1)}, u32[]{:S(2)}, u32[]{:S(2)}) collective-permute-start(bf16[80,3584]{1,0:T(8,128)(2,1)S(1)} %fusion.6), channel_id=1, source_target_pairs={{0,12},{1,13},{2,14},{3,15},{4,0},{5,1},{6,2},{7,3},{8,4},{9,5},{1... | collective-permute-start | bytes 1720328 | tf_op jit(solution)/shard_map/ppermute | solution.py:91
  99.9 13.2 %collective-permute-start.25 = (bf16[80,3584]{1,0:T(8,128)(2,1)S(1)}, bf16[80,3584]{1,0:T(8,128)(2,1)S(1)}, u32[]{:S(2)}, u32[]{:S(2)}) collective-permute-start(bf16[80,3584]{1,0:T(8,128)(2,1)S(1)} %slice.76), channel_id=1, source_target_pairs={{0,2},{1,3},{2,0},{3,1},{4,6},{5,7},{6,4},{7,5},{8,10},{9,11},{10,... | collective-permute-start | bytes 1720328 | tf_op jit(solution)/shard_map/ppermute | solution.py:91
  100.7 1.5 collective-permute-start.17
  100.7 2.0 %copy-start.3 = (bf16[1,3584,512]{2,1,0:T(8,128)(2,1)S(1)}, bf16[1,3584,512]{2,1,0:T(8,128)(2,1)}, u32[]{:S(2)}) copy-start(bf16[1,3584,512]{2,1,0:T(8,128)(2,1)} %param.10) | copy-start | bytes 11010052
  107.7 6.3 %collective-permute-start.18 = (bf16[64,3584]{1,0:T(8,128)(2,1)S(1)}, bf16[64,3584]{1,0:T(8,128)(2,1)S(1)}, u32[]{:S(2)}, u32[]{:S(2)}) collective-permute-start(bf16[64,3584]{1,0:T(8,128)(2,1)S(1)} %get-tuple-element.44), channel_id=1, source_target_pairs={{0,1},{1,0},{2,3},{3,2},{4,5},{5,4},{6,7},{7,6},{8,9},{9,8},{10,11... | collective-permute-start | bytes 1376264 | tf_op jit(solution)/shard_map/ppermute | solution.py:91
  113.1 8.2 %collective-permute-start.26 = (bf16[48,3584]{1,0:T(8,128)(2,1)S(1)}, bf16[48,3584]{1,0:T(8,128)(2,1)S(1)}, u32[]{:S(2)}, u32[]{:S(2)}) collective-permute-start(bf16[48,3584]{1,0:T(8,128)(2,1)S(1)} %slice.79), channel_id=1, source_target_pairs={{0,2},{1,3},{2,0},{3,1},{4,6},{5,7},{6,4},{7,5},{8,10},{9,11},{10,... | collective-permute-start | bytes 1032200 | tf_op jit(solution)/shard_map/ppermute | solution.py:91
  114.0 16.0 %collective-permute-start.30 = (bf16[80,3584]{1,0:T(8,128)(2,1)S(1)}, bf16[80,3584]{1,0:T(8,128)(2,1)S(1)}, u32[]{:S(2)}, u32[]{:S(2)}) collective-permute-start(bf16[80,3584]{1,0:T(8,128)(2,1)S(1)} %fusion.5), channel_id=1, source_target_pairs={{0,4},{1,5},{2,6},{3,7},{4,8},{5,9},{6,10},{7,11},{8,12},{9,13},{1... | collective-permute-start | bytes 1720328 | tf_op jit(solution)/shard_map/ppermute | solution.py:91
  121.4 8.6 %collective-permute-start.27 = (bf16[32,3584]{1,0:T(8,128)(2,1)S(1)}, bf16[32,3584]{1,0:T(8,128)(2,1)S(1)}, u32[]{:S(2)}, u32[]{:S(2)}) collective-permute-start(bf16[32,3584]{1,0:T(8,128)(2,1)S(1)} %slice.80), channel_id=1, source_target_pairs={{0,2},{1,3},{2,0},{3,1},{4,6},{5,7},{6,4},{7,5},{8,10},{9,11},{10,... | collective-permute-start | bytes 688136 | tf_op jit(solution)/shard_map/ppermute | solution.py:91
  130.0 15.1 %collective-permute-start.31 = (bf16[48,3584]{1,0:T(8,128)(2,1)S(1)}, bf16[48,3584]{1,0:T(8,128)(2,1)S(1)}, u32[]{:S(2)}, u32[]{:S(2)}) collective-permute-start(bf16[48,3584]{1,0:T(8,128)(2,1)S(1)} %fusion.8), channel_id=1, source_target_pairs={{0,8},{1,9},{2,10},{3,11},{4,12},{5,13},{6,14},{7,15},{8,0},{9,1},... | collective-permute-start | bytes 1032200 | tf_op jit(solution)/shard_map/ppermute | solution.py:91
  130.0 23.9 %collective-permute-start.28 = (bf16[80,3584]{1,0:T(8,128)(2,1)S(1)}, bf16[80,3584]{1,0:T(8,128)(2,1)S(1)}, u32[]{:S(2)}, u32[]{:S(2)}) collective-permute-start(bf16[80,3584]{1,0:T(8,128)(2,1)S(1)} %slice.78), channel_id=1, source_target_pairs={{0,2},{1,3},{2,0},{3,1},{4,6},{5,7},{6,4},{7,5},{8,10},{9,11},{10,... | collective-permute-start | bytes 1720328 | tf_op jit(solution)/shard_map/ppermute | solution.py:91
  145.0 8.4 %collective-permute-start.32 = (bf16[32,3584]{1,0:T(8,128)(2,1)S(1)}, bf16[32,3584]{1,0:T(8,128)(2,1)S(1)}, u32[]{:S(2)}, u32[]{:S(2)}) collective-permute-start(bf16[32,3584]{1,0:T(8,128)(2,1)S(1)} %fusion.10), channel_id=1, source_target_pairs={{0,8},{1,9},{2,10},{3,11},{4,12},{5,13},{6,14},{7,15},{8,0},{9,1},... | collective-permute-start | bytes 688136 | tf_op jit(solution)/shard_map/ppermute | solution.py:91

commit v3 on v1

v3 whole, which is shorter than its diff:
```python
import jax
import jax.numpy as jnp
from jax import lax
from jax.experimental import pallas as pl
from jax.experimental.pallas import tpu as pltpu
from jax.sharding import PartitionSpec as P

FF = 2048
BF = jnp.bfloat16
F32 = jnp.float32


def load_kernel(wg, wu, wd, vg, vu, vd, sems):
    copies = [
        pltpu.make_async_copy(src, dst, sems.at[i])
        for i, (src, dst) in enumerate(((wg, vg), (wu, vu), (wd, vd)))
    ]
    for copy in copies:
        copy.start()
    for copy in copies:
        copy.wait()


def load(*weights):
    far = pl.BlockSpec(memory_space=pltpu.HBM)
    near = pl.BlockSpec(memory_space=pltpu.VMEM)
    return pl.pallas_call(
        load_kernel,
        out_shape=[jax.ShapeDtypeStruct(w.shape, w.dtype) for w in weights],
        in_specs=[far] * 3,
        out_specs=[near] * 3,
        scratch_shapes=[pltpu.SemaphoreType.DMA((3,))],
        compiler_params=pltpu.CompilerParams(vmem_limit_bytes=16 * 2**20),
        cost_estimate=pl.CostEstimate(flops=0, bytes_accessed=1024, transcendentals=0),
    )(*weights)


def ffn_kernel(a, b, vg, vu, vd, keep, send, rows, hidden):
    n = a.shape[0]
    rows[:n, :] = a[...]
    rows[n:, :] = b[...]
    gate = jnp.dot(rows[...], vg[...], preferred_element_type=F32)
    up = jnp.dot(rows[...], vu[...], preferred_element_type=F32)
    hidden[...] = (gate / (1.0 + jnp.exp(-gate)) * up).astype(BF)
    wide = vd.shape[1] // 2

    @pl.loop(0, 2)
    def _(j):
        cols = pl.ds(pl.multiple_of(j * wide, 128), wide)
        part = jnp.dot(hidden[...], vd[:, cols], preferred_element_type=F32)
        keep[:, cols] = part[:n]
        send[:, cols] = part[n:].astype(BF)


def ffn(mine, mate, wg, wu, wd):
    n, features = mine.shape
    units = wg.shape[1]
    near = pl.BlockSpec(memory_space=pltpu.VMEM)
    return pl.pallas_call(
        ffn_kernel,
        out_shape=(
            jax.ShapeDtypeStruct((n, features), F32),
            jax.ShapeDtypeStruct((n, features), BF),
        ),
        in_specs=[near] * 5,
        out_specs=(near,) * 2,
        scratch_shapes=[pltpu.VMEM((2 * n, features), BF), pltpu.VMEM((2 * n, units), BF)],
        compiler_params=pltpu.CompilerParams(vmem_limit_bytes=24 * 2**20),
        cost_estimate=pl.CostEstimate(
            flops=48 * n * features * units, bytes_accessed=6 * features * units, transcendentals=0
        ),
    )(mine, mate, wg, wu, wd)


def after(x, *done):
    done = [d for d in done if d is not None]
    return lax.optimization_barrier((x, *done))[0] if done else x


def local(tokens, expert_ids, gate_weights, w_gate, w_up, w_down):
    tok_rows, features = tokens.shape
    routes = expert_ids.shape[1]
    devices = lax.axis_size("expert")
    shards = FF // w_gate.shape[2]
    experts = devices // shards
    capacity = -(-5 * tok_rows * routes // (4 * experts))
    capacity = -(-capacity // 16) * 16
    me = lax.axis_index("expert") // shards

    def move(x, to):
        return lax.ppermute(x, "expert", [(d, to(d)) for d in range(devices)])

    def turn(x, k):
        return move(x, lambda d: (d + k * shards) % devices)

    def chip(x):
        return move(x, lambda d: d ^ 2)

    def core(x):
        return move(x, lambda d: d ^ 1)

    named = (expert_ids[:, :, None] == jnp.arange(experts, dtype=jnp.int32)).astype(F32)
    both = jnp.sum(named, axis=1)
    earlier = jnp.tril(jnp.ones((tok_rows, tok_rows), F32), -1)
    slot = jnp.dot(earlier, both, preferred_element_type=F32)

    def pack(chunk):
        k, first, size = chunk
        e = (me + k) % experts
        hot = lax.dynamic_index_in_dim(both, e, 1, keepdims=False)
        at = lax.dynamic_index_in_dim(slot, e, 1, keepdims=False)
        slots = jnp.arange(first, first + size, dtype=F32)
        pick = jnp.where((at[None, :] == slots[:, None]) & (hot[None, :] > 0), 1.0, 0.0).astype(BF)
        return jnp.dot(pick, tokens, preferred_element_type=F32).astype(BF)

    def combine(chunk, back):
        k, first, size = chunk
        e = (me + k) % experts
        hot = lax.dynamic_index_in_dim(named, e, 2, keepdims=False)
        at = lax.dynamic_index_in_dim(slot, e, 1, keepdims=False)
        slots = jnp.arange(first, first + size, dtype=F32)
        pick = jnp.where((at[:, None] == slots[None, :]), 1.0, 0.0).astype(BF)
        weight = jnp.sum(hot * gate_weights, axis=1)
        return weight[:, None] * jnp.dot(pick, back, preferred_element_type=F32)

    chunks = [(0, 0, capacity)]
    for k in range(1, (experts + 1) // 2):
        chunks += [(k, 0, capacity), (experts - k, 0, capacity)]
    if experts % 2 == 0:
        head = -(-capacity // 32) * 16
        chunks += [(experts // 2, 0, head)]
        if capacity > head:
            chunks += [(experts // 2, head, capacity - head)]
    count = len(chunks)
    live = {}

    def send_out(i):
        with jax.named_scope(f"zout{i}"):
            live["here", i] = turn(live["here", i], chunks[i][0])

    def cross(i):
        with jax.named_scope(f"yout{i}"):
            live["other", i] = chip(live["here", i])

    def work(i):
        mine = jnp.concatenate([live.pop(("here", i)), live.pop(("other", i))])
        with jax.named_scope(f"cout{i}"):
            mate = core(mine)
        with jax.named_scope(f"ffn{i}"):
            live["keep", i], live["send", i] = ffn(mine, mate, live["w", 0], live["w", 1], live["w", 2])

    def swap(i):
        with jax.named_scope(f"cback{i}"):
            live["got", i] = core(live.pop(("send", i)))

    def add(i):
        live["sum", i] = live.pop(("keep", i)) + live.pop(("got", i)).astype(F32)

    def cross_back(i):
        n = chunks[i][2]
        with jax.named_scope(f"yback{i}"):
            total = live.pop(("sum", i))
            got = chip(total[n:].astype(BF))
        live["back", i] = (total[:n] + got.astype(F32)).astype(BF)

    def cross_back_part(i, first, last):
        with jax.named_scope(f"ypart{i}"):
            total = live["sum", i]
            n = chunks[i][2]
            got = chip(total[n + first : n + last].astype(BF))
        live["part", i, first] = (total[first:last] + got.astype(F32)).astype(BF)

    def send_back(i):
        with jax.named_scope(f"zback{i}"):
            live["back", i] = turn(live["back", i], -chunks[i][0])

    def settle():
        keys = list(live)
        for key, value in zip(keys, lax.optimization_barrier([live[key] for key in keys])):
            live[key] = value

    for i, weight in enumerate(load(w_gate[0], w_up[0], w_down[0])):
        live["w", i] = weight
    for i, chunk in enumerate(chunks):
        live["here", i] = pack(chunk)
    if count == 5:
        send_out(1)
        cross(0)
        settle()
        send_out(2)
        cross(1)
        work(0)
        settle()
        send_out(3)
        cross(2)
        swap(0)
        work(1)
        settle()
        send_out(4)
        cross(3)
        swap(1)
        add(0)
        add(1)
        cross_back(1)
        work(2)
        settle()
        swap(2)
        add(2)
        send_back(1)
        cross(4)
        cross_back(2)
        work(3)
        settle()
        swap(3)
        add(3)
        send_back(2)
        cross_back(3)
        cross_back_part(0, 0, 32)
        work(4)
        settle()
        swap(4)
        add(4)
        send_back(3)
        cross_back(4)
        cross_back_part(0, 32, capacity)
        live["back", 0] = jnp.concatenate([live["part", 0, 0], live["part", 0, 32]])
        send_back(4)
    else:
        for i in range(count):
            if i:
                send_out(i)
            cross(i)
            work(i)
            swap(i)
            add(i)
            cross_back(i)
            if i:
                send_back(i)
    backs = [live["back", i] for i in range(count)]
    total = 0.0
    for i, chunk in enumerate(chunks):
        total = total + combine(chunk, backs[i])
    return total.astype(BF)


def solution(mesh):
    placed = (
        P(("groups", "expert"), None),
        P(("groups", "expert"), None),
        P(("groups", "expert"), None),
        P("expert", None, None),
        P("expert", None, None),
        P("expert", None, None),
    )
    return jax.shard_map(
        local, mesh=mesh, in_specs=placed, out_specs=P(("groups", "expert"), None), check_vma=False
    )
```

time: 240 us -> 151 us (0.63)
  matrix products: 51.6 us -> 4.8 us
  waiting for transfers between devices: 131 us -> 91.9 us
  local copies, waits for them, and re-layouts: 27.3 us -> 4.82 us
  Pallas kernels: 0 us -> 17.6 us
  starting transfers between devices: 20.8 us -> 29.4 us
  other arithmetic: 7.62 us -> 2.11 us
    dot_general x12 -> x5, matrix products: 48.6 us -> 1.46 us  [pack(): return jnp.dot(pick, tokens, preferred_element_type=F32).astype(BF)]
    ppermute x26 -> x29, waiting for transfers between devices: 131 us -> 91.9 us  [move(): return lax.ppermute(x, 'expert', [(d, to(d)) for d in range(devices)])]
    pallas_call x0 -> x6, Pallas kernels: none -> 17.6 us  [the longest x5 16.8 us: ffn(): pl.pallas_call(ffn_kernel, out_shape=(jax.ShapeDtypeStruct((n, features),...]
    unnamed x41 -> x19, local copies, waits for them, and re-layouts: 15.4 us -> 4.4 us
    slice x8 -> x6, local copies, waits for them, and re-layouts: 8.84 us -> 0.24 us  [the longest x4 0.18 us: cross_back(): got = chip(total[n:].astype(BF))]
    ppermute x26 -> x29, starting transfers between devices: 20.8 us -> 29.4 us  [move(): return lax.ppermute(x, 'expert', [(d, to(d)) for d in range(devices)])]
    add x4 -> x6, other arithmetic: 6.48 us -> 0.88 us  [the longest x5 0.87 us: add(): live['sum', i] = live.pop(('keep', i)) + live.pop(('got', i)).astype(F32)]
    concatenate x3 -> x5, local copies, waits for them, and re-layouts: 3.05 us -> 0.16 us  [work(): mine = jnp.concatenate([live.pop(('here', i)), live.pop(('other', i))])]
  transfers between devices with their start and end apart: 26 -> 29, of which waited for: 8 -> 15; matrix products, arithmetic and copies ran while one was open for 34% -> 3% of each run, Pallas kernels for 0% -> 12%
where the time goes in v3:
time: 151 us
  waiting for transfers between devices  91.9 us (61%)
  starting transfers between devices  29.4 us (19%)
  Pallas kernels  17.6 us (12%)
  local copies, waits for them, and re-layouts  4.82 us (3%)
  matrix products  4.8 us (3%)
  other arithmetic  2.11 us (1%)
    ppermute x29, waiting for transfers between devices, move(): return lax.ppermute(x, 'expert', [(d, to(d)) for d in range(devices)])  91.9 us
    ppermute x29, starting transfers between devices, move(): return lax.ppermute(x, 'expert', [(d, to(d)) for d in range(devices)])  29.4 us
    pallas_call x5, Pallas kernels, ffn(): pl.pallas_call(ffn_kernel, out_shape=(jax.ShapeDtypeStruct((n, features),...  16.8 us
    unnamed x19, local copies, waits for them, and re-layouts  4.4 us
    dot_general x5, matrix products, combine(): return weight[:, None] * jnp.dot(pick, back, preferred_element_type=F32)  3.14 us
  transfers between devices with their start and end apart: 29, of which 15 were waited for; matrix products, arithmetic and copies ran while one was open for 3% of the time, Pallas kernels for 12%

profile of v3, /device:TPU:0, one launch (start us, length us, event | category | flops | bytes accessed | tf_op | source)
XLA Modules:
  0.0 151.1 jit_solution(336144332058424861)
XLA Ops:
  0.0 0.8 fusion.97
  1.5 3.1 %collective-permute-start = (bf16[80,3584]{1,0:T(8,128)(2,1)S(1)}, bf16[80,3584]{1,0:T(8,128)(2,1)S(1)}, u32[]{:S(2)}, u32[]{:S(2)}) collective-permute-start(bf16[80,3584]{1,0:T(8,128)(2,1)S(1)} %convolution_convert_fusion.1), channel_id=1, source_target_pairs={{0,4},{1,5},{2,6},{3,7},{4,8},{5,9},{6,10},{7,11},{8,12},{9,13},{1... | collective-permute-start | bytes 1720328 | tf_op jit(solution)/shard_map/zout1/ppermute | solution.py:91
  4.9 1.6 %collective-permute-start.1 = (bf16[80,3584]{1,0:T(8,128)(2,1)S(1)}, bf16[80,3584]{1,0:T(8,128)(2,1)S(1)}, u32[]{:S(2)}, u32[]{:S(2)}) collective-permute-start(bf16[80,3584]{1,0:T(8,128)(2,1)S(1)} %convolution_convert_fusion.2), channel_id=1, source_target_pairs={{0,2},{1,3},{2,0},{3,1},{4,6},{5,7},{6,4},{7,5},{8,10},{9,11},{10,... | collective-permute-start | bytes 1720328 | tf_op jit(solution)/shard_map/yout0/ppermute | solution.py:91
  6.8 2.0 %copy-done.3 = bf16[1,3584,512]{2,1,0:T(8,128)(2,1)S(1)} copy-done((bf16[1,3584,512]{2,1,0:T(8,128)(2,1)S(1)}, bf16[1,3584,512]{2,1,0:T(8,128)(2,1)}, u32[]{:S(2)}) %copy-start.3) | copy-done | bytes 3670040
  8.8 2.0 %copy-done.4 = bf16[1,512,3584]{2,1,0:T(8,128)(2,1)S(1)} copy-done((bf16[1,512,3584]{2,1,0:T(8,128)(2,1)S(1)}, bf16[1,512,3584]{2,1,0:T(8,128)(2,1)}, u32[]{:S(2)}) %copy-start.4) | copy-done | bytes 3670040
  10.9 0.8 shard_map.64
  12.2 7.3 %collective-permute-done = bf16[80,3584]{1,0:T(8,128)(2,1)S(1)} collective-permute-done((bf16[80,3584]{1,0:T(8,128)(2,1)S(1)}, bf16[80,3584]{1,0:T(8,128)(2,1)S(1)}, u32[]{:S(2)}, u32[]{:S(2)}) %collective-permute-start) | collective-permute-done | bytes 573472 | tf_op jit(solution)/shard_map/zout1/ppermute | solution.py:91
  19.8 2.2 %collective-permute-start.2 = (bf16[80,3584]{1,0:T(8,128)(2,1)S(1)}, bf16[80,3584]{1,0:T(8,128)(2,1)S(1)}, u32[]{:S(2)}, u32[]{:S(2)}) collective-permute-start(bf16[80,3584]{1,0:T(8,128)(2,1)S(1)} %convolution_convert_fusion), channel_id=1, source_target_pairs={{0,12},{1,13},{2,14},{3,15},{4,0},{5,1},{6,2},{7,3},{8,4},{9,5},{1... | collective-permute-start | bytes 1720328 | tf_op jit(solution)/shard_map/zout2/ppermute | solution.py:91
  21.9 1.5 %collective-permute-start.3 = (bf16[80,3584]{1,0:T(8,128)(2,1)S(1)}, bf16[80,3584]{1,0:T(8,128)(2,1)S(1)}, u32[]{:S(2)}, u32[]{:S(2)}) collective-permute-start(bf16[80,3584]{1,0:T(8,128)(2,1)S(1)} %collective-permute-done), channel_id=1, source_target_pairs={{0,2},{1,3},{2,0},{3,1},{4,6},{5,7},{6,4},{7,5},{8,10},{9,11},{10,... | collective-permute-start | bytes 1720328 | tf_op jit(solution)/shard_map/yout1/ppermute | solution.py:91
  23.5 4.1 %ffn0.1 = (f32[160,3584]{1,0:T(8,128)S(1)}, bf16[160,3584]{1,0:T(8,128)(2,1)S(1)}) custom-call(bf16[160,3584]{1,0:T(8,128)(2,1)S(1)} %constant_dynamic-update-slice_fusion.a, bf16[160,3584]{1,0:T(8,128)(2,1)S(1)} %collective-permute-done.4.b, bf16[3584,512]{1,0:T(8,128)(2,1)S(1)} %get-tuple-element.126.vg, bf16[3584,512]{1,0:T(8,128)(2,1)S(1)} %get-tuple-element.127.vu, ...), custom_call_target="tpu_custom_call" | custom-call | flops 14092861440 | bytes 11010048 | tf_op jit(solution)/shard_map/ffn0/pallas_call | solution.py:59
  27.5 7.6 %collective-permute-done.2 = bf16[80,3584]{1,0:T(8,128)(2,1)S(1)} collective-permute-done((bf16[80,3584]{1,0:T(8,128)(2,1)S(1)}, bf16[80,3584]{1,0:T(8,128)(2,1)S(1)}, u32[]{:S(2)}, u32[]{:S(2)}) %collective-permute-start.2) | collective-permute-done | bytes 573472 | tf_op jit(solution)/shard_map/zout2/ppermute | solution.py:91
  35.1 1.8 %collective-permute-done.3 = bf16[80,3584]{1,0:T(8,128)(2,1)S(1)} collective-permute-done((bf16[80,3584]{1,0:T(8,128)(2,1)S(1)}, bf16[80,3584]{1,0:T(8,128)(2,1)S(1)}, u32[]{:S(2)}, u32[]{:S(2)}) %collective-permute-start.3) | collective-permute-done | bytes 573472 | tf_op jit(solution)/shard_map/yout1/ppermute | solution.py:91
  37.1 0.8 collective-permute-start.5
  37.9 1.5 %collective-permute-start.6 = (bf16[80,3584]{1,0:T(8,128)(2,1)S(1)}, bf16[80,3584]{1,0:T(8,128)(2,1)S(1)}, u32[]{:S(2)}, u32[]{:S(2)}) collective-permute-start(bf16[80,3584]{1,0:T(8,128)(2,1)S(1)} %collective-permute-done.2), channel_id=1, source_target_pairs={{0,2},{1,3},{2,0},{3,1},{4,6},{5,7},{6,4},{7,5},{8,10},{9,11},{10,... | collective-permute-start | bytes 1720328 | tf_op jit(solution)/shard_map/yout2/ppermute | solution.py:91
  39.5 0.5 collective-permute-done.8.b
  39.9 4.1 %ffn1.1 = (f32[160,3584]{1,0:T(8,128)S(1)}, bf16[160,3584]{1,0:T(8,128)(2,1)S(1)}) custom-call(bf16[160,3584]{1,0:T(8,128)(2,1)S(1)} %constant_dynamic-update-slice_fusion.2.a, bf16[160,3584]{1,0:T(8,128)(2,1)S(1)} %collective-permute-done.8.b, bf16[3584,512]{1,0:T(8,128)(2,1)S(1)} %get-tuple-element.126.vg, bf16[3584,512]{1,0:T(8,128)(2,1)S(1)} %get-tuple-element.127.vu, ...), custom_call_target="tpu_custom_call" | custom-call | flops 14092861440 | bytes 11010048 | tf_op jit(solution)/shard_map/ffn1/pallas_call | solution.py:59
  44.0 11.3 %collective-permute-done.5 = bf16[48,3584]{1,0:T(8,128)(2,1)S(1)} collective-permute-done((bf16[48,3584]{1,0:T(8,128)(2,1)S(1)}, bf16[48,3584]{1,0:T(8,128)(2,1)S(1)}, u32[]{:S(2)}, u32[]{:S(2)}) %collective-permute-start.5) | collective-permute-done | bytes 344096 | tf_op jit(solution)/shard_map/zout3/ppermute | solution.py:91
  55.3 1.6 %collective-permute-start.10 = (bf16[48,3584]{1,0:T(8,128)(2,1)S(1)}, bf16[48,3584]{1,0:T(8,128)(2,1)S(1)}, u32[]{:S(2)}, u32[]{:S(2)}) collective-permute-start(bf16[48,3584]{1,0:T(8,128)(2,1)S(1)} %collective-permute-done.5), channel_id=1, source_target_pairs={{0,2},{1,3},{2,0},{3,1},{4,6},{5,7},{6,4},{7,5},{8,10},{9,11},{10,... | collective-permute-start | bytes 1032200 | tf_op jit(solution)/shard_map/yout3/ppermute | solution.py:91
  57.0 0.6 collective-permute-start.13
  57.8 1.9 %collective-permute-done.11 = bf16[160,3584]{1,0:T(8,128)(2,1)S(1)} collective-permute-done((bf16[160,3584]{1,0:T(8,128)(2,1)S(1)}, bf16[160,3584]{1,0:T(8,128)(2,1)S(1)}, u32[]{:S(2)}, u32[]{:S(2)}) %collective-permute-start.11) | collective-permute-done | bytes 1146912 | tf_op jit(solution)/shard_map/cback1/ppermute | solution.py:91
  60.0 0.6 collective-permute-start.12
  60.6 0.8 collective-permute-done.13.b
  61.4 4.1 %ffn2.1 = (f32[160,3584]{1,0:T(8,128)S(1)}, bf16[160,3584]{1,0:T(8,128)(2,1)S(1)}) custom-call(bf16[160,3584]{1,0:T(8,128)(2,1)S(1)} %constant_dynamic-update-slice_fusion.4.a, bf16[160,3584]{1,0:T(8,128)(2,1)S(1)} %collective-permute-done.13.b, bf16[3584,512]{1,0:T(8,128)(2,1)S(1)} %get-tuple-element.126.vg, bf16[3584,512]{1,0:T(8,128)(2,1)S(1)} %get-tuple-element.127.vu, ...), custom_call_target="tpu_custom_call" | custom-call | flops 14092861440 | bytes 11010048 | tf_op jit(solution)/shard_map/ffn2/pallas_call | solution.py:59
  65.4 12.3 %collective-permute-done.12 = bf16[80,3584]{1,0:T(8,128)(2,1)S(1)} collective-permute-done((bf16[80,3584]{1,0:T(8,128)(2,1)S(1)}, bf16[80,3584]{1,0:T(8,128)(2,1)S(1)}, u32[]{:S(2)}, u32[]{:S(2)}) %collective-permute-start.12) | collective-permute-done | bytes 573472 | tf_op jit(solution)/shard_map/yback1/ppermute | solution.py:91
  77.9 2.4 %collective-permute-start.14 = (bf16[80,3584]{1,0:T(8,128)(2,1)S(1)}, bf16[80,3584]{1,0:T(8,128)(2,1)S(1)}, u32[]{:S(2)}, u32[]{:S(2)}) collective-permute-start(bf16[80,3584]{1,0:T(8,128)(2,1)S(1)} %fusion.6), channel_id=1, source_target_pairs={{0,12},{1,13},{2,14},{3,15},{4,0},{5,1},{6,2},{7,3},{8,4},{9,5},{1... | collective-permute-start | bytes 1720328 | tf_op jit(solution)/shard_map/zback1/ppermute | solution.py:91
  80.3 1.5 %collective-permute-start.15 = (bf16[32,3584]{1,0:T(8,128)(2,1)S(1)}, bf16[32,3584]{1,0:T(8,128)(2,1)S(1)}, u32[]{:S(2)}, u32[]{:S(2)}) collective-permute-start(bf16[32,3584]{1,0:T(8,128)(2,1)S(1)} %collective-permute-done.9), channel_id=1, source_target_pairs={{0,2},{1,3},{2,0},{3,1},{4,6},{5,7},{6,4},{7,5},{8,10},{9,11},{10,... | collective-permute-start | bytes 688136 | tf_op jit(solution)/shard_map/yout4/ppermute | solution.py:91
  82.3 0.6 collective-permute-start.17
  82.9 1.2 collective-permute-done.18.b
  84.1 2.7 %ffn3.1 = (f32[96,3584]{1,0:T(8,128)S(1)}, bf16[96,3584]{1,0:T(8,128)(2,1)S(1)}) custom-call(bf16[96,3584]{1,0:T(8,128)(2,1)S(1)} %constant_dynamic-update-slice_fusion.6.a, bf16[96,3584]{1,0:T(8,128)(2,1)S(1)} %collective-permute-done.18.b, bf16[3584,512]{1,0:T(8,128)(2,1)S(1)} %get-tuple-element.126.vg, bf16[3584,512]{1,0:T(8,128)(2,1)S(1)} %get-tuple-element.127.vu, ...), custom_call_target="tpu_custom_call" | custom-call | flops 8455716864 | bytes 11010048 | tf_op jit(solution)/shard_map/ffn3/pallas_call | solution.py:59
  86.8 13.3 %collective-permute-done.17 = bf16[80,3584]{1,0:T(8,128)(2,1)S(1)} collective-permute-done((bf16[80,3584]{1,0:T(8,128)(2,1)S(1)}, bf16[80,3584]{1,0:T(8,128)(2,1)S(1)}, u32[]{:S(2)}, u32[]{:S(2)}) %collective-permute-start.17) | collective-permute-done | bytes 573472 | tf_op jit(solution)/shard_map/yback2/ppermute | solution.py:91
  100.2 0.5 collective-permute-start.19
  100.8 1.6 %collective-permute-start.22 = (bf16[32,3584]{1,0:T(8,128)(2,1)S(1)}, bf16[32,3584]{1,0:T(8,128)(2,1)S(1)}, u32[]{:S(2)}, u32[]{:S(2)}) collective-permute-start(bf16[32,3584]{1,0:T(8,128)(2,1)S(1)} %slice.89), channel_id=1, source_target_pairs={{0,2},{1,3},{2,0},{3,1},{4,6},{5,7},{6,4},{7,5},{8,10},{9,11},{10,... | collective-permute-start | bytes 688136 | tf_op jit(solution)/shard_map/ypart0/ppermute | solution.py:91
  102.8 6.2 %collective-permute-done.22 = bf16[32,3584]{1,0:T(8,128)(2,1)S(1)} collective-permute-done((bf16[32,3584]{1,0:T(8,128)(2,1)S(1)}, bf16[32,3584]{1,0:T(8,128)(2,1)S(1)}, u32[]{:S(2)}, u32[]{:S(2)}) %collective-permute-start.22) | collective-permute-done | bytes 229408 | tf_op jit(solution)/shard_map/ypart0/ppermute | solution.py:91
  109.1 1.6 %collective-permute-start.21 = (bf16[48,3584]{1,0:T(8,128)(2,1)S(1)}, bf16[48,3584]{1,0:T(8,128)(2,1)S(1)}, u32[]{:S(2)}, u32[]{:S(2)}) collective-permute-start(bf16[48,3584]{1,0:T(8,128)(2,1)S(1)} %slice.87), channel_id=1, source_target_pairs={{0,2},{1,3},{2,0},{3,1},{4,6},{5,7},{6,4},{7,5},{8,10},{9,11},{10,... | collective-permute-start | bytes 1032200 | tf_op jit(solution)/shard_map/yback3/ppermute | solution.py:91
  110.7 2.0 %ffn4.1 = (f32[64,3584]{1,0:T(8,128)S(1)}, bf16[64,3584]{1,0:T(8,128)(2,1)S(1)}) custom-call(bf16[64,3584]{1,0:T(8,128)(2,1)S(1)} %constant_dynamic-update-slice_fusion.8.a, bf16[64,3584]{1,0:T(8,128)(2,1)S(1)} %collective-permute-done.23.b, bf16[3584,512]{1,0:T(8,128)(2,1)S(1)} %get-tuple-element.126.vg, bf16[3584,512]{1,0:T(8,128)(2,1)S(1)} %get-tuple-element.127.vu, ...), custom_call_target="tpu_custom_call" | custom-call | flops 5637144576 | bytes 11010048 | tf_op jit(solution)/shard_map/ffn4/pallas_call | solution.py:59
  112.7 6.2 %collective-permute-done.21 = bf16[48,3584]{1,0:T(8,128)(2,1)S(1)} collective-permute-done((bf16[48,3584]{1,0:T(8,128)(2,1)S(1)}, bf16[48,3584]{1,0:T(8,128)(2,1)S(1)}, u32[]{:S(2)}, u32[]{:S(2)}) %collective-permute-start.21) | collective-permute-done | bytes 344096 | tf_op jit(solution)/shard_map/yback3/ppermute | solution.py:91
  119.0 1.6 %collective-permute-start.24 = (bf16[48,3584]{1,0:T(8,128)(2,1)S(1)}, bf16[48,3584]{1,0:T(8,128)(2,1)S(1)}, u32[]{:S(2)}, u32[]{:S(2)}) collective-permute-start(bf16[48,3584]{1,0:T(8,128)(2,1)S(1)} %slice.86), channel_id=1, source_target_pairs={{0,2},{1,3},{2,0},{3,1},{4,6},{5,7},{6,4},{7,5},{8,10},{9,11},{10,... | collective-permute-start | bytes 1032200 | tf_op jit(solution)/shard_map/ypart0/ppermute | solution.py:91
  120.7 2.0 %collective-permute-start.25 = (bf16[48,3584]{1,0:T(8,128)(2,1)S(1)}, bf16[48,3584]{1,0:T(8,128)(2,1)S(1)}, u32[]{:S(2)}, u32[]{:S(2)}) collective-permute-start(bf16[48,3584]{1,0:T(8,128)(2,1)S(1)} %fusion.7), channel_id=1, source_target_pairs={{0,8},{1,9},{2,10},{3,11},{4,12},{5,13},{6,14},{7,15},{8,0},{9,1},... | collective-permute-start | bytes 1032200 | tf_op jit(solution)/shard_map/zback3/ppermute | solution.py:91
  122.7 5.2 %collective-permute-done.24 = bf16[48,3584]{1,0:T(8,128)(2,1)S(1)} collective-permute-done((bf16[48,3584]{1,0:T(8,128)(2,1)S(1)}, bf16[48,3584]{1,0:T(8,128)(2,1)S(1)}, u32[]{:S(2)}, u32[]{:S(2)}) %collective-permute-start.24) | collective-permute-done | bytes 344096 | tf_op jit(solution)/shard_map/ypart0/ppermute | solution.py:91
  127.9 0.4 convolution_multiply_fusion.4
  128.5 1.6 %collective-permute-start.27 = (bf16[32,3584]{1,0:T(8,128)(2,1)S(1)}, bf16[32,3584]{1,0:T(8,128)(2,1)S(1)}, u32[]{:S(2)}, u32[]{:S(2)}) collective-permute-start(bf16[32,3584]{1,0:T(8,128)(2,1)S(1)} %slice.88), channel_id=1, source_target_pairs={{0,2},{1,3},{2,0},{3,1},{4,6},{5,7},{6,4},{7,5},{8,10},{9,11},{10,... | collective-permute-start | bytes 688136 | tf_op jit(solution)/shard_map/yback4/ppermute | solution.py:91
  130.1 0.4 fusion.3
  130.6 4.1 %collective-permute-done.27 = bf16[32,3584]{1,0:T(8,128)(2,1)S(1)} collective-permute-done((bf16[32,3584]{1,0:T(8,128)(2,1)S(1)}, bf16[32,3584]{1,0:T(8,128)(2,1)S(1)}, u32[]{:S(2)}, u32[]{:S(2)}) %collective-permute-start.27) | collective-permute-done | bytes 229408 | tf_op jit(solution)/shard_map/yback4/ppermute | solution.py:91
  134.7 2.0 %collective-permute-start.28 = (bf16[32,3584]{1,0:T(8,128)(2,1)S(1)}, bf16[32,3584]{1,0:T(8,128)(2,1)S(1)}, u32[]{:S(2)}, u32[]{:S(2)}) collective-permute-start(bf16[32,3584]{1,0:T(8,128)(2,1)S(1)} %fusion.11), channel_id=1, source_target_pairs={{0,8},{1,9},{2,10},{3,11},{4,12},{5,13},{6,14},{7,15},{8,0},{9,1},... | collective-permute-start | bytes 688136 | tf_op jit(solution)/shard_map/zback4/ppermute | solution.py:91
  136.6 0.4 fusion.2
  137.1 12.2 %collective-permute-done.28 = bf16[32,3584]{1,0:T(8,128)(2,1)S(1)} collective-permute-done((bf16[32,3584]{1,0:T(8,128)(2,1)S(1)}, bf16[32,3584]{1,0:T(8,128)(2,1)S(1)}, u32[]{:S(2)}, u32[]{:S(2)}) %collective-permute-start.28) | collective-permute-done | bytes 229408 | tf_op jit(solution)/shard_map/zback4/ppermute | solution.py:91
  149.3 0.4 convolution_multiply_fusion
  149.8 1.4 fusion.4
  (75 shorter events, 4.4 us)
Async XLA Ops:
  0.0 1.2 copy-start
  1.2 5.6 %copy-start.2 = (bf16[1,3584,512]{2,1,0:T(8,128)(2,1)S(1)}, bf16[1,3584,512]{2,1,0:T(8,128)(2,1)}, u32[]{:S(2)}) copy-start(bf16[1,3584,512]{2,1,0:T(8,128)(2,1)} %param.9) | copy-start | bytes 11010052
  1.5 18.1 %collective-permute-start = (bf16[80,3584]{1,0:T(8,128)(2,1)S(1)}, bf16[80,3584]{1,0:T(8,128)(2,1)S(1)}, u32[]{:S(2)}, u32[]{:S(2)}) collective-permute-start(bf16[80,3584]{1,0:T(8,128)(2,1)S(1)} %convolution_convert_fusion.1), channel_id=1, source_target_pairs={{0,4},{1,5},{2,6},{3,7},{4,8},{5,9},{6,10},{7,11},{8,12},{9,13},{1... | collective-permute-start | bytes 1720328 | tf_op jit(solution)/shard_map/zout1/ppermute | solution.py:91
  4.9 14.7 %collective-permute-start.1 = (bf16[80,3584]{1,0:T(8,128)(2,1)S(1)}, bf16[80,3584]{1,0:T(8,128)(2,1)S(1)}, u32[]{:S(2)}, u32[]{:S(2)}) collective-permute-start(bf16[80,3584]{1,0:T(8,128)(2,1)S(1)} %convolution_convert_fusion.2), channel_id=1, source_target_pairs={{0,2},{1,3},{2,0},{3,1},{4,6},{5,7},{6,4},{7,5},{8,10},{9,11},{10,... | collective-permute-start | bytes 1720328 | tf_op jit(solution)/shard_map/yout0/ppermute | solution.py:91
  6.8 2.0 %copy-start.3 = (bf16[1,3584,512]{2,1,0:T(8,128)(2,1)S(1)}, bf16[1,3584,512]{2,1,0:T(8,128)(2,1)}, u32[]{:S(2)}) copy-start(bf16[1,3584,512]{2,1,0:T(8,128)(2,1)} %param.10) | copy-start | bytes 11010052
  8.8 2.0 %copy-start.4 = (bf16[1,512,3584]{2,1,0:T(8,128)(2,1)S(1)}, bf16[1,512,3584]{2,1,0:T(8,128)(2,1)}, u32[]{:S(2)}) copy-start(bf16[1,512,3584]{2,1,0:T(8,128)(2,1)} %param.11) | copy-start | bytes 11010052
  19.7 3.8 %collective-permute-start.4 = (bf16[160,3584]{1,0:T(8,128)(2,1)S(1)}, bf16[160,3584]{1,0:T(8,128)(2,1)S(1)}, u32[]{:S(2)}, u32[]{:S(2)}) collective-permute-start(bf16[160,3584]{1,0:T(8,128)(2,1)S(1)} %constant_dynamic-update-slice_fusion.a), channel_id=1, source_target_pairs={{0,1},{1,0},{2,3},{3,2},{4,5},{5,4},{6,7},{7,6},{8,9},{9,8},{10,11... | collective-permute-start | bytes 3440648 | tf_op jit(solution)/shard_map/cout0/ppermute | solution.py:91
  19.8 15.4 %collective-permute-start.2 = (bf16[80,3584]{1,0:T(8,128)(2,1)S(1)}, bf16[80,3584]{1,0:T(8,128)(2,1)S(1)}, u32[]{:S(2)}, u32[]{:S(2)}) collective-permute-start(bf16[80,3584]{1,0:T(8,128)(2,1)S(1)} %convolution_convert_fusion), channel_id=1, source_target_pairs={{0,12},{1,13},{2,14},{3,15},{4,0},{5,1},{6,2},{7,3},{8,4},{9,5},{1... | collective-permute-start | bytes 1720328 | tf_op jit(solution)/shard_map/zout2/ppermute | solution.py:91
  21.9 15.0 %collective-permute-start.3 = (bf16[80,3584]{1,0:T(8,128)(2,1)S(1)}, bf16[80,3584]{1,0:T(8,128)(2,1)S(1)}, u32[]{:S(2)}, u32[]{:S(2)}) collective-permute-start(bf16[80,3584]{1,0:T(8,128)(2,1)S(1)} %collective-permute-done), channel_id=1, source_target_pairs={{0,2},{1,3},{2,0},{3,1},{4,6},{5,7},{6,4},{7,5},{8,10},{9,11},{10,... | collective-permute-start | bytes 1720328 | tf_op jit(solution)/shard_map/yout1/ppermute | solution.py:91
  37.1 2.9 %collective-permute-start.8 = (bf16[160,3584]{1,0:T(8,128)(2,1)S(1)}, bf16[160,3584]{1,0:T(8,128)(2,1)S(1)}, u32[]{:S(2)}, u32[]{:S(2)}) collective-permute-start(bf16[160,3584]{1,0:T(8,128)(2,1)S(1)} %constant_dynamic-update-slice_fusion.2.a), channel_id=1, source_target_pairs={{0,1},{1,0},{2,3},{3,2},{4,5},{5,4},{6,7},{7,6},{8,9},{9,8},{10,11... | collective-permute-start | bytes 3440648 | tf_op jit(solution)/shard_map/cout1/ppermute | solution.py:91
  37.1 18.2 %collective-permute-start.5 = (bf16[48,3584]{1,0:T(8,128)(2,1)S(1)}, bf16[48,3584]{1,0:T(8,128)(2,1)S(1)}, u32[]{:S(2)}, u32[]{:S(2)}) collective-permute-start(bf16[48,3584]{1,0:T(8,128)(2,1)S(1)} %convolution_convert_fusion.3), channel_id=1, source_target_pairs={{0,8},{1,9},{2,10},{3,11},{4,12},{5,13},{6,14},{7,15},{8,0},{9,1},... | collective-permute-start | bytes 1032200 | tf_op jit(solution)/shard_map/zout3/ppermute | solution.py:91
  37.9 17.4 %collective-permute-start.6 = (bf16[80,3584]{1,0:T(8,128)(2,1)S(1)}, bf16[80,3584]{1,0:T(8,128)(2,1)S(1)}, u32[]{:S(2)}, u32[]{:S(2)}) collective-permute-start(bf16[80,3584]{1,0:T(8,128)(2,1)S(1)} %collective-permute-done.2), channel_id=1, source_target_pairs={{0,2},{1,3},{2,0},{3,1},{4,6},{5,7},{6,4},{7,5},{8,10},{9,11},{10,... | collective-permute-start | bytes 1720328 | tf_op jit(solution)/shard_map/yout2/ppermute | solution.py:91
  39.4 15.9 %collective-permute-start.7 = (bf16[160,3584]{1,0:T(8,128)(2,1)S(1)}, bf16[160,3584]{1,0:T(8,128)(2,1)S(1)}, u32[]{:S(2)}, u32[]{:S(2)}) collective-permute-start(bf16[160,3584]{1,0:T(8,128)(2,1)S(1)} %get-tuple-element.96), channel_id=1, source_target_pairs={{0,1},{1,0},{2,3},{3,2},{4,5},{5,4},{6,7},{7,6},{8,9},{9,8},{10,11... | collective-permute-start | bytes 3440648 | tf_op jit(solution)/shard_map/cback0/ppermute | solution.py:91
  55.3 22.5 %collective-permute-start.9 = (bf16[32,3584]{1,0:T(8,128)(2,1)S(1)}, bf16[32,3584]{1,0:T(8,128)(2,1)S(1)}, u32[]{:S(2)}, u32[]{:S(2)}) collective-permute-start(bf16[32,3584]{1,0:T(8,128)(2,1)S(1)} %convolution_convert_fusion.4), channel_id=1, source_target_pairs={{0,8},{1,9},{2,10},{3,11},{4,12},{5,13},{6,14},{7,15},{8,0},{9,1},... | collective-permute-start | bytes 688136 | tf_op jit(solution)/shard_map/zout4/ppermute | solution.py:91
  55.3 22.5 %collective-permute-start.10 = (bf16[48,3584]{1,0:T(8,128)(2,1)S(1)}, bf16[48,3584]{1,0:T(8,128)(2,1)S(1)}, u32[]{:S(2)}, u32[]{:S(2)}) collective-permute-start(bf16[48,3584]{1,0:T(8,128)(2,1)S(1)} %collective-permute-done.5), channel_id=1, source_target_pairs={{0,2},{1,3},{2,0},{3,1},{4,6},{5,7},{6,4},{7,5},{8,10},{9,11},{10,... | collective-permute-start | bytes 1032200 | tf_op jit(solution)/shard_map/yout3/ppermute | solution.py:91
  56.9 2.8 %collective-permute-start.11 = (bf16[160,3584]{1,0:T(8,128)(2,1)S(1)}, bf16[160,3584]{1,0:T(8,128)(2,1)S(1)}, u32[]{:S(2)}, u32[]{:S(2)}) collective-permute-start(bf16[160,3584]{1,0:T(8,128)(2,1)S(1)} %get-tuple-element.109), channel_id=1, source_target_pairs={{0,1},{1,0},{2,3},{3,2},{4,5},{5,4},{6,7},{7,6},{8,9},{9,8},{10,11... | collective-permute-start | bytes 3440648 | tf_op jit(solution)/shard_map/cback1/ppermute | solution.py:91
  57.0 4.3 %collective-permute-start.13 = (bf16[160,3584]{1,0:T(8,128)(2,1)S(1)}, bf16[160,3584]{1,0:T(8,128)(2,1)S(1)}, u32[]{:S(2)}, u32[]{:S(2)}) collective-permute-start(bf16[160,3584]{1,0:T(8,128)(2,1)S(1)} %constant_dynamic-update-slice_fusion.4.a), channel_id=1, source_target_pairs={{0,1},{1,0},{2,3},{3,2},{4,5},{5,4},{6,7},{7,6},{8,9},{9,8},{10,11... | collective-permute-start | bytes 3440648 | tf_op jit(solution)/shard_map/cout2/ppermute | solution.py:91
  60.0 17.7 %collective-permute-start.12 = (bf16[80,3584]{1,0:T(8,128)(2,1)S(1)}, bf16[80,3584]{1,0:T(8,128)(2,1)S(1)}, u32[]{:S(2)}, u32[]{:S(2)}) collective-permute-start(bf16[80,3584]{1,0:T(8,128)(2,1)S(1)} %slice.85), channel_id=1, source_target_pairs={{0,2},{1,3},{2,0},{3,1},{4,6},{5,7},{6,4},{7,5},{8,10},{9,11},{10,... | collective-permute-start | bytes 1720328 | tf_op jit(solution)/shard_map/yback1/ppermute | solution.py:91
  77.8 4.2 %collective-permute-start.16 = (bf16[160,3584]{1,0:T(8,128)(2,1)S(1)}, bf16[160,3584]{1,0:T(8,128)(2,1)S(1)}, u32[]{:S(2)}, u32[]{:S(2)}) collective-permute-start(bf16[160,3584]{1,0:T(8,128)(2,1)S(1)} %get-tuple-element.121), channel_id=1, source_target_pairs={{0,1},{1,0},{2,3},{3,2},{4,5},{5,4},{6,7},{7,6},{8,9},{9,8},{10,11... | collective-permute-start | bytes 3440648 | tf_op jit(solution)/shard_map/cback2/ppermute | solution.py:91
  77.9 22.3 %collective-permute-start.14 = (bf16[80,3584]{1,0:T(8,128)(2,1)S(1)}, bf16[80,3584]{1,0:T(8,128)(2,1)S(1)}, u32[]{:S(2)}, u32[]{:S(2)}) collective-permute-start(bf16[80,3584]{1,0:T(8,128)(2,1)S(1)} %fusion.6), channel_id=1, source_target_pairs={{0,12},{1,13},{2,14},{3,15},{4,0},{5,1},{6,2},{7,3},{8,4},{9,5},{1... | collective-permute-start | bytes 1720328 | tf_op jit(solution)/shard_map/zback1/ppermute | solution.py:91
  80.3 19.9 %collective-permute-start.15 = (bf16[32,3584]{1,0:T(8,128)(2,1)S(1)}, bf16[32,3584]{1,0:T(8,128)(2,1)S(1)}, u32[]{:S(2)}, u32[]{:S(2)}) collective-permute-start(bf16[32,3584]{1,0:T(8,128)(2,1)S(1)} %collective-permute-done.9), channel_id=1, source_target_pairs={{0,2},{1,3},{2,0},{3,1},{4,6},{5,7},{6,4},{7,5},{8,10},{9,11},{10,... | collective-permute-start | bytes 688136 | tf_op jit(solution)/shard_map/yout4/ppermute | solution.py:91
  81.9 2.2 %collective-permute-start.18 = (bf16[96,3584]{1,0:T(8,128)(2,1)S(1)}, bf16[96,3584]{1,0:T(8,128)(2,1)S(1)}, u32[]{:S(2)}, u32[]{:S(2)}) collective-permute-start(bf16[96,3584]{1,0:T(8,128)(2,1)S(1)} %constant_dynamic-update-slice_fusion.6.a), channel_id=1, source_target_pairs={{0,1},{1,0},{2,3},{3,2},{4,5},{5,4},{6,7},{7,6},{8,9},{9,8},{10,11... | collective-permute-start | bytes 2064392 | tf_op jit(solution)/shard_map/cout3/ppermute | solution.py:91
  82.3 17.8 %collective-permute-start.17 = (bf16[80,3584]{1,0:T(8,128)(2,1)S(1)}, bf16[80,3584]{1,0:T(8,128)(2,1)S(1)}, u32[]{:S(2)}, u32[]{:S(2)}) collective-permute-start(bf16[80,3584]{1,0:T(8,128)(2,1)S(1)} %slice.84), channel_id=1, source_target_pairs={{0,2},{1,3},{2,0},{3,1},{4,6},{5,7},{6,4},{7,5},{8,10},{9,11},{10,... | collective-permute-start | bytes 1720328 | tf_op jit(solution)/shard_map/yback2/ppermute | solution.py:91
  100.2 18.7 %collective-permute-start.19 = (bf16[80,3584]{1,0:T(8,128)(2,1)S(1)}, bf16[80,3584]{1,0:T(8,128)(2,1)S(1)}, u32[]{:S(2)}, u32[]{:S(2)}) collective-permute-start(bf16[80,3584]{1,0:T(8,128)(2,1)S(1)} %fusion.5), channel_id=1, source_target_pairs={{0,4},{1,5},{2,6},{3,7},{4,8},{5,9},{6,10},{7,11},{8,12},{9,13},{1... | collective-permute-start | bytes 1720328 | tf_op jit(solution)/shard_map/zback2/ppermute | solution.py:91
  100.8 8.2 %collective-permute-start.20 = (bf16[96,3584]{1,0:T(8,128)(2,1)S(1)}, bf16[96,3584]{1,0:T(8,128)(2,1)S(1)}, u32[]{:S(2)}, u32[]{:S(2)}) collective-permute-start(bf16[96,3584]{1,0:T(8,128)(2,1)S(1)} %get-tuple-element.133), channel_id=1, source_target_pairs={{0,1},{1,0},{2,3},{3,2},{4,5},{5,4},{6,7},{7,6},{8,9},{9,8},{10,11... | collective-permute-start | bytes 2064392 | tf_op jit(solution)/shard_map/cback3/ppermute | solution.py:91
  100.8 8.1 %collective-permute-start.22 = (bf16[32,3584]{1,0:T(8,128)(2,1)S(1)}, bf16[32,3584]{1,0:T(8,128)(2,1)S(1)}, u32[]{:S(2)}, u32[]{:S(2)}) collective-permute-start(bf16[32,3584]{1,0:T(8,128)(2,1)S(1)} %slice.89), channel_id=1, source_target_pairs={{0,2},{1,3},{2,0},{3,1},{4,6},{5,7},{6,4},{7,5},{8,10},{9,11},{10,... | collective-permute-start | bytes 688136 | tf_op jit(solution)/shard_map/ypart0/ppermute | solution.py:91
  102.5 8.3 %collective-permute-start.23 = (bf16[64,3584]{1,0:T(8,128)(2,1)S(1)}, bf16[64,3584]{1,0:T(8,128)(2,1)S(1)}, u32[]{:S(2)}, u32[]{:S(2)}) collective-permute-start(bf16[64,3584]{1,0:T(8,128)(2,1)S(1)} %constant_dynamic-update-slice_fusion.8.a), channel_id=1, source_target_pairs={{0,1},{1,0},{2,3},{3,2},{4,5},{5,4},{6,7},{7,6},{8,9},{9,8},{10,11... | collective-permute-start | bytes 1376264 | tf_op jit(solution)/shard_map/cout4/ppermute | solution.py:91
  109.1 9.8 %collective-permute-start.21 = (bf16[48,3584]{1,0:T(8,128)(2,1)S(1)}, bf16[48,3584]{1,0:T(8,128)(2,1)S(1)}, u32[]{:S(2)}, u32[]{:S(2)}) collective-permute-start(bf16[48,3584]{1,0:T(8,128)(2,1)S(1)} %slice.87), channel_id=1, source_target_pairs={{0,2},{1,3},{2,0},{3,1},{4,6},{5,7},{6,4},{7,5},{8,10},{9,11},{10,... | collective-permute-start | bytes 1032200 | tf_op jit(solution)/shard_map/yback3/ppermute | solution.py:91
  112.7 7.9 %copy-start.5 = (s32[128,2]{0,1:T(2,128)S(1)}, s32[128,2]{0,1:T(2,128)}, u32[]{:S(2)}) copy-start(s32[128,2]{0,1:T(2,128)} %param.7) | copy-start | bytes 3076
  112.7 7.9 %copy-start.6 = (f32[128,2]{0,1:T(2,128)S(1)}, f32[128,2]{0,1:T(2,128)}, u32[]{:S(2)}) copy-start(f32[128,2]{0,1:T(2,128)} %param.8) | copy-start | bytes 3076
  119.0 8.9 %collective-permute-start.24 = (bf16[48,3584]{1,0:T(8,128)(2,1)S(1)}, bf16[48,3584]{1,0:T(8,128)(2,1)S(1)}, u32[]{:S(2)}, u32[]{:S(2)}) collective-permute-start(bf16[48,3584]{1,0:T(8,128)(2,1)S(1)} %slice.86), channel_id=1, source_target_pairs={{0,2},{1,3},{2,0},{3,1},{4,6},{5,7},{6,4},{7,5},{8,10},{9,11},{10,... | collective-permute-start | bytes 1032200 | tf_op jit(solution)/shard_map/ypart0/ppermute | solution.py:91
  120.7 7.8 %collective-permute-start.26 = (bf16[64,3584]{1,0:T(8,128)(2,1)S(1)}, bf16[64,3584]{1,0:T(8,128)(2,1)S(1)}, u32[]{:S(2)}, u32[]{:S(2)}) collective-permute-start(bf16[64,3584]{1,0:T(8,128)(2,1)S(1)} %get-tuple-element.144), channel_id=1, source_target_pairs={{0,1},{1,0},{2,3},{3,2},{4,5},{5,4},{6,7},{7,6},{8,9},{9,8},{10,11... | collective-permute-start | bytes 1376264 | tf_op jit(solution)/shard_map/cback4/ppermute | solution.py:91
  120.7 29.0 %collective-permute-start.25 = (bf16[48,3584]{1,0:T(8,128)(2,1)S(1)}, bf16[48,3584]{1,0:T(8,128)(2,1)S(1)}, u32[]{:S(2)}, u32[]{:S(2)}) collective-permute-start(bf16[48,3584]{1,0:T(8,128)(2,1)S(1)} %fusion.7), channel_id=1, source_target_pairs={{0,8},{1,9},{2,10},{3,11},{4,12},{5,13},{6,14},{7,15},{8,0},{9,1},... | collective-permute-start | bytes 1032200 | tf_op jit(solution)/shard_map/zback3/ppermute | solution.py:91
  128.5 6.1 %collective-permute-start.27 = (bf16[32,3584]{1,0:T(8,128)(2,1)S(1)}, bf16[32,3584]{1,0:T(8,128)(2,1)S(1)}, u32[]{:S(2)}, u32[]{:S(2)}) collective-permute-start(bf16[32,3584]{1,0:T(8,128)(2,1)S(1)} %slice.88), channel_id=1, source_target_pairs={{0,2},{1,3},{2,0},{3,1},{4,6},{5,7},{6,4},{7,5},{8,10},{9,11},{10,... | collective-permute-start | bytes 688136 | tf_op jit(solution)/shard_map/yback4/ppermute | solution.py:91
  134.7 14.6 %collective-permute-start.28 = (bf16[32,3584]{1,0:T(8,128)(2,1)S(1)}, bf16[32,3584]{1,0:T(8,128)(2,1)S(1)}, u32[]{:S(2)}, u32[]{:S(2)}) collective-permute-start(bf16[32,3584]{1,0:T(8,128)(2,1)S(1)} %fusion.11), channel_id=1, source_target_pairs={{0,8},{1,9},{2,10},{3,11},{4,12},{5,13},{6,14},{7,15},{8,0},{9,1},... | collective-permute-start | bytes 688136 | tf_op jit(solution)/shard_map/zback4/ppermute | solution.py:91
  149.3 1.8 %copy-start.1 = (bf16[128,3584]{1,0:T(8,128)(2,1)S(1)}, bf16[128,3584]{1,0:T(8,128)(2,1)}, u32[]{:S(2)}) copy-start(bf16[128,3584]{1,0:T(8,128)(2,1)} %param.6) | copy-start | bytes 2752516

commit v4 on v3

--- a/solution.py
+++ b/solution.py
@@ -190,7 +190,6 @@
         send_out(2)
         cross(1)
         work(0)
-        settle()
         send_out(3)
         cross(2)
         swap(0)
@@ -215,15 +214,13 @@
         add(3)
         send_back(2)
         cross_back(3)
-        cross_back_part(0, 0, 32)
         work(4)
-        settle()
         swap(4)
         add(4)
         send_back(3)
         cross_back(4)
-        cross_back_part(0, 32, capacity)
-        live["back", 0] = jnp.concatenate([live["part", 0, 0], live["part", 0, 32]])
+        live["sum", 0], live["back", 4] = lax.optimization_barrier((live["sum", 0], live["back", 4]))
+        cross_back(0)
         send_back(4)
     else:
         for i in range(count):

time: 151 us -> 143 us (0.947)
  waiting for transfers between devices: 91.9 us -> 86.3 us
  starting transfers between devices: 29.4 us -> 26.5 us
    ppermute x29 -> x28, waiting for transfers between devices: 91.9 us -> 86.3 us  [move(): return lax.ppermute(x, 'expert', [(d, to(d)) for d in range(devices)])]
    ppermute x29 -> x28, starting transfers between devices: 29.4 us -> 26.5 us  [move(): return lax.ppermute(x, 'expert', [(d, to(d)) for d in range(devices)])]
  transfers between devices with their start and end apart: 29 -> 28, of which waited for: 15 -> 15; matrix products, arithmetic and copies ran while one was open for 3% -> 3% of each run, Pallas kernels for 12% -> 12%
where the time goes in v4:
time: 143 us
  waiting for transfers between devices  86.3 us (60%)
  starting transfers between devices  26.5 us (19%)
  Pallas kernels  17.6 us (12%)
  matrix products  4.9 us (3%)
  local copies, waits for them, and re-layouts  4.82 us (3%)
  other arithmetic  2.01 us (1%)
    ppermute x28, waiting for transfers between devices, move(): return lax.ppermute(x, 'expert', [(d, to(d)) for d in range(devices)])  86.3 us
    ppermute x28, starting transfers between devices, move(): return lax.ppermute(x, 'expert', [(d, to(d)) for d in range(devices)])  26.5 us
    pallas_call x5, Pallas kernels, ffn(): pl.pallas_call(ffn_kernel, out_shape=(jax.ShapeDtypeStruct((n, features),...  16.8 us
    unnamed x19, local copies, waits for them, and re-layouts  4.4 us
    dot_general x5, matrix products, combine(): return weight[:, None] * jnp.dot(pick, back, preferred_element_type=F32)  3.24 us
  transfers between devices with their start and end apart: 28, of which 15 were waited for; matrix products, arithmetic and copies ran while one was open for 3% of the time, Pallas kernels for 12%

profile of v4, /device:TPU:0, one launch (start us, length us, event | category | flops | bytes accessed | tf_op | source)
XLA Modules:
  0.0 142.6 jit_solution(8412813915526416541)
XLA Ops:
  0.0 0.8 fusion.93
  1.5 3.1 %collective-permute-start = (bf16[80,3584]{1,0:T(8,128)(2,1)S(1)}, bf16[80,3584]{1,0:T(8,128)(2,1)S(1)}, u32[]{:S(2)}, u32[]{:S(2)}) collective-permute-start(bf16[80,3584]{1,0:T(8,128)(2,1)S(1)} %convolution_convert_fusion.1), channel_id=1, source_target_pairs={{0,4},{1,5},{2,6},{3,7},{4,8},{5,9},{6,10},{7,11},{8,12},{9,13},{1... | collective-permute-start | bytes 1720328 | tf_op jit(solution)/shard_map/zout1/ppermute | solution.py:91
  4.9 1.6 %collective-permute-start.1 = (bf16[80,3584]{1,0:T(8,128)(2,1)S(1)}, bf16[80,3584]{1,0:T(8,128)(2,1)S(1)}, u32[]{:S(2)}, u32[]{:S(2)}) collective-permute-start(bf16[80,3584]{1,0:T(8,128)(2,1)S(1)} %convolution_convert_fusion.2), channel_id=1, source_target_pairs={{0,2},{1,3},{2,0},{3,1},{4,6},{5,7},{6,4},{7,5},{8,10},{9,11},{10,... | collective-permute-start | bytes 1720328 | tf_op jit(solution)/shard_map/yout0/ppermute | solution.py:91
  6.8 2.0 %copy-done.3 = bf16[1,3584,512]{2,1,0:T(8,128)(2,1)S(1)} copy-done((bf16[1,3584,512]{2,1,0:T(8,128)(2,1)S(1)}, bf16[1,3584,512]{2,1,0:T(8,128)(2,1)}, u32[]{:S(2)}) %copy-start.3) | copy-done | bytes 3670040
  8.8 2.0 %copy-done.4 = bf16[1,512,3584]{2,1,0:T(8,128)(2,1)S(1)} copy-done((bf16[1,512,3584]{2,1,0:T(8,128)(2,1)S(1)}, bf16[1,512,3584]{2,1,0:T(8,128)(2,1)}, u32[]{:S(2)}) %copy-start.4) | copy-done | bytes 3670040
  10.9 0.8 shard_map.64
  12.2 7.3 %collective-permute-done = bf16[80,3584]{1,0:T(8,128)(2,1)S(1)} collective-permute-done((bf16[80,3584]{1,0:T(8,128)(2,1)S(1)}, bf16[80,3584]{1,0:T(8,128)(2,1)S(1)}, u32[]{:S(2)}, u32[]{:S(2)}) %collective-permute-start) | collective-permute-done | bytes 573472 | tf_op jit(solution)/shard_map/zout1/ppermute | solution.py:91
  19.8 1.6 %collective-permute-start.7 = (bf16[80,3584]{1,0:T(8,128)(2,1)S(1)}, bf16[80,3584]{1,0:T(8,128)(2,1)S(1)}, u32[]{:S(2)}, u32[]{:S(2)}) collective-permute-start(bf16[80,3584]{1,0:T(8,128)(2,1)S(1)} %collective-permute-done), channel_id=1, source_target_pairs={{0,2},{1,3},{2,0},{3,1},{4,6},{5,7},{6,4},{7,5},{8,10},{9,11},{10,... | collective-permute-start | bytes 1720328 | tf_op jit(solution)/shard_map/yout1/ppermute | solution.py:91
  21.3 2.1 %collective-permute-start.2 = (bf16[80,3584]{1,0:T(8,128)(2,1)S(1)}, bf16[80,3584]{1,0:T(8,128)(2,1)S(1)}, u32[]{:S(2)}, u32[]{:S(2)}) collective-permute-start(bf16[80,3584]{1,0:T(8,128)(2,1)S(1)} %convolution_convert_fusion), channel_id=1, source_target_pairs={{0,12},{1,13},{2,14},{3,15},{4,0},{5,1},{6,2},{7,3},{8,4},{9,5},{1... | collective-permute-start | bytes 1720328 | tf_op jit(solution)/shard_map/zout2/ppermute | solution.py:91
  23.5 0.8 collective-permute-start.3
  24.3 10.9 %collective-permute-done.7 = bf16[80,3584]{1,0:T(8,128)(2,1)S(1)} collective-permute-done((bf16[80,3584]{1,0:T(8,128)(2,1)S(1)}, bf16[80,3584]{1,0:T(8,128)(2,1)S(1)}, u32[]{:S(2)}, u32[]{:S(2)}) %collective-permute-start.7) | collective-permute-done | bytes 573472 | tf_op jit(solution)/shard_map/yout1/ppermute | solution.py:91
  35.3 1.6 %collective-permute-done.2 = bf16[80,3584]{1,0:T(8,128)(2,1)S(1)} collective-permute-done((bf16[80,3584]{1,0:T(8,128)(2,1)S(1)}, bf16[80,3584]{1,0:T(8,128)(2,1)S(1)}, u32[]{:S(2)}, u32[]{:S(2)}) %collective-permute-start.2) | collective-permute-done | bytes 573472 | tf_op jit(solution)/shard_map/zout2/ppermute | solution.py:91
  36.8 0.5 collective-permute-start.5
  37.3 4.1 %ffn0.1 = (f32[160,3584]{1,0:T(8,128)S(1)}, bf16[160,3584]{1,0:T(8,128)(2,1)S(1)}) custom-call(bf16[160,3584]{1,0:T(8,128)(2,1)S(1)} %constant_dynamic-update-slice_fusion.a, bf16[160,3584]{1,0:T(8,128)(2,1)S(1)} %collective-permute-done.4.b, bf16[3584,512]{1,0:T(8,128)(2,1)S(1)} %get-tuple-element.104.vg, bf16[3584,512]{1,0:T(8,128)(2,1)S(1)} %get-tuple-element.105.vu, ...), custom_call_target="tpu_custom_call" | custom-call | flops 14092861440 | bytes 11010048 | tf_op jit(solution)/shard_map/ffn0/pallas_call | solution.py:59
  41.5 4.1 %ffn1.1 = (f32[160,3584]{1,0:T(8,128)S(1)}, bf16[160,3584]{1,0:T(8,128)(2,1)S(1)}) custom-call(bf16[160,3584]{1,0:T(8,128)(2,1)S(1)} %constant_dynamic-update-slice_fusion.2.a, bf16[160,3584]{1,0:T(8,128)(2,1)S(1)} %collective-permute-done.8.b, bf16[3584,512]{1,0:T(8,128)(2,1)S(1)} %get-tuple-element.104.vg, bf16[3584,512]{1,0:T(8,128)(2,1)S(1)} %get-tuple-element.105.vu, ...), custom_call_target="tpu_custom_call" | custom-call | flops 14092861440 | bytes 11010048 | tf_op jit(solution)/shard_map/ffn1/pallas_call | solution.py:59
  45.6 6.3 %collective-permute-done.3 = bf16[48,3584]{1,0:T(8,128)(2,1)S(1)} collective-permute-done((bf16[48,3584]{1,0:T(8,128)(2,1)S(1)}, bf16[48,3584]{1,0:T(8,128)(2,1)S(1)}, u32[]{:S(2)}, u32[]{:S(2)}) %collective-permute-start.3) | collective-permute-done | bytes 344096 | tf_op jit(solution)/shard_map/zout3/ppermute | solution.py:91
  52.0 1.1 collective-permute-start.9
  53.0 1.5 %collective-permute-start.10 = (bf16[48,3584]{1,0:T(8,128)(2,1)S(1)}, bf16[48,3584]{1,0:T(8,128)(2,1)S(1)}, u32[]{:S(2)}, u32[]{:S(2)}) collective-permute-start(bf16[48,3584]{1,0:T(8,128)(2,1)S(1)} %collective-permute-done.3), channel_id=1, source_target_pairs={{0,2},{1,3},{2,0},{3,1},{4,6},{5,7},{6,4},{7,5},{8,10},{9,11},{10,... | collective-permute-start | bytes 1032200 | tf_op jit(solution)/shard_map/yout3/ppermute | solution.py:91
  54.7 0.6 collective-permute-start.13
  55.5 1.9 %collective-permute-done.11 = bf16[160,3584]{1,0:T(8,128)(2,1)S(1)} collective-permute-done((bf16[160,3584]{1,0:T(8,128)(2,1)S(1)}, bf16[160,3584]{1,0:T(8,128)(2,1)S(1)}, u32[]{:S(2)}, u32[]{:S(2)}) %collective-permute-start.11) | collective-permute-done | bytes 1146912 | tf_op jit(solution)/shard_map/cback1/ppermute | solution.py:91
  57.7 0.6 collective-permute-start.12
  58.2 0.8 collective-permute-done.13.b
  59.0 4.1 %ffn2.1 = (f32[160,3584]{1,0:T(8,128)S(1)}, bf16[160,3584]{1,0:T(8,128)(2,1)S(1)}) custom-call(bf16[160,3584]{1,0:T(8,128)(2,1)S(1)} %constant_dynamic-update-slice_fusion.4.a, bf16[160,3584]{1,0:T(8,128)(2,1)S(1)} %collective-permute-done.13.b, bf16[3584,512]{1,0:T(8,128)(2,1)S(1)} %get-tuple-element.104.vg, bf16[3584,512]{1,0:T(8,128)(2,1)S(1)} %get-tuple-element.105.vu, ...), custom_call_target="tpu_custom_call" | custom-call | flops 14092861440 | bytes 11010048 | tf_op jit(solution)/shard_map/ffn2/pallas_call | solution.py:59
  63.1 10.5 %collective-permute-done.12 = bf16[80,3584]{1,0:T(8,128)(2,1)S(1)} collective-permute-done((bf16[80,3584]{1,0:T(8,128)(2,1)S(1)}, bf16[80,3584]{1,0:T(8,128)(2,1)S(1)}, u32[]{:S(2)}, u32[]{:S(2)}) %collective-permute-start.12) | collective-permute-done | bytes 573472 | tf_op jit(solution)/shard_map/yback1/ppermute | solution.py:91
  73.8 4.0 %collective-permute-start.14 = (bf16[80,3584]{1,0:T(8,128)(2,1)S(1)}, bf16[80,3584]{1,0:T(8,128)(2,1)S(1)}, u32[]{:S(2)}, u32[]{:S(2)}) collective-permute-start(bf16[80,3584]{1,0:T(8,128)(2,1)S(1)} %fusion.6), channel_id=1, source_target_pairs={{0,12},{1,13},{2,14},{3,15},{4,0},{5,1},{6,2},{7,3},{8,4},{9,5},{1... | collective-permute-start | bytes 1720328 | tf_op jit(solution)/shard_map/zback1/ppermute | solution.py:91
  77.8 0.5 collective-permute-start.15
  78.8 1.6 %collective-permute-start.17 = (bf16[80,3584]{1,0:T(8,128)(2,1)S(1)}, bf16[80,3584]{1,0:T(8,128)(2,1)S(1)}, u32[]{:S(2)}, u32[]{:S(2)}) collective-permute-start(bf16[80,3584]{1,0:T(8,128)(2,1)S(1)} %slice.74), channel_id=1, source_target_pairs={{0,2},{1,3},{2,0},{3,1},{4,6},{5,7},{6,4},{7,5},{8,10},{9,11},{10,... | collective-permute-start | bytes 1720328 | tf_op jit(solution)/shard_map/yback2/ppermute | solution.py:91
  80.6 2.7 %ffn3.1 = (f32[96,3584]{1,0:T(8,128)S(1)}, bf16[96,3584]{1,0:T(8,128)(2,1)S(1)}) custom-call(bf16[96,3584]{1,0:T(8,128)(2,1)S(1)} %constant_dynamic-update-slice_fusion.6.a, bf16[96,3584]{1,0:T(8,128)(2,1)S(1)} %collective-permute-done.18.b, bf16[3584,512]{1,0:T(8,128)(2,1)S(1)} %get-tuple-element.104.vg, bf16[3584,512]{1,0:T(8,128)(2,1)S(1)} %get-tuple-element.105.vu, ...), custom_call_target="tpu_custom_call" | custom-call | flops 8455716864 | bytes 11010048 | tf_op jit(solution)/shard_map/ffn3/pallas_call | solution.py:59
  83.3 14.3 %collective-permute-done.17 = bf16[80,3584]{1,0:T(8,128)(2,1)S(1)} collective-permute-done((bf16[80,3584]{1,0:T(8,128)(2,1)S(1)}, bf16[80,3584]{1,0:T(8,128)(2,1)S(1)}, u32[]{:S(2)}, u32[]{:S(2)}) %collective-permute-start.17) | collective-permute-done | bytes 573472 | tf_op jit(solution)/shard_map/yback2/ppermute | solution.py:91
  97.9 0.5 collective-permute-start.24
  98.4 0.5 collective-permute-start.23
  99.0 0.7 collective-permute-done.19.b
  99.7 2.0 %ffn4.1 = (f32[64,3584]{1,0:T(8,128)S(1)}, bf16[64,3584]{1,0:T(8,128)(2,1)S(1)}) custom-call(bf16[64,3584]{1,0:T(8,128)(2,1)S(1)} %constant_dynamic-update-slice_fusion.8.a, bf16[64,3584]{1,0:T(8,128)(2,1)S(1)} %collective-permute-done.19.b, bf16[3584,512]{1,0:T(8,128)(2,1)S(1)} %get-tuple-element.104.vg, bf16[3584,512]{1,0:T(8,128)(2,1)S(1)} %get-tuple-element.105.vu, ...), custom_call_target="tpu_custom_call" | custom-call | flops 5637144576 | bytes 11010048 | tf_op jit(solution)/shard_map/ffn4/pallas_call | solution.py:59
  102.0 0.6 collective-permute-start.25
  102.6 0.9 collective-permute-done.20
  103.6 0.7 collective-permute-start.21
  104.3 8.7 %collective-permute-done.25 = bf16[48,3584]{1,0:T(8,128)(2,1)S(1)} collective-permute-done((bf16[48,3584]{1,0:T(8,128)(2,1)S(1)}, bf16[48,3584]{1,0:T(8,128)(2,1)S(1)}, u32[]{:S(2)}, u32[]{:S(2)}) %collective-permute-start.25) | collective-permute-done | bytes 344096 | tf_op jit(solution)/shard_map/yback3/ppermute | solution.py:91
  113.0 1.7 %collective-permute-start.26 = (bf16[48,3584]{1,0:T(8,128)(2,1)S(1)}, bf16[48,3584]{1,0:T(8,128)(2,1)S(1)}, u32[]{:S(2)}, u32[]{:S(2)}) collective-permute-start(bf16[48,3584]{1,0:T(8,128)(2,1)S(1)} %fusion.7), channel_id=1, source_target_pairs={{0,8},{1,9},{2,10},{3,11},{4,12},{5,13},{6,14},{7,15},{8,0},{9,1},... | collective-permute-start | bytes 1032200 | tf_op jit(solution)/shard_map/zback3/ppermute | solution.py:91
  114.8 2.6 %collective-permute-done.21 = bf16[32,3584]{1,0:T(8,128)(2,1)S(1)} collective-permute-done((bf16[32,3584]{1,0:T(8,128)(2,1)S(1)}, bf16[32,3584]{1,0:T(8,128)(2,1)S(1)}, u32[]{:S(2)}, u32[]{:S(2)}) %collective-permute-start.21) | collective-permute-done | bytes 229408 | tf_op jit(solution)/shard_map/yback4/ppermute | solution.py:91
  117.5 0.6 collective-permute-start.22
  118.0 0.4 convolution_multiply_fusion.3
  118.5 1.7 %collective-permute-start.27 = (bf16[32,3584]{1,0:T(8,128)(2,1)S(1)}, bf16[32,3584]{1,0:T(8,128)(2,1)S(1)}, u32[]{:S(2)}, u32[]{:S(2)}) collective-permute-start(bf16[32,3584]{1,0:T(8,128)(2,1)S(1)} %fusion.8), channel_id=1, source_target_pairs={{0,8},{1,9},{2,10},{3,11},{4,12},{5,13},{6,14},{7,15},{8,0},{9,1},... | collective-permute-start | bytes 688136 | tf_op jit(solution)/shard_map/zback4/ppermute | solution.py:91
  120.2 15.9 %collective-permute-done.26 = bf16[48,3584]{1,0:T(8,128)(2,1)S(1)} collective-permute-done((bf16[48,3584]{1,0:T(8,128)(2,1)S(1)}, bf16[48,3584]{1,0:T(8,128)(2,1)S(1)}, u32[]{:S(2)}, u32[]{:S(2)}) %collective-permute-start.26) | collective-permute-done | bytes 344096 | tf_op jit(solution)/shard_map/zback3/ppermute | solution.py:91
  136.1 0.4 convolution_multiply_fusion.1
  136.5 3.7 %collective-permute-done.27 = bf16[32,3584]{1,0:T(8,128)(2,1)S(1)} collective-permute-done((bf16[32,3584]{1,0:T(8,128)(2,1)S(1)}, bf16[32,3584]{1,0:T(8,128)(2,1)S(1)}, u32[]{:S(2)}, u32[]{:S(2)}) %collective-permute-start.27) | collective-permute-done | bytes 229408 | tf_op jit(solution)/shard_map/zback4/ppermute | solution.py:91
  140.2 0.4 convolution_multiply_fusion
  140.6 0.4 fusion.3
  141.1 1.5 %fusion.4 = bf16[128,3584]{1,0:T(8,128)(2,1)} fusion(f32[128,3584]{1,0:T(8,128)S(1)} %convolution_multiply_fusion, f32[128,3584]{1,0:T(8,128)S(1)} %convolution_multiply_fusion.1, f32[128,3584]{1,0:T(8,128)S(1)} %fusion.3, bf16[80,3584]{1,0:T(8,128)(2,1)S(1)} %collective-permute-done.23, f32[128]{0:T(128)S(1)} %get-tuple-element.115, ...), kind=kOutput, calls=%fused_computation.9 | convolution fusion | flops 75724800 | bytes 6996992 | tf_op jit(solution)/shard_map/dot_general | solution.py:124
  (70 shorter events, 4.5 us)
Async XLA Ops:
  0.0 1.2 copy-start
  1.2 5.6 %copy-start.2 = (bf16[1,3584,512]{2,1,0:T(8,128)(2,1)S(1)}, bf16[1,3584,512]{2,1,0:T(8,128)(2,1)}, u32[]{:S(2)}) copy-start(bf16[1,3584,512]{2,1,0:T(8,128)(2,1)} %param.9) | copy-start | bytes 11010052
  1.5 18.1 %collective-permute-start = (bf16[80,3584]{1,0:T(8,128)(2,1)S(1)}, bf16[80,3584]{1,0:T(8,128)(2,1)S(1)}, u32[]{:S(2)}, u32[]{:S(2)}) collective-permute-start(bf16[80,3584]{1,0:T(8,128)(2,1)S(1)} %convolution_convert_fusion.1), channel_id=1, source_target_pairs={{0,4},{1,5},{2,6},{3,7},{4,8},{5,9},{6,10},{7,11},{8,12},{9,13},{1... | collective-permute-start | bytes 1720328 | tf_op jit(solution)/shard_map/zout1/ppermute | solution.py:91
  4.9 14.7 %collective-permute-start.1 = (bf16[80,3584]{1,0:T(8,128)(2,1)S(1)}, bf16[80,3584]{1,0:T(8,128)(2,1)S(1)}, u32[]{:S(2)}, u32[]{:S(2)}) collective-permute-start(bf16[80,3584]{1,0:T(8,128)(2,1)S(1)} %convolution_convert_fusion.2), channel_id=1, source_target_pairs={{0,2},{1,3},{2,0},{3,1},{4,6},{5,7},{6,4},{7,5},{8,10},{9,11},{10,... | collective-permute-start | bytes 1720328 | tf_op jit(solution)/shard_map/yout0/ppermute | solution.py:91
  6.8 2.0 %copy-start.3 = (bf16[1,3584,512]{2,1,0:T(8,128)(2,1)S(1)}, bf16[1,3584,512]{2,1,0:T(8,128)(2,1)}, u32[]{:S(2)}) copy-start(bf16[1,3584,512]{2,1,0:T(8,128)(2,1)} %param.10) | copy-start | bytes 11010052
  8.8 2.0 %copy-start.4 = (bf16[1,512,3584]{2,1,0:T(8,128)(2,1)S(1)}, bf16[1,512,3584]{2,1,0:T(8,128)(2,1)}, u32[]{:S(2)}) copy-start(bf16[1,512,3584]{2,1,0:T(8,128)(2,1)} %param.11) | copy-start | bytes 11010052
  19.7 17.7 %collective-permute-start.4 = (bf16[160,3584]{1,0:T(8,128)(2,1)S(1)}, bf16[160,3584]{1,0:T(8,128)(2,1)S(1)}, u32[]{:S(2)}, u32[]{:S(2)}) collective-permute-start(bf16[160,3584]{1,0:T(8,128)(2,1)S(1)} %constant_dynamic-update-slice_fusion.a), channel_id=1, source_target_pairs={{0,1},{1,0},{2,3},{3,2},{4,5},{5,4},{6,7},{7,6},{8,9},{9,8},{10,11... | collective-permute-start | bytes 3440648 | tf_op jit(solution)/shard_map/cout0/ppermute | solution.py:91
  19.8 15.4 %collective-permute-start.7 = (bf16[80,3584]{1,0:T(8,128)(2,1)S(1)}, bf16[80,3584]{1,0:T(8,128)(2,1)S(1)}, u32[]{:S(2)}, u32[]{:S(2)}) collective-permute-start(bf16[80,3584]{1,0:T(8,128)(2,1)S(1)} %collective-permute-done), channel_id=1, source_target_pairs={{0,2},{1,3},{2,0},{3,1},{4,6},{5,7},{6,4},{7,5},{8,10},{9,11},{10,... | collective-permute-start | bytes 1720328 | tf_op jit(solution)/shard_map/yout1/ppermute | solution.py:91
  21.3 15.5 %collective-permute-start.2 = (bf16[80,3584]{1,0:T(8,128)(2,1)S(1)}, bf16[80,3584]{1,0:T(8,128)(2,1)S(1)}, u32[]{:S(2)}, u32[]{:S(2)}) collective-permute-start(bf16[80,3584]{1,0:T(8,128)(2,1)S(1)} %convolution_convert_fusion), channel_id=1, source_target_pairs={{0,12},{1,13},{2,14},{3,15},{4,0},{5,1},{6,2},{7,3},{8,4},{9,5},{1... | collective-permute-start | bytes 1720328 | tf_op jit(solution)/shard_map/zout2/ppermute | solution.py:91
  23.5 28.4 %collective-permute-start.3 = (bf16[48,3584]{1,0:T(8,128)(2,1)S(1)}, bf16[48,3584]{1,0:T(8,128)(2,1)S(1)}, u32[]{:S(2)}, u32[]{:S(2)}) collective-permute-start(bf16[48,3584]{1,0:T(8,128)(2,1)S(1)} %convolution_convert_fusion.3), channel_id=1, source_target_pairs={{0,8},{1,9},{2,10},{3,11},{4,12},{5,13},{6,14},{7,15},{8,0},{9,1},... | collective-permute-start | bytes 1032200 | tf_op jit(solution)/shard_map/zout3/ppermute | solution.py:91
  35.2 6.3 %collective-permute-start.8 = (bf16[160,3584]{1,0:T(8,128)(2,1)S(1)}, bf16[160,3584]{1,0:T(8,128)(2,1)S(1)}, u32[]{:S(2)}, u32[]{:S(2)}) collective-permute-start(bf16[160,3584]{1,0:T(8,128)(2,1)S(1)} %constant_dynamic-update-slice_fusion.2.a), channel_id=1, source_target_pairs={{0,1},{1,0},{2,3},{3,2},{4,5},{5,4},{6,7},{7,6},{8,9},{9,8},{10,11... | collective-permute-start | bytes 3440648 | tf_op jit(solution)/shard_map/cout1/ppermute | solution.py:91
  36.8 15.1 %collective-permute-start.5 = (bf16[80,3584]{1,0:T(8,128)(2,1)S(1)}, bf16[80,3584]{1,0:T(8,128)(2,1)S(1)}, u32[]{:S(2)}, u32[]{:S(2)}) collective-permute-start(bf16[80,3584]{1,0:T(8,128)(2,1)S(1)} %collective-permute-done.2), channel_id=1, source_target_pairs={{0,2},{1,3},{2,0},{3,1},{4,6},{5,7},{6,4},{7,5},{8,10},{9,11},{10,... | collective-permute-start | bytes 1720328 | tf_op jit(solution)/shard_map/yout2/ppermute | solution.py:91
  41.4 10.5 %collective-permute-start.6 = (bf16[160,3584]{1,0:T(8,128)(2,1)S(1)}, bf16[160,3584]{1,0:T(8,128)(2,1)S(1)}, u32[]{:S(2)}, u32[]{:S(2)}) collective-permute-start(bf16[160,3584]{1,0:T(8,128)(2,1)S(1)} %get-tuple-element.72), channel_id=1, source_target_pairs={{0,1},{1,0},{2,3},{3,2},{4,5},{5,4},{6,7},{7,6},{8,9},{9,8},{10,11... | collective-permute-start | bytes 3440648 | tf_op jit(solution)/shard_map/cback0/ppermute | solution.py:91
  52.0 21.8 %collective-permute-start.9 = (bf16[32,3584]{1,0:T(8,128)(2,1)S(1)}, bf16[32,3584]{1,0:T(8,128)(2,1)S(1)}, u32[]{:S(2)}, u32[]{:S(2)}) collective-permute-start(bf16[32,3584]{1,0:T(8,128)(2,1)S(1)} %convolution_convert_fusion.4), channel_id=1, source_target_pairs={{0,8},{1,9},{2,10},{3,11},{4,12},{5,13},{6,14},{7,15},{8,0},{9,1},... | collective-permute-start | bytes 688136 | tf_op jit(solution)/shard_map/zout4/ppermute | solution.py:91
  53.0 20.7 %collective-permute-start.10 = (bf16[48,3584]{1,0:T(8,128)(2,1)S(1)}, bf16[48,3584]{1,0:T(8,128)(2,1)S(1)}, u32[]{:S(2)}, u32[]{:S(2)}) collective-permute-start(bf16[48,3584]{1,0:T(8,128)(2,1)S(1)} %collective-permute-done.3), channel_id=1, source_target_pairs={{0,2},{1,3},{2,0},{3,1},{4,6},{5,7},{6,4},{7,5},{8,10},{9,11},{10,... | collective-permute-start | bytes 1032200 | tf_op jit(solution)/shard_map/yout3/ppermute | solution.py:91
  54.6 2.8 %collective-permute-start.11 = (bf16[160,3584]{1,0:T(8,128)(2,1)S(1)}, bf16[160,3584]{1,0:T(8,128)(2,1)S(1)}, u32[]{:S(2)}, u32[]{:S(2)}) collective-permute-start(bf16[160,3584]{1,0:T(8,128)(2,1)S(1)} %get-tuple-element.84), channel_id=1, source_target_pairs={{0,1},{1,0},{2,3},{3,2},{4,5},{5,4},{6,7},{7,6},{8,9},{9,8},{10,11... | collective-permute-start | bytes 3440648 | tf_op jit(solution)/shard_map/cback1/ppermute | solution.py:91
  54.7 4.3 %collective-permute-start.13 = (bf16[160,3584]{1,0:T(8,128)(2,1)S(1)}, bf16[160,3584]{1,0:T(8,128)(2,1)S(1)}, u32[]{:S(2)}, u32[]{:S(2)}) collective-permute-start(bf16[160,3584]{1,0:T(8,128)(2,1)S(1)} %constant_dynamic-update-slice_fusion.4.a), channel_id=1, source_target_pairs={{0,1},{1,0},{2,3},{3,2},{4,5},{5,4},{6,7},{7,6},{8,9},{9,8},{10,11... | collective-permute-start | bytes 3440648 | tf_op jit(solution)/shard_map/cout2/ppermute | solution.py:91
  57.7 16.0 %collective-permute-start.12 = (bf16[80,3584]{1,0:T(8,128)(2,1)S(1)}, bf16[80,3584]{1,0:T(8,128)(2,1)S(1)}, u32[]{:S(2)}, u32[]{:S(2)}) collective-permute-start(bf16[80,3584]{1,0:T(8,128)(2,1)S(1)} %slice.75), channel_id=1, source_target_pairs={{0,2},{1,3},{2,0},{3,1},{4,6},{5,7},{6,4},{7,5},{8,10},{9,11},{10,... | collective-permute-start | bytes 1720328 | tf_op jit(solution)/shard_map/yback1/ppermute | solution.py:91
  73.7 4.7 %collective-permute-start.16 = (bf16[160,3584]{1,0:T(8,128)(2,1)S(1)}, bf16[160,3584]{1,0:T(8,128)(2,1)S(1)}, u32[]{:S(2)}, u32[]{:S(2)}) collective-permute-start(bf16[160,3584]{1,0:T(8,128)(2,1)S(1)} %get-tuple-element.96), channel_id=1, source_target_pairs={{0,1},{1,0},{2,3},{3,2},{4,5},{5,4},{6,7},{7,6},{8,9},{9,8},{10,11... | collective-permute-start | bytes 3440648 | tf_op jit(solution)/shard_map/cback2/ppermute | solution.py:91
  73.8 23.9 %collective-permute-start.14 = (bf16[80,3584]{1,0:T(8,128)(2,1)S(1)}, bf16[80,3584]{1,0:T(8,128)(2,1)S(1)}, u32[]{:S(2)}, u32[]{:S(2)}) collective-permute-start(bf16[80,3584]{1,0:T(8,128)(2,1)S(1)} %fusion.6), channel_id=1, source_target_pairs={{0,12},{1,13},{2,14},{3,15},{4,0},{5,1},{6,2},{7,3},{8,4},{9,5},{1... | collective-permute-start | bytes 1720328 | tf_op jit(solution)/shard_map/zback1/ppermute | solution.py:91
  77.8 19.9 %collective-permute-start.15 = (bf16[32,3584]{1,0:T(8,128)(2,1)S(1)}, bf16[32,3584]{1,0:T(8,128)(2,1)S(1)}, u32[]{:S(2)}, u32[]{:S(2)}) collective-permute-start(bf16[32,3584]{1,0:T(8,128)(2,1)S(1)} %collective-permute-done.9), channel_id=1, source_target_pairs={{0,2},{1,3},{2,0},{3,1},{4,6},{5,7},{6,4},{7,5},{8,10},{9,11},{10,... | collective-permute-start | bytes 688136 | tf_op jit(solution)/shard_map/yout4/ppermute | solution.py:91
  78.4 2.2 %collective-permute-start.18 = (bf16[96,3584]{1,0:T(8,128)(2,1)S(1)}, bf16[96,3584]{1,0:T(8,128)(2,1)S(1)}, u32[]{:S(2)}, u32[]{:S(2)}) collective-permute-start(bf16[96,3584]{1,0:T(8,128)(2,1)S(1)} %constant_dynamic-update-slice_fusion.6.a), channel_id=1, source_target_pairs={{0,1},{1,0},{2,3},{3,2},{4,5},{5,4},{6,7},{7,6},{8,9},{9,8},{10,11... | collective-permute-start | bytes 2064392 | tf_op jit(solution)/shard_map/cout3/ppermute | solution.py:91
  78.8 18.8 %collective-permute-start.17 = (bf16[80,3584]{1,0:T(8,128)(2,1)S(1)}, bf16[80,3584]{1,0:T(8,128)(2,1)S(1)}, u32[]{:S(2)}, u32[]{:S(2)}) collective-permute-start(bf16[80,3584]{1,0:T(8,128)(2,1)S(1)} %slice.74), channel_id=1, source_target_pairs={{0,2},{1,3},{2,0},{3,1},{4,6},{5,7},{6,4},{7,5},{8,10},{9,11},{10,... | collective-permute-start | bytes 1720328 | tf_op jit(solution)/shard_map/yback2/ppermute | solution.py:91
  83.3 15.1 %copy-start.5 = (s32[128,2]{0,1:T(2,128)S(1)}, s32[128,2]{0,1:T(2,128)}, u32[]{:S(2)}) copy-start(s32[128,2]{0,1:T(2,128)} %param.7) | copy-start | bytes 3076
  83.3 15.1 %copy-start.6 = (f32[128,2]{0,1:T(2,128)S(1)}, f32[128,2]{0,1:T(2,128)}, u32[]{:S(2)}) copy-start(f32[128,2]{0,1:T(2,128)} %param.8) | copy-start | bytes 3076
  97.8 1.9 %collective-permute-start.19 = (bf16[64,3584]{1,0:T(8,128)(2,1)S(1)}, bf16[64,3584]{1,0:T(8,128)(2,1)S(1)}, u32[]{:S(2)}, u32[]{:S(2)}) collective-permute-start(bf16[64,3584]{1,0:T(8,128)(2,1)S(1)} %constant_dynamic-update-slice_fusion.8.a), channel_id=1, source_target_pairs={{0,1},{1,0},{2,3},{3,2},{4,5},{5,4},{6,7},{7,6},{8,9},{9,8},{10,11... | collective-permute-start | bytes 1376264 | tf_op jit(solution)/shard_map/cout4/ppermute | solution.py:91
  97.9 4.0 %collective-permute-start.24 = (bf16[96,3584]{1,0:T(8,128)(2,1)S(1)}, bf16[96,3584]{1,0:T(8,128)(2,1)S(1)}, u32[]{:S(2)}, u32[]{:S(2)}) collective-permute-start(bf16[96,3584]{1,0:T(8,128)(2,1)S(1)} %get-tuple-element.113), channel_id=1, source_target_pairs={{0,1},{1,0},{2,3},{3,2},{4,5},{5,4},{6,7},{7,6},{8,9},{9,8},{10,11... | collective-permute-start | bytes 2064392 | tf_op jit(solution)/shard_map/cback3/ppermute | solution.py:91
  98.4 42.7 %collective-permute-start.23 = (bf16[80,3584]{1,0:T(8,128)(2,1)S(1)}, bf16[80,3584]{1,0:T(8,128)(2,1)S(1)}, u32[]{:S(2)}, u32[]{:S(2)}) collective-permute-start(bf16[80,3584]{1,0:T(8,128)(2,1)S(1)} %fusion.5), channel_id=1, source_target_pairs={{0,4},{1,5},{2,6},{3,7},{4,8},{5,9},{6,10},{7,11},{8,12},{9,13},{1... | collective-permute-start | bytes 1720328 | tf_op jit(solution)/shard_map/zback2/ppermute | solution.py:91
  101.6 1.9 %collective-permute-start.20 = (bf16[64,3584]{1,0:T(8,128)(2,1)S(1)}, bf16[64,3584]{1,0:T(8,128)(2,1)S(1)}, u32[]{:S(2)}, u32[]{:S(2)}) collective-permute-start(bf16[64,3584]{1,0:T(8,128)(2,1)S(1)} %get-tuple-element.108), channel_id=1, source_target_pairs={{0,1},{1,0},{2,3},{3,2},{4,5},{5,4},{6,7},{7,6},{8,9},{9,8},{10,11... | collective-permute-start | bytes 1376264 | tf_op jit(solution)/shard_map/cback4/ppermute | solution.py:91
  102.0 11.0 %collective-permute-start.25 = (bf16[48,3584]{1,0:T(8,128)(2,1)S(1)}, bf16[48,3584]{1,0:T(8,128)(2,1)S(1)}, u32[]{:S(2)}, u32[]{:S(2)}) collective-permute-start(bf16[48,3584]{1,0:T(8,128)(2,1)S(1)} %slice.76), channel_id=1, source_target_pairs={{0,2},{1,3},{2,0},{3,1},{4,6},{5,7},{6,4},{7,5},{8,10},{9,11},{10,... | collective-permute-start | bytes 1032200 | tf_op jit(solution)/shard_map/yback3/ppermute | solution.py:91
  103.6 13.7 %collective-permute-start.21 = (bf16[32,3584]{1,0:T(8,128)(2,1)S(1)}, bf16[32,3584]{1,0:T(8,128)(2,1)S(1)}, u32[]{:S(2)}, u32[]{:S(2)}) collective-permute-start(bf16[32,3584]{1,0:T(8,128)(2,1)S(1)} %slice.77), channel_id=1, source_target_pairs={{0,2},{1,3},{2,0},{3,1},{4,6},{5,7},{6,4},{7,5},{8,10},{9,11},{10,... | collective-permute-start | bytes 688136 | tf_op jit(solution)/shard_map/yback4/ppermute | solution.py:91
  113.0 23.0 %collective-permute-start.26 = (bf16[48,3584]{1,0:T(8,128)(2,1)S(1)}, bf16[48,3584]{1,0:T(8,128)(2,1)S(1)}, u32[]{:S(2)}, u32[]{:S(2)}) collective-permute-start(bf16[48,3584]{1,0:T(8,128)(2,1)S(1)} %fusion.7), channel_id=1, source_target_pairs={{0,8},{1,9},{2,10},{3,11},{4,12},{5,13},{6,14},{7,15},{8,0},{9,1},... | collective-permute-start | bytes 1032200 | tf_op jit(solution)/shard_map/zback3/ppermute | solution.py:91
  117.5 23.2 %collective-permute-start.22 = (bf16[80,3584]{1,0:T(8,128)(2,1)S(1)}, bf16[80,3584]{1,0:T(8,128)(2,1)S(1)}, u32[]{:S(2)}, u32[]{:S(2)}) collective-permute-start(bf16[80,3584]{1,0:T(8,128)(2,1)S(1)} %slice.73), channel_id=1, source_target_pairs={{0,2},{1,3},{2,0},{3,1},{4,6},{5,7},{6,4},{7,5},{8,10},{9,11},{10,... | collective-permute-start | bytes 1720328 | tf_op jit(solution)/shard_map/yback0/ppermute | solution.py:91
  118.5 21.7 %collective-permute-start.27 = (bf16[32,3584]{1,0:T(8,128)(2,1)S(1)}, bf16[32,3584]{1,0:T(8,128)(2,1)S(1)}, u32[]{:S(2)}, u32[]{:S(2)}) collective-permute-start(bf16[32,3584]{1,0:T(8,128)(2,1)S(1)} %fusion.8), channel_id=1, source_target_pairs={{0,8},{1,9},{2,10},{3,11},{4,12},{5,13},{6,14},{7,15},{8,0},{9,1},... | collective-permute-start | bytes 688136 | tf_op jit(solution)/shard_map/zback4/ppermute | solution.py:91
  141.1 1.5 %copy-start.1 = (bf16[128,3584]{1,0:T(8,128)(2,1)S(1)}, bf16[128,3584]{1,0:T(8,128)(2,1)}, u32[]{:S(2)}) copy-start(bf16[128,3584]{1,0:T(8,128)(2,1)} %param.6) | copy-start | bytes 2752516

commit v5 on v4

--- a/solution.py
+++ b/solution.py
@@ -235,8 +235,9 @@
                 send_back(i)
     backs = [live["back", i] for i in range(count)]
     total = 0.0
-    for i, chunk in enumerate(chunks):
-        total = total + combine(chunk, backs[i])
+    late = max(1, count - 2)
+    for i in [*range(1, late), 0, *range(late, count)]:
+        total = total + combine(chunks[i], backs[i])
     return total.astype(BF)
 
 

time: 143 us -> 150 us (1.049)
  waiting for transfers between devices: 86.3 us -> 96.3 us
  starting transfers between devices: 26.5 us -> 23.8 us
    ppermute x28, waiting for transfers between devices: 86.3 us -> 96.3 us  [move(): return lax.ppermute(x, 'expert', [(d, to(d)) for d in range(devices)])]
    ppermute x28, starting transfers between devices: 26.5 us -> 23.8 us  [move(): return lax.ppermute(x, 'expert', [(d, to(d)) for d in range(devices)])]
  transfers between devices with their start and end apart: 28 -> 28, of which waited for: 15 -> 16; matrix products, arithmetic and copies ran while one was open for 3% -> 3% of each run, Pallas kernels for 12% -> 12%
where the time goes in v5:
time: 150 us
  waiting for transfers between devices  96.3 us (64%)
  starting transfers between devices  23.8 us (16%)
  Pallas kernels  17.6 us (12%)
  local copies, waits for them, and re-layouts  4.82 us (3%)
  matrix products  4.8 us (3%)
  other arithmetic  2.01 us (1%)
    ppermute x28, waiting for transfers between devices, move(): return lax.ppermute(x, 'expert', [(d, to(d)) for d in range(devices)])  96.3 us
    ppermute x28, starting transfers between devices, move(): return lax.ppermute(x, 'expert', [(d, to(d)) for d in range(devices)])  23.8 us
    pallas_call x5, Pallas kernels, ffn(): pl.pallas_call(ffn_kernel, out_shape=(jax.ShapeDtypeStruct((n, features),...  16.8 us
    unnamed x19, local copies, waits for them, and re-layouts  4.4 us
    dot_general x5, matrix products, combine(): return weight[:, None] * jnp.dot(pick, back, preferred_element_type=F32)  3.14 us
  transfers between devices with their start and end apart: 28, of which 16 were waited for; matrix products, arithmetic and copies ran while one was open for 3% of the time, Pallas kernels for 12%

profile of v5, /device:TPU:0, one launch (start us, length us, event | category | flops | bytes accessed | tf_op | source)
XLA Modules:
  0.0 149.8 jit_solution(12573861366493816958)
XLA Ops:
  0.0 0.8 fusion.93
  1.2 0.3 convolution_convert_fusion.1
  1.5 3.1 %collective-permute-start = (bf16[80,3584]{1,0:T(8,128)(2,1)S(1)}, bf16[80,3584]{1,0:T(8,128)(2,1)S(1)}, u32[]{:S(2)}, u32[]{:S(2)}) collective-permute-start(bf16[80,3584]{1,0:T(8,128)(2,1)S(1)} %convolution_convert_fusion.1), channel_id=1, source_target_pairs={{0,4},{1,5},{2,6},{3,7},{4,8},{5,9},{6,10},{7,11},{8,12},{9,13},{1... | collective-permute-start | bytes 1720328 | tf_op jit(solution)/shard_map/zout1/ppermute | solution.py:91
  4.9 1.6 %collective-permute-start.1 = (bf16[80,3584]{1,0:T(8,128)(2,1)S(1)}, bf16[80,3584]{1,0:T(8,128)(2,1)S(1)}, u32[]{:S(2)}, u32[]{:S(2)}) collective-permute-start(bf16[80,3584]{1,0:T(8,128)(2,1)S(1)} %convolution_convert_fusion.2), channel_id=1, source_target_pairs={{0,2},{1,3},{2,0},{3,1},{4,6},{5,7},{6,4},{7,5},{8,10},{9,11},{10,... | collective-permute-start | bytes 1720328 | tf_op jit(solution)/shard_map/yout0/ppermute | solution.py:91
  6.5 0.3 convolution_convert_fusion.4
  6.8 2.0 %copy-done.3 = bf16[1,3584,512]{2,1,0:T(8,128)(2,1)S(1)} copy-done((bf16[1,3584,512]{2,1,0:T(8,128)(2,1)S(1)}, bf16[1,3584,512]{2,1,0:T(8,128)(2,1)}, u32[]{:S(2)}) %copy-start.3) | copy-done | bytes 3670040
  8.8 2.0 %copy-done.4 = bf16[1,512,3584]{2,1,0:T(8,128)(2,1)S(1)} copy-done((bf16[1,512,3584]{2,1,0:T(8,128)(2,1)S(1)}, bf16[1,512,3584]{2,1,0:T(8,128)(2,1)}, u32[]{:S(2)}) %copy-start.4) | copy-done | bytes 3670040
  10.9 0.8 shard_map.64
  11.9 0.3 convolution_convert_fusion
  12.2 7.3 %collective-permute-done = bf16[80,3584]{1,0:T(8,128)(2,1)S(1)} collective-permute-done((bf16[80,3584]{1,0:T(8,128)(2,1)S(1)}, bf16[80,3584]{1,0:T(8,128)(2,1)S(1)}, u32[]{:S(2)}, u32[]{:S(2)}) %collective-permute-start) | collective-permute-done | bytes 573472 | tf_op jit(solution)/shard_map/zout1/ppermute | solution.py:91
  19.8 1.6 %collective-permute-start.7 = (bf16[80,3584]{1,0:T(8,128)(2,1)S(1)}, bf16[80,3584]{1,0:T(8,128)(2,1)S(1)}, u32[]{:S(2)}, u32[]{:S(2)}) collective-permute-start(bf16[80,3584]{1,0:T(8,128)(2,1)S(1)} %collective-permute-done), channel_id=1, source_target_pairs={{0,2},{1,3},{2,0},{3,1},{4,6},{5,7},{6,4},{7,5},{8,10},{9,11},{10,... | collective-permute-start | bytes 1720328 | tf_op jit(solution)/shard_map/yout1/ppermute | solution.py:91
  21.3 2.1 %collective-permute-start.2 = (bf16[80,3584]{1,0:T(8,128)(2,1)S(1)}, bf16[80,3584]{1,0:T(8,128)(2,1)S(1)}, u32[]{:S(2)}, u32[]{:S(2)}) collective-permute-start(bf16[80,3584]{1,0:T(8,128)(2,1)S(1)} %convolution_convert_fusion), channel_id=1, source_target_pairs={{0,12},{1,13},{2,14},{3,15},{4,0},{5,1},{6,2},{7,3},{8,4},{9,5},{1... | collective-permute-start | bytes 1720328 | tf_op jit(solution)/shard_map/zout2/ppermute | solution.py:91
  23.5 0.8 collective-permute-start.3
  24.3 10.9 %collective-permute-done.7 = bf16[80,3584]{1,0:T(8,128)(2,1)S(1)} collective-permute-done((bf16[80,3584]{1,0:T(8,128)(2,1)S(1)}, bf16[80,3584]{1,0:T(8,128)(2,1)S(1)}, u32[]{:S(2)}, u32[]{:S(2)}) %collective-permute-start.7) | collective-permute-done | bytes 573472 | tf_op jit(solution)/shard_map/yout1/ppermute | solution.py:91
  35.3 1.6 %collective-permute-done.2 = bf16[80,3584]{1,0:T(8,128)(2,1)S(1)} collective-permute-done((bf16[80,3584]{1,0:T(8,128)(2,1)S(1)}, bf16[80,3584]{1,0:T(8,128)(2,1)S(1)}, u32[]{:S(2)}, u32[]{:S(2)}) %collective-permute-start.2) | collective-permute-done | bytes 573472 | tf_op jit(solution)/shard_map/zout2/ppermute | solution.py:91
  36.8 0.5 collective-permute-start.5
  37.3 4.1 %ffn0.1 = (f32[160,3584]{1,0:T(8,128)S(1)}, bf16[160,3584]{1,0:T(8,128)(2,1)S(1)}) custom-call(bf16[160,3584]{1,0:T(8,128)(2,1)S(1)} %constant_dynamic-update-slice_fusion.a, bf16[160,3584]{1,0:T(8,128)(2,1)S(1)} %collective-permute-done.4.b, bf16[3584,512]{1,0:T(8,128)(2,1)S(1)} %get-tuple-element.106.vg, bf16[3584,512]{1,0:T(8,128)(2,1)S(1)} %get-tuple-element.107.vu, ...), custom_call_target="tpu_custom_call" | custom-call | flops 14092861440 | bytes 11010048 | tf_op jit(solution)/shard_map/ffn0/pallas_call | solution.py:59
  41.5 4.1 %ffn1.1 = (f32[160,3584]{1,0:T(8,128)S(1)}, bf16[160,3584]{1,0:T(8,128)(2,1)S(1)}) custom-call(bf16[160,3584]{1,0:T(8,128)(2,1)S(1)} %constant_dynamic-update-slice_fusion.2.a, bf16[160,3584]{1,0:T(8,128)(2,1)S(1)} %collective-permute-done.8.b, bf16[3584,512]{1,0:T(8,128)(2,1)S(1)} %get-tuple-element.106.vg, bf16[3584,512]{1,0:T(8,128)(2,1)S(1)} %get-tuple-element.107.vu, ...), custom_call_target="tpu_custom_call" | custom-call | flops 14092861440 | bytes 11010048 | tf_op jit(solution)/shard_map/ffn1/pallas_call | solution.py:59
  45.6 6.3 %collective-permute-done.3 = bf16[48,3584]{1,0:T(8,128)(2,1)S(1)} collective-permute-done((bf16[48,3584]{1,0:T(8,128)(2,1)S(1)}, bf16[48,3584]{1,0:T(8,128)(2,1)S(1)}, u32[]{:S(2)}, u32[]{:S(2)}) %collective-permute-start.3) | collective-permute-done | bytes 344096 | tf_op jit(solution)/shard_map/zout3/ppermute | solution.py:91
  52.0 1.1 collective-permute-start.9
  53.0 1.5 %collective-permute-start.10 = (bf16[48,3584]{1,0:T(8,128)(2,1)S(1)}, bf16[48,3584]{1,0:T(8,128)(2,1)S(1)}, u32[]{:S(2)}, u32[]{:S(2)}) collective-permute-start(bf16[48,3584]{1,0:T(8,128)(2,1)S(1)} %collective-permute-done.3), channel_id=1, source_target_pairs={{0,2},{1,3},{2,0},{3,1},{4,6},{5,7},{6,4},{7,5},{8,10},{9,11},{10,... | collective-permute-start | bytes 1032200 | tf_op jit(solution)/shard_map/yout3/ppermute | solution.py:91
  54.7 0.6 collective-permute-start.13
  55.5 1.9 %collective-permute-done.11 = bf16[160,3584]{1,0:T(8,128)(2,1)S(1)} collective-permute-done((bf16[160,3584]{1,0:T(8,128)(2,1)S(1)}, bf16[160,3584]{1,0:T(8,128)(2,1)S(1)}, u32[]{:S(2)}, u32[]{:S(2)}) %collective-permute-start.11) | collective-permute-done | bytes 1146912 | tf_op jit(solution)/shard_map/cback1/ppermute | solution.py:91
  57.7 0.6 collective-permute-start.12
  58.2 0.8 collective-permute-done.13.b
  59.0 4.1 %ffn2.1 = (f32[160,3584]{1,0:T(8,128)S(1)}, bf16[160,3584]{1,0:T(8,128)(2,1)S(1)}) custom-call(bf16[160,3584]{1,0:T(8,128)(2,1)S(1)} %constant_dynamic-update-slice_fusion.4.a, bf16[160,3584]{1,0:T(8,128)(2,1)S(1)} %collective-permute-done.13.b, bf16[3584,512]{1,0:T(8,128)(2,1)S(1)} %get-tuple-element.106.vg, bf16[3584,512]{1,0:T(8,128)(2,1)S(1)} %get-tuple-element.107.vu, ...), custom_call_target="tpu_custom_call" | custom-call | flops 14092861440 | bytes 11010048 | tf_op jit(solution)/shard_map/ffn2/pallas_call | solution.py:59
  63.1 10.5 %collective-permute-done.12 = bf16[80,3584]{1,0:T(8,128)(2,1)S(1)} collective-permute-done((bf16[80,3584]{1,0:T(8,128)(2,1)S(1)}, bf16[80,3584]{1,0:T(8,128)(2,1)S(1)}, u32[]{:S(2)}, u32[]{:S(2)}) %collective-permute-start.12) | collective-permute-done | bytes 573472 | tf_op jit(solution)/shard_map/yback1/ppermute | solution.py:91
  73.8 4.0 %collective-permute-start.14 = (bf16[80,3584]{1,0:T(8,128)(2,1)S(1)}, bf16[80,3584]{1,0:T(8,128)(2,1)S(1)}, u32[]{:S(2)}, u32[]{:S(2)}) collective-permute-start(bf16[80,3584]{1,0:T(8,128)(2,1)S(1)} %fusion.6), channel_id=1, source_target_pairs={{0,12},{1,13},{2,14},{3,15},{4,0},{5,1},{6,2},{7,3},{8,4},{9,5},{1... | collective-permute-start | bytes 1720328 | tf_op jit(solution)/shard_map/zback1/ppermute | solution.py:91
  77.8 0.5 collective-permute-start.15
  78.8 1.6 %collective-permute-start.17 = (bf16[80,3584]{1,0:T(8,128)(2,1)S(1)}, bf16[80,3584]{1,0:T(8,128)(2,1)S(1)}, u32[]{:S(2)}, u32[]{:S(2)}) collective-permute-start(bf16[80,3584]{1,0:T(8,128)(2,1)S(1)} %slice.74), channel_id=1, source_target_pairs={{0,2},{1,3},{2,0},{3,1},{4,6},{5,7},{6,4},{7,5},{8,10},{9,11},{10,... | collective-permute-start | bytes 1720328 | tf_op jit(solution)/shard_map/yback2/ppermute | solution.py:91
  80.6 2.7 %ffn3.1 = (f32[96,3584]{1,0:T(8,128)S(1)}, bf16[96,3584]{1,0:T(8,128)(2,1)S(1)}) custom-call(bf16[96,3584]{1,0:T(8,128)(2,1)S(1)} %constant_dynamic-update-slice_fusion.6.a, bf16[96,3584]{1,0:T(8,128)(2,1)S(1)} %collective-permute-done.18.b, bf16[3584,512]{1,0:T(8,128)(2,1)S(1)} %get-tuple-element.106.vg, bf16[3584,512]{1,0:T(8,128)(2,1)S(1)} %get-tuple-element.107.vu, ...), custom_call_target="tpu_custom_call" | custom-call | flops 8455716864 | bytes 11010048 | tf_op jit(solution)/shard_map/ffn3/pallas_call | solution.py:59
  83.3 14.3 %collective-permute-done.17 = bf16[80,3584]{1,0:T(8,128)(2,1)S(1)} collective-permute-done((bf16[80,3584]{1,0:T(8,128)(2,1)S(1)}, bf16[80,3584]{1,0:T(8,128)(2,1)S(1)}, u32[]{:S(2)}, u32[]{:S(2)}) %collective-permute-start.17) | collective-permute-done | bytes 573472 | tf_op jit(solution)/shard_map/yback2/ppermute | solution.py:91
  97.9 0.5 collective-permute-start.19
  98.7 1.0 collective-permute-done.20.b
  99.7 2.0 %ffn4.1 = (f32[64,3584]{1,0:T(8,128)S(1)}, bf16[64,3584]{1,0:T(8,128)(2,1)S(1)}) custom-call(bf16[64,3584]{1,0:T(8,128)(2,1)S(1)} %constant_dynamic-update-slice_fusion.8.a, bf16[64,3584]{1,0:T(8,128)(2,1)S(1)} %collective-permute-done.20.b, bf16[3584,512]{1,0:T(8,128)(2,1)S(1)} %get-tuple-element.106.vg, bf16[3584,512]{1,0:T(8,128)(2,1)S(1)} %get-tuple-element.107.vu, ...), custom_call_target="tpu_custom_call" | custom-call | flops 5637144576 | bytes 11010048 | tf_op jit(solution)/shard_map/ffn4/pallas_call | solution.py:59
  101.8 13.2 %collective-permute-done.19 = bf16[80,3584]{1,0:T(8,128)(2,1)S(1)} collective-permute-done((bf16[80,3584]{1,0:T(8,128)(2,1)S(1)}, bf16[80,3584]{1,0:T(8,128)(2,1)S(1)}, u32[]{:S(2)}, u32[]{:S(2)}) %collective-permute-start.19) | collective-permute-done | bytes 573472 | tf_op jit(solution)/shard_map/zback2/ppermute | solution.py:91
  115.1 0.4 convolution_multiply_fusion.3
  115.5 0.4 fusion.3
  116.1 0.6 collective-permute-start.22
  116.8 1.6 %collective-permute-start.25 = (bf16[48,3584]{1,0:T(8,128)(2,1)S(1)}, bf16[48,3584]{1,0:T(8,128)(2,1)S(1)}, u32[]{:S(2)}, u32[]{:S(2)}) collective-permute-start(bf16[48,3584]{1,0:T(8,128)(2,1)S(1)} %slice.76), channel_id=1, source_target_pairs={{0,2},{1,3},{2,0},{3,1},{4,6},{5,7},{6,4},{7,5},{8,10},{9,11},{10,... | collective-permute-start | bytes 1032200 | tf_op jit(solution)/shard_map/yback3/ppermute | solution.py:91
  118.4 6.3 %collective-permute-done.22 = bf16[32,3584]{1,0:T(8,128)(2,1)S(1)} collective-permute-done((bf16[32,3584]{1,0:T(8,128)(2,1)S(1)}, bf16[32,3584]{1,0:T(8,128)(2,1)S(1)}, u32[]{:S(2)}, u32[]{:S(2)}) %collective-permute-start.22) | collective-permute-done | bytes 229408 | tf_op jit(solution)/shard_map/yback4/ppermute | solution.py:91
  124.9 0.5 collective-permute-start.23
  125.4 6.6 %collective-permute-done.25 = bf16[48,3584]{1,0:T(8,128)(2,1)S(1)} collective-permute-done((bf16[48,3584]{1,0:T(8,128)(2,1)S(1)}, bf16[48,3584]{1,0:T(8,128)(2,1)S(1)}, u32[]{:S(2)}, u32[]{:S(2)}) %collective-permute-start.25) | collective-permute-done | bytes 344096 | tf_op jit(solution)/shard_map/yback3/ppermute | solution.py:91
  132.2 10.1 %collective-permute-done.27 = bf16[32,3584]{1,0:T(8,128)(2,1)S(1)} collective-permute-done((bf16[32,3584]{1,0:T(8,128)(2,1)S(1)}, bf16[32,3584]{1,0:T(8,128)(2,1)S(1)}, u32[]{:S(2)}, u32[]{:S(2)}) %collective-permute-start.27) | collective-permute-done | bytes 229408 | tf_op jit(solution)/shard_map/zback4/ppermute | solution.py:91
  142.3 0.4 convolution_multiply_fusion
  143.0 0.5 fusion.2
  143.5 4.9 %collective-permute-done.26 = bf16[48,3584]{1,0:T(8,128)(2,1)S(1)} collective-permute-done((bf16[48,3584]{1,0:T(8,128)(2,1)S(1)}, bf16[48,3584]{1,0:T(8,128)(2,1)S(1)}, u32[]{:S(2)}, u32[]{:S(2)}) %collective-permute-start.26) | collective-permute-done | bytes 344096 | tf_op jit(solution)/shard_map/zback3/ppermute | solution.py:91
  148.4 1.4 fusion.4
  (70 shorter events, 4.2 us)
Async XLA Ops:
  0.0 1.2 copy-start
  1.2 5.6 %copy-start.2 = (bf16[1,3584,512]{2,1,0:T(8,128)(2,1)S(1)}, bf16[1,3584,512]{2,1,0:T(8,128)(2,1)}, u32[]{:S(2)}) copy-start(bf16[1,3584,512]{2,1,0:T(8,128)(2,1)} %param.9) | copy-start | bytes 11010052
  1.5 18.1 %collective-permute-start = (bf16[80,3584]{1,0:T(8,128)(2,1)S(1)}, bf16[80,3584]{1,0:T(8,128)(2,1)S(1)}, u32[]{:S(2)}, u32[]{:S(2)}) collective-permute-start(bf16[80,3584]{1,0:T(8,128)(2,1)S(1)} %convolution_convert_fusion.1), channel_id=1, source_target_pairs={{0,4},{1,5},{2,6},{3,7},{4,8},{5,9},{6,10},{7,11},{8,12},{9,13},{1... | collective-permute-start | bytes 1720328 | tf_op jit(solution)/shard_map/zout1/ppermute | solution.py:91
  4.9 14.7 %collective-permute-start.1 = (bf16[80,3584]{1,0:T(8,128)(2,1)S(1)}, bf16[80,3584]{1,0:T(8,128)(2,1)S(1)}, u32[]{:S(2)}, u32[]{:S(2)}) collective-permute-start(bf16[80,3584]{1,0:T(8,128)(2,1)S(1)} %convolution_convert_fusion.2), channel_id=1, source_target_pairs={{0,2},{1,3},{2,0},{3,1},{4,6},{5,7},{6,4},{7,5},{8,10},{9,11},{10,... | collective-permute-start | bytes 1720328 | tf_op jit(solution)/shard_map/yout0/ppermute | solution.py:91
  6.8 2.0 %copy-start.3 = (bf16[1,3584,512]{2,1,0:T(8,128)(2,1)S(1)}, bf16[1,3584,512]{2,1,0:T(8,128)(2,1)}, u32[]{:S(2)}) copy-start(bf16[1,3584,512]{2,1,0:T(8,128)(2,1)} %param.10) | copy-start | bytes 11010052
  8.8 2.0 %copy-start.4 = (bf16[1,512,3584]{2,1,0:T(8,128)(2,1)S(1)}, bf16[1,512,3584]{2,1,0:T(8,128)(2,1)}, u32[]{:S(2)}) copy-start(bf16[1,512,3584]{2,1,0:T(8,128)(2,1)} %param.11) | copy-start | bytes 11010052
  19.7 17.7 %collective-permute-start.4 = (bf16[160,3584]{1,0:T(8,128)(2,1)S(1)}, bf16[160,3584]{1,0:T(8,128)(2,1)S(1)}, u32[]{:S(2)}, u32[]{:S(2)}) collective-permute-start(bf16[160,3584]{1,0:T(8,128)(2,1)S(1)} %constant_dynamic-update-slice_fusion.a), channel_id=1, source_target_pairs={{0,1},{1,0},{2,3},{3,2},{4,5},{5,4},{6,7},{7,6},{8,9},{9,8},{10,11... | collective-permute-start | bytes 3440648 | tf_op jit(solution)/shard_map/cout0/ppermute | solution.py:91
  19.8 15.4 %collective-permute-start.7 = (bf16[80,3584]{1,0:T(8,128)(2,1)S(1)}, bf16[80,3584]{1,0:T(8,128)(2,1)S(1)}, u32[]{:S(2)}, u32[]{:S(2)}) collective-permute-start(bf16[80,3584]{1,0:T(8,128)(2,1)S(1)} %collective-permute-done), channel_id=1, source_target_pairs={{0,2},{1,3},{2,0},{3,1},{4,6},{5,7},{6,4},{7,5},{8,10},{9,11},{10,... | collective-permute-start | bytes 1720328 | tf_op jit(solution)/shard_map/yout1/ppermute | solution.py:91
  21.3 15.5 %collective-permute-start.2 = (bf16[80,3584]{1,0:T(8,128)(2,1)S(1)}, bf16[80,3584]{1,0:T(8,128)(2,1)S(1)}, u32[]{:S(2)}, u32[]{:S(2)}) collective-permute-start(bf16[80,3584]{1,0:T(8,128)(2,1)S(1)} %convolution_convert_fusion), channel_id=1, source_target_pairs={{0,12},{1,13},{2,14},{3,15},{4,0},{5,1},{6,2},{7,3},{8,4},{9,5},{1... | collective-permute-start | bytes 1720328 | tf_op jit(solution)/shard_map/zout2/ppermute | solution.py:91
  23.5 28.4 %collective-permute-start.3 = (bf16[48,3584]{1,0:T(8,128)(2,1)S(1)}, bf16[48,3584]{1,0:T(8,128)(2,1)S(1)}, u32[]{:S(2)}, u32[]{:S(2)}) collective-permute-start(bf16[48,3584]{1,0:T(8,128)(2,1)S(1)} %convolution_convert_fusion.3), channel_id=1, source_target_pairs={{0,8},{1,9},{2,10},{3,11},{4,12},{5,13},{6,14},{7,15},{8,0},{9,1},... | collective-permute-start | bytes 1032200 | tf_op jit(solution)/shard_map/zout3/ppermute | solution.py:91
  35.2 6.3 %collective-permute-start.8 = (bf16[160,3584]{1,0:T(8,128)(2,1)S(1)}, bf16[160,3584]{1,0:T(8,128)(2,1)S(1)}, u32[]{:S(2)}, u32[]{:S(2)}) collective-permute-start(bf16[160,3584]{1,0:T(8,128)(2,1)S(1)} %constant_dynamic-update-slice_fusion.2.a), channel_id=1, source_target_pairs={{0,1},{1,0},{2,3},{3,2},{4,5},{5,4},{6,7},{7,6},{8,9},{9,8},{10,11... | collective-permute-start | bytes 3440648 | tf_op jit(solution)/shard_map/cout1/ppermute | solution.py:91
  36.8 15.1 %collective-permute-start.5 = (bf16[80,3584]{1,0:T(8,128)(2,1)S(1)}, bf16[80,3584]{1,0:T(8,128)(2,1)S(1)}, u32[]{:S(2)}, u32[]{:S(2)}) collective-permute-start(bf16[80,3584]{1,0:T(8,128)(2,1)S(1)} %collective-permute-done.2), channel_id=1, source_target_pairs={{0,2},{1,3},{2,0},{3,1},{4,6},{5,7},{6,4},{7,5},{8,10},{9,11},{10,... | collective-permute-start | bytes 1720328 | tf_op jit(solution)/shard_map/yout2/ppermute | solution.py:91
  41.4 10.5 %collective-permute-start.6 = (bf16[160,3584]{1,0:T(8,128)(2,1)S(1)}, bf16[160,3584]{1,0:T(8,128)(2,1)S(1)}, u32[]{:S(2)}, u32[]{:S(2)}) collective-permute-start(bf16[160,3584]{1,0:T(8,128)(2,1)S(1)} %get-tuple-element.72), channel_id=1, source_target_pairs={{0,1},{1,0},{2,3},{3,2},{4,5},{5,4},{6,7},{7,6},{8,9},{9,8},{10,11... | collective-permute-start | bytes 3440648 | tf_op jit(solution)/shard_map/cback0/ppermute | solution.py:91
  52.0 21.8 %collective-permute-start.9 = (bf16[32,3584]{1,0:T(8,128)(2,1)S(1)}, bf16[32,3584]{1,0:T(8,128)(2,1)S(1)}, u32[]{:S(2)}, u32[]{:S(2)}) collective-permute-start(bf16[32,3584]{1,0:T(8,128)(2,1)S(1)} %convolution_convert_fusion.4), channel_id=1, source_target_pairs={{0,8},{1,9},{2,10},{3,11},{4,12},{5,13},{6,14},{7,15},{8,0},{9,1},... | collective-permute-start | bytes 688136 | tf_op jit(solution)/shard_map/zout4/ppermute | solution.py:91
  53.0 20.7 %collective-permute-start.10 = (bf16[48,3584]{1,0:T(8,128)(2,1)S(1)}, bf16[48,3584]{1,0:T(8,128)(2,1)S(1)}, u32[]{:S(2)}, u32[]{:S(2)}) collective-permute-start(bf16[48,3584]{1,0:T(8,128)(2,1)S(1)} %collective-permute-done.3), channel_id=1, source_target_pairs={{0,2},{1,3},{2,0},{3,1},{4,6},{5,7},{6,4},{7,5},{8,10},{9,11},{10,... | collective-permute-start | bytes 1032200 | tf_op jit(solution)/shard_map/yout3/ppermute | solution.py:91
  54.6 2.8 %collective-permute-start.11 = (bf16[160,3584]{1,0:T(8,128)(2,1)S(1)}, bf16[160,3584]{1,0:T(8,128)(2,1)S(1)}, u32[]{:S(2)}, u32[]{:S(2)}) collective-permute-start(bf16[160,3584]{1,0:T(8,128)(2,1)S(1)} %get-tuple-element.84), channel_id=1, source_target_pairs={{0,1},{1,0},{2,3},{3,2},{4,5},{5,4},{6,7},{7,6},{8,9},{9,8},{10,11... | collective-permute-start | bytes 3440648 | tf_op jit(solution)/shard_map/cback1/ppermute | solution.py:91
  54.7 4.3 %collective-permute-start.13 = (bf16[160,3584]{1,0:T(8,128)(2,1)S(1)}, bf16[160,3584]{1,0:T(8,128)(2,1)S(1)}, u32[]{:S(2)}, u32[]{:S(2)}) collective-permute-start(bf16[160,3584]{1,0:T(8,128)(2,1)S(1)} %constant_dynamic-update-slice_fusion.4.a), channel_id=1, source_target_pairs={{0,1},{1,0},{2,3},{3,2},{4,5},{5,4},{6,7},{7,6},{8,9},{9,8},{10,11... | collective-permute-start | bytes 3440648 | tf_op jit(solution)/shard_map/cout2/ppermute | solution.py:91
  57.7 16.0 %collective-permute-start.12 = (bf16[80,3584]{1,0:T(8,128)(2,1)S(1)}, bf16[80,3584]{1,0:T(8,128)(2,1)S(1)}, u32[]{:S(2)}, u32[]{:S(2)}) collective-permute-start(bf16[80,3584]{1,0:T(8,128)(2,1)S(1)} %slice.75), channel_id=1, source_target_pairs={{0,2},{1,3},{2,0},{3,1},{4,6},{5,7},{6,4},{7,5},{8,10},{9,11},{10,... | collective-permute-start | bytes 1720328 | tf_op jit(solution)/shard_map/yback1/ppermute | solution.py:91
  73.7 4.7 %collective-permute-start.16 = (bf16[160,3584]{1,0:T(8,128)(2,1)S(1)}, bf16[160,3584]{1,0:T(8,128)(2,1)S(1)}, u32[]{:S(2)}, u32[]{:S(2)}) collective-permute-start(bf16[160,3584]{1,0:T(8,128)(2,1)S(1)} %get-tuple-element.96), channel_id=1, source_target_pairs={{0,1},{1,0},{2,3},{3,2},{4,5},{5,4},{6,7},{7,6},{8,9},{9,8},{10,11... | collective-permute-start | bytes 3440648 | tf_op jit(solution)/shard_map/cback2/ppermute | solution.py:91
  73.8 23.9 %collective-permute-start.14 = (bf16[80,3584]{1,0:T(8,128)(2,1)S(1)}, bf16[80,3584]{1,0:T(8,128)(2,1)S(1)}, u32[]{:S(2)}, u32[]{:S(2)}) collective-permute-start(bf16[80,3584]{1,0:T(8,128)(2,1)S(1)} %fusion.6), channel_id=1, source_target_pairs={{0,12},{1,13},{2,14},{3,15},{4,0},{5,1},{6,2},{7,3},{8,4},{9,5},{1... | collective-permute-start | bytes 1720328 | tf_op jit(solution)/shard_map/zback1/ppermute | solution.py:91
  77.8 19.9 %collective-permute-start.15 = (bf16[32,3584]{1,0:T(8,128)(2,1)S(1)}, bf16[32,3584]{1,0:T(8,128)(2,1)S(1)}, u32[]{:S(2)}, u32[]{:S(2)}) collective-permute-start(bf16[32,3584]{1,0:T(8,128)(2,1)S(1)} %collective-permute-done.9), channel_id=1, source_target_pairs={{0,2},{1,3},{2,0},{3,1},{4,6},{5,7},{6,4},{7,5},{8,10},{9,11},{10,... | collective-permute-start | bytes 688136 | tf_op jit(solution)/shard_map/yout4/ppermute | solution.py:91
  78.4 2.2 %collective-permute-start.18 = (bf16[96,3584]{1,0:T(8,128)(2,1)S(1)}, bf16[96,3584]{1,0:T(8,128)(2,1)S(1)}, u32[]{:S(2)}, u32[]{:S(2)}) collective-permute-start(bf16[96,3584]{1,0:T(8,128)(2,1)S(1)} %constant_dynamic-update-slice_fusion.6.a), channel_id=1, source_target_pairs={{0,1},{1,0},{2,3},{3,2},{4,5},{5,4},{6,7},{7,6},{8,9},{9,8},{10,11... | collective-permute-start | bytes 2064392 | tf_op jit(solution)/shard_map/cout3/ppermute | solution.py:91
  78.8 18.8 %collective-permute-start.17 = (bf16[80,3584]{1,0:T(8,128)(2,1)S(1)}, bf16[80,3584]{1,0:T(8,128)(2,1)S(1)}, u32[]{:S(2)}, u32[]{:S(2)}) collective-permute-start(bf16[80,3584]{1,0:T(8,128)(2,1)S(1)} %slice.74), channel_id=1, source_target_pairs={{0,2},{1,3},{2,0},{3,1},{4,6},{5,7},{6,4},{7,5},{8,10},{9,11},{10,... | collective-permute-start | bytes 1720328 | tf_op jit(solution)/shard_map/yback2/ppermute | solution.py:91
  83.3 14.6 %copy-start.5 = (s32[128,2]{0,1:T(2,128)S(1)}, s32[128,2]{0,1:T(2,128)}, u32[]{:S(2)}) copy-start(s32[128,2]{0,1:T(2,128)} %param.7) | copy-start | bytes 3076
  83.3 15.2 %copy-start.6 = (f32[128,2]{0,1:T(2,128)S(1)}, f32[128,2]{0,1:T(2,128)}, u32[]{:S(2)}) copy-start(f32[128,2]{0,1:T(2,128)} %param.8) | copy-start | bytes 3076
  97.8 1.9 %collective-permute-start.20 = (bf16[64,3584]{1,0:T(8,128)(2,1)S(1)}, bf16[64,3584]{1,0:T(8,128)(2,1)S(1)}, u32[]{:S(2)}, u32[]{:S(2)}) collective-permute-start(bf16[64,3584]{1,0:T(8,128)(2,1)S(1)} %constant_dynamic-update-slice_fusion.8.a), channel_id=1, source_target_pairs={{0,1},{1,0},{2,3},{3,2},{4,5},{5,4},{6,7},{7,6},{8,9},{9,8},{10,11... | collective-permute-start | bytes 1376264 | tf_op jit(solution)/shard_map/cout4/ppermute | solution.py:91
  97.9 17.2 %collective-permute-start.19 = (bf16[80,3584]{1,0:T(8,128)(2,1)S(1)}, bf16[80,3584]{1,0:T(8,128)(2,1)S(1)}, u32[]{:S(2)}, u32[]{:S(2)}) collective-permute-start(bf16[80,3584]{1,0:T(8,128)(2,1)S(1)} %fusion.5), channel_id=1, source_target_pairs={{0,4},{1,5},{2,6},{3,7},{4,8},{5,9},{6,10},{7,11},{8,12},{9,13},{1... | collective-permute-start | bytes 1720328 | tf_op jit(solution)/shard_map/zback2/ppermute | solution.py:91
  98.5 18.2 %collective-permute-start.24 = (bf16[96,3584]{1,0:T(8,128)(2,1)S(1)}, bf16[96,3584]{1,0:T(8,128)(2,1)S(1)}, u32[]{:S(2)}, u32[]{:S(2)}) collective-permute-start(bf16[96,3584]{1,0:T(8,128)(2,1)S(1)} %get-tuple-element.113), channel_id=1, source_target_pairs={{0,1},{1,0},{2,3},{3,2},{4,5},{5,4},{6,7},{7,6},{8,9},{9,8},{10,11... | collective-permute-start | bytes 2064392 | tf_op jit(solution)/shard_map/cback3/ppermute | solution.py:91
  101.6 14.3 %collective-permute-start.21 = (bf16[64,3584]{1,0:T(8,128)(2,1)S(1)}, bf16[64,3584]{1,0:T(8,128)(2,1)S(1)}, u32[]{:S(2)}, u32[]{:S(2)}) collective-permute-start(bf16[64,3584]{1,0:T(8,128)(2,1)S(1)} %get-tuple-element.110), channel_id=1, source_target_pairs={{0,1},{1,0},{2,3},{3,2},{4,5},{5,4},{6,7},{7,6},{8,9},{9,8},{10,11... | collective-permute-start | bytes 1376264 | tf_op jit(solution)/shard_map/cback4/ppermute | solution.py:91
  116.1 8.6 %collective-permute-start.22 = (bf16[32,3584]{1,0:T(8,128)(2,1)S(1)}, bf16[32,3584]{1,0:T(8,128)(2,1)S(1)}, u32[]{:S(2)}, u32[]{:S(2)}) collective-permute-start(bf16[32,3584]{1,0:T(8,128)(2,1)S(1)} %slice.77), channel_id=1, source_target_pairs={{0,2},{1,3},{2,0},{3,1},{4,6},{5,7},{6,4},{7,5},{8,10},{9,11},{10,... | collective-permute-start | bytes 688136 | tf_op jit(solution)/shard_map/yback4/ppermute | solution.py:91
  116.8 15.2 %collective-permute-start.25 = (bf16[48,3584]{1,0:T(8,128)(2,1)S(1)}, bf16[48,3584]{1,0:T(8,128)(2,1)S(1)}, u32[]{:S(2)}, u32[]{:S(2)}) collective-permute-start(bf16[48,3584]{1,0:T(8,128)(2,1)S(1)} %slice.76), channel_id=1, source_target_pairs={{0,2},{1,3},{2,0},{3,1},{4,6},{5,7},{6,4},{7,5},{8,10},{9,11},{10,... | collective-permute-start | bytes 1032200 | tf_op jit(solution)/shard_map/yback3/ppermute | solution.py:91
  124.7 17.6 %collective-permute-start.27 = (bf16[32,3584]{1,0:T(8,128)(2,1)S(1)}, bf16[32,3584]{1,0:T(8,128)(2,1)S(1)}, u32[]{:S(2)}, u32[]{:S(2)}) collective-permute-start(bf16[32,3584]{1,0:T(8,128)(2,1)S(1)} %fusion.8), channel_id=1, source_target_pairs={{0,8},{1,9},{2,10},{3,11},{4,12},{5,13},{6,14},{7,15},{8,0},{9,1},... | collective-permute-start | bytes 688136 | tf_op jit(solution)/shard_map/zback4/ppermute | solution.py:91
  124.9 18.1 %collective-permute-start.23 = (bf16[80,3584]{1,0:T(8,128)(2,1)S(1)}, bf16[80,3584]{1,0:T(8,128)(2,1)S(1)}, u32[]{:S(2)}, u32[]{:S(2)}) collective-permute-start(bf16[80,3584]{1,0:T(8,128)(2,1)S(1)} %slice.73), channel_id=1, source_target_pairs={{0,2},{1,3},{2,0},{3,1},{4,6},{5,7},{6,4},{7,5},{8,10},{9,11},{10,... | collective-permute-start | bytes 1720328 | tf_op jit(solution)/shard_map/yback0/ppermute | solution.py:91
  132.1 16.3 %collective-permute-start.26 = (bf16[48,3584]{1,0:T(8,128)(2,1)S(1)}, bf16[48,3584]{1,0:T(8,128)(2,1)S(1)}, u32[]{:S(2)}, u32[]{:S(2)}) collective-permute-start(bf16[48,3584]{1,0:T(8,128)(2,1)S(1)} %fusion.7), channel_id=1, source_target_pairs={{0,8},{1,9},{2,10},{3,11},{4,12},{5,13},{6,14},{7,15},{8,0},{9,1},... | collective-permute-start | bytes 1032200 | tf_op jit(solution)/shard_map/zback3/ppermute | solution.py:91
  143.0 6.8 %copy-start.1 = (bf16[128,3584]{1,0:T(8,128)(2,1)S(1)}, bf16[128,3584]{1,0:T(8,128)(2,1)}, u32[]{:S(2)}) copy-start(bf16[128,3584]{1,0:T(8,128)(2,1)} %param.6) | copy-start | bytes 2752516
